TPU v7x, 1024 devices: a whole 4x8x16 slice. The times are simulated.
1024 devices in a mesh: wide: 16 (over y, core), narrow: 16 (over z), tp: 4 (over x).
Axes of the slice: x: 4, y: 8, z: 16, core: 2. Of those that a mesh axis runs over, the one named last changes fastest.
Arguments:
- d_out: bfloat16 [4096, 3584], P(('wide', 'narrow')), may hold values from -1.5 to 1.5
- expert_ids: int32 [4096, 8], P(('wide', 'narrow')), may hold values from 0 to 127, as said below
- gate_values: bfloat16 [4096, 8], P(('wide', 'narrow')), may hold values from 0.049804688 to 0.59765625
- stored_preacts: bfloat16 [16, 16, 256, 2, 512], P('wide', 'narrow', None, None, 'tp'), may hold values from -6 to 6
- w_gate: bfloat16 [16, 16, 3584, 512], P('wide', 'narrow', None, 'tp'), may hold values from -0.09375 to 0.09375
- w_up: bfloat16 [16, 16, 3584, 512], P('wide', 'narrow', None, 'tp'), may hold values from -0.09375 to 0.09375
- w_down: bfloat16 [16, 16, 512, 3584], P('wide', 'narrow', 'tp'), may hold values from -0.1875 to 0.1875
Outputs:
- d_tokens: bfloat16 [4096, 3584], P(('wide', 'narrow'), 'tp')
- d_gates: float32 [4096, 8], P(('wide', 'narrow'))
Inputs may be any that keep to these rules, and one draw needn't show every extreme that they name: `expert_ids`: each token names 8 distinct experts; expert e lies in group e // 8, and a token's experts lie in exactly 4 groups, 2 in each.
All inputs are finite; a program needn't handle non-finite values.
Results may differ from a plain program's by a relative error of at most 0.017.
Values may be sent and summed in bfloat16 or wider, within the bound.
No kernel may reach another device: no remote copies, remote signals or barrier semaphores. Data moves between devices by JAX's collectives and lax.ppermute only.
A program may use at most 32 MiB of HBM per device.

v0:
```python
import jax
import jax.numpy as jnp
from jax import lax
from jax.sharding import PartitionSpec as P

TOP = 8
LIMIT = 4
HALVES = 2
PER_GROUP = 2


def swish_parts(gate_pre):
    sigmoid_value = jax.nn.sigmoid(gate_pre)
    swish_value = gate_pre * sigmoid_value
    return (swish_value, sigmoid_value * (1.0 + gate_pre * (1.0 - sigmoid_value)))


def spread_rows(placement, values):
    return lax.dot_general(
        placement.astype(jnp.bfloat16),
        values,
        (((0,), (0,)), ((), ())),
        preferred_element_type=jnp.float32,
    )


def gather_rows(placement, values):
    if values.dtype == jnp.bfloat16:
        return lax.dot_general(
            placement.astype(jnp.bfloat16),
            values,
            (((1,), (0,)), ((), ())),
            preferred_element_type=jnp.float32,
        )
    return lax.dot_general(
        placement.astype(jnp.float32),
        values,
        (((1,), (0,)), ((), ())),
        precision=lax.Precision.HIGHEST,
        preferred_element_type=jnp.float32,
    )


def combine_rows(place_two, lane_hit, back_input, back_score):
    row_count, group_width, lane_cap = place_two.shape
    both_halves = jnp.concatenate(
        [place_two.reshape(row_count, group_width * lane_cap)] * HALVES, axis=1
    )
    row_input = gather_rows(both_halves, back_input.reshape(HALVES * group_width * lane_cap, -1))
    score_sum = jnp.sum(
        back_score.astype(jnp.float32).reshape(HALVES, group_width, lane_cap), axis=0
    )
    lane_score = jnp.sum(place_two.astype(jnp.float32) * score_sum[None, :, :], axis=2)
    row_score = jnp.sum(lane_hit.astype(jnp.float32) * lane_score[:, None, :], axis=2)
    return (row_input, row_score)


def combine_tokens(place_one, pair_hit, source_input, source_score):
    token_count, wide_count, group_cap = place_one.shape
    token_input = gather_rows(
        place_one.reshape(token_count, wide_count * group_cap),
        source_input.reshape(wide_count * group_cap, -1),
    )
    group_score = jnp.sum(
        place_one.astype(jnp.float32)[:, :, :, None] * source_score[None, :, :, :], axis=2
    )
    token_score = jnp.sum(pair_hit.astype(jnp.float32) * group_score[:, None, :, :], axis=(2, 3))
    return (token_input, token_score)


def per_device(d_out, expert_ids, gate_values, stored_preacts, w_gate, w_up, w_down):
    wide_count = lax.axis_size("wide")
    lane_count = lax.axis_size("narrow")
    split_count = lax.axis_size("tp")
    group_width = lane_count // HALVES
    token_count = d_out.shape[0]
    model_width = d_out.shape[1]
    slot_count = stored_preacts.shape[2]
    lane_cap = slot_count // lane_count
    group_cap = min(token_count, max(1, 3 * token_count * LIMIT // (2 * wide_count)))
    token_group = expert_ids // group_width
    token_lane = expert_ids % group_width
    route_order = jnp.arange(TOP, dtype=jnp.int32)
    same_group = token_group[:, :, None] == token_group[:, None, :]
    sub_index = jnp.sum(
        (same_group & (route_order[None, :] < route_order[:, None])[None, :, :]).astype(jnp.int32),
        axis=2,
    )
    group_hit = (
        token_group[:, :, None] == jnp.arange(wide_count, dtype=jnp.int32)[None, None, :]
    ).astype(jnp.int32)
    sub_hit = (
        sub_index[:, :, None] == jnp.arange(PER_GROUP, dtype=jnp.int32)[None, None, :]
    ).astype(jnp.int32)
    member = jnp.max(group_hit, axis=1)
    first_rank = jnp.cumsum(member, axis=0) - member
    first_keep = (member > 0) & (first_rank < group_cap)
    place_one = (
        first_keep[:, :, None]
        & (first_rank[:, :, None] == jnp.arange(group_cap, dtype=jnp.int32)[None, None, :])
    ).astype(jnp.int32)
    pair_hit = group_hit[:, :, :, None] * sub_hit[:, :, None, :]
    lane_code = jnp.sum(pair_hit * (token_lane + 1)[:, :, None, None], axis=1)
    gate_code = jnp.sum(
        pair_hit.astype(jnp.float32) * gate_values.astype(jnp.float32)[:, :, None, None], axis=1
    )
    slot_lane = jnp.sum(place_one[:, :, :, None] * lane_code[:, :, None, :], axis=0) - 1
    slot_gate = jnp.sum(
        place_one[:, :, :, None].astype(jnp.float32) * gate_code[:, :, None, :], axis=0
    ).astype(jnp.bfloat16)
    send_rows = (
        spread_rows(place_one.reshape(token_count, wide_count * group_cap), d_out)
        .astype(jnp.bfloat16)
        .reshape(wide_count, group_cap, model_width)
    )
    got_rows, got_lanes, got_gates = (
        lax.all_to_all(send_rows, "wide", split_axis=0, concat_axis=0, tiled=True),
        lax.all_to_all(slot_lane, "wide", split_axis=0, concat_axis=0, tiled=True),
        lax.all_to_all(slot_gate, "wide", split_axis=0, concat_axis=0, tiled=True),
    )
    row_count = wide_count * group_cap
    row_data = got_rows.reshape(row_count, model_width)
    row_lanes = got_lanes.reshape(row_count, PER_GROUP)
    row_gates = got_gates.reshape(row_count, PER_GROUP).astype(jnp.float32)
    lane_hit = (
        row_lanes[:, :, None] == jnp.arange(group_width, dtype=jnp.int32)[None, None, :]
    ).astype(jnp.int32)
    per_lane = jnp.max(lane_hit, axis=1)
    second_rank = jnp.cumsum(per_lane, axis=0) - per_lane
    second_keep = (per_lane > 0) & (second_rank < lane_cap)
    place_two = (
        second_keep[:, :, None]
        & (second_rank[:, :, None] == jnp.arange(lane_cap, dtype=jnp.int32)[None, None, :])
    ).astype(jnp.int32)
    lane_gate = jnp.sum(lane_hit.astype(jnp.float32) * row_gates[:, :, None], axis=1)
    forward_gate = jnp.sum(place_two.astype(jnp.float32) * lane_gate[:, :, None], axis=0).astype(
        jnp.bfloat16
    )
    forward_rows = (
        spread_rows(place_two.reshape(row_count, group_width * lane_cap), row_data)
        .astype(jnp.bfloat16)
        .reshape(group_width, lane_cap, model_width)
    )
    expert_rows, expert_gates = (
        lax.all_to_all(
            jnp.concatenate([forward_rows] * HALVES, axis=0),
            "narrow",
            split_axis=0,
            concat_axis=0,
            tiled=True,
        ),
        lax.all_to_all(
            jnp.concatenate([forward_gate] * HALVES, axis=0),
            "narrow",
            split_axis=0,
            concat_axis=0,
            tiled=True,
        ),
    )
    slot_rows = expert_rows.reshape(slot_count, model_width)
    slot_scale = expert_gates.reshape(slot_count).astype(jnp.float32)
    gate_pre = stored_preacts[0, 0, :, 0, :].astype(jnp.float32)
    up_pre = stored_preacts[0, 0, :, 1, :].astype(jnp.float32)
    back_proj = lax.dot_general(
        slot_rows, w_down[0, 0], (((1,), (1,)), ((), ())), preferred_element_type=jnp.float32
    )
    swish_value, swish_slope = swish_parts(gate_pre)
    hidden = swish_value * up_pre
    score_term = jnp.sum(hidden * back_proj, axis=1).astype(jnp.bfloat16)
    hidden_grad = slot_scale[:, None] * back_proj
    grad_gate = (hidden_grad * up_pre * swish_slope).astype(jnp.bfloat16)
    grad_up = (hidden_grad * swish_value).astype(jnp.bfloat16)
    input_sum = lax.dot_general(
        grad_gate, w_gate[0, 0], (((1,), (1,)), ((), ())), preferred_element_type=jnp.float32
    )
    input_sum = input_sum + lax.dot_general(
        grad_up, w_up[0, 0], (((1,), (1,)), ((), ())), preferred_element_type=jnp.float32
    )
    input_term = input_sum.astype(jnp.bfloat16)
    back_input, back_score = (
        lax.all_to_all(
            input_term.reshape(lane_count, lane_cap, model_width),
            "narrow",
            split_axis=0,
            concat_axis=0,
            tiled=True,
        ),
        lax.all_to_all(
            score_term.reshape(lane_count, lane_cap),
            "narrow",
            split_axis=0,
            concat_axis=0,
            tiled=True,
        ),
    )
    row_input, row_score = combine_rows(place_two, lane_hit, back_input, back_score)
    source_input, source_score = (
        lax.all_to_all(
            row_input.reshape(wide_count, group_cap, model_width).astype(jnp.bfloat16),
            "wide",
            split_axis=0,
            concat_axis=0,
            tiled=True,
        ).astype(jnp.float32),
        lax.all_to_all(
            row_score.reshape(wide_count, group_cap, PER_GROUP).astype(jnp.bfloat16),
            "wide",
            split_axis=0,
            concat_axis=0,
            tiled=True,
        ).astype(jnp.float32),
    )
    token_input, token_score = combine_tokens(place_one, pair_hit, source_input, source_score)
    score_wide = jnp.broadcast_to(token_score[:, None, :], (token_count, split_count, TOP)).reshape(
        token_count, split_count * TOP
    )
    final_input, final_score = (
        lax.psum_scatter(
            token_input.astype(jnp.bfloat16), "tp", scatter_dimension=1, tiled=True
        ).astype(jnp.float32),
        lax.psum_scatter(
            score_wide.astype(jnp.bfloat16), "tp", scatter_dimension=1, tiled=True
        ).astype(jnp.float32),
    )
    return (final_input.astype(jnp.bfloat16), final_score)


def solution(mesh):
    return jax.shard_map(
        per_device,
        mesh=mesh,
        in_specs=(
            P(("wide", "narrow"), None),
            P(("wide", "narrow"), None),
            P(("wide", "narrow"), None),
            P("wide", "narrow", None, None, "tp"),
            P("wide", "narrow", None, "tp"),
            P("wide", "narrow", None, "tp"),
            P("wide", "narrow", "tp", None),
        ),
        out_specs=(P(("wide", "narrow"), "tp"), P(("wide", "narrow"), None)),
        check_vma=False,
    )
```

profile of v0, /device:TPU:1, one launch (start us, length us, event | category | flops | bytes accessed | tf_op | source)
XLA Modules:
  0.0 375.0 jit_solution(8547126856817071990)
XLA Ops:
  7.2 0.8 add_select_fusion.1
  8.5 0.2 fusion.16
  8.8 0.7 copy.133
  9.5 17.4 %all-to-all-start = ((s32[16,6,2]{1,2,0:T(2,128)}), s32[16,6,2]{1,2,0:T(2,128)S(1)}, u32[]{:S(2)}, u32[]{:S(2)}) async-start(s32[16,6,2]{1,2,0:T(2,128)} %copy.133), calls=%async_computation | async-start | bytes 32768 | tf_op jit(solution)/shard_map/all_to_all | solution.py:118
  27.2 1.3 convolution_convert_fusion.2
  28.5 1.2 reshape.195
  29.7 4.6 %all-to-all-done = s32[16,6,2]{1,2,0:T(2,128)S(1)} async-done(((s32[16,6,2]{1,2,0:T(2,128)}), s32[16,6,2]{1,2,0:T(2,128)S(1)}, u32[]{:S(2)}, u32[]{:S(2)}) %all-to-all-start) | async-done | bytes 800 | tf_op jit(solution)/shard_map/all_to_all | solution.py:118
  34.3 3.8 %all-to-all-start.3 = ((bf16[16,6,3584]{2,1,0:T(8,128)(2,1)}), bf16[16,6,3584]{2,1,0:T(8,128)(2,1)S(1)}, u32[]{:S(2)}, u32[]{:S(2)}) async-start(bf16[16,6,3584]{2,1,0:T(8,128)(2,1)} %reshape.195), calls=%async_computation.3 | async-start | bytes 1835008 | tf_op jit(solution)/shard_map/all_to_all | solution.py:117
  38.3 0.1 reduce_window_sum.23
  38.6 24.9 %all-to-all-done.3 = bf16[16,6,3584]{2,1,0:T(8,128)(2,1)S(1)} async-done(((bf16[16,6,3584]{2,1,0:T(8,128)(2,1)}), bf16[16,6,3584]{2,1,0:T(8,128)(2,1)S(1)}, u32[]{:S(2)}, u32[]{:S(2)}) %all-to-all-start.3) | async-done | bytes 688160 | tf_op jit(solution)/shard_map/all_to_all | solution.py:117
  63.5 0.2 reshape.196
  63.7 0.4 convolution_convert_fusion
  64.1 1.4 pad_maximum_fusion
  65.5 9.8 %all-to-all-start.4 = ((bf16[16,16,3584]{2,1,0:T(8,128)(2,1)}), bf16[16,16,3584]{2,1,0:T(8,128)(2,1)S(1)}, u32[]{:S(2)}, u32[]{:S(2)}) async-start(bf16[16,16,3584]{2,1,0:T(8,128)(2,1)} %pad_maximum_fusion), calls=%async_computation.4 | async-start | bytes 3670016 | tf_op jit(solution)/shard_map/all_to_all | solution.py:145
  75.3 0.2 fusion.51
  75.5 0.1 copy.161
  75.7 0.1 copy.160
  75.8 80.1 %all-to-all-done.4 = bf16[16,16,3584]{2,1,0:T(8,128)(2,1)S(1)} async-done(((bf16[16,16,3584]{2,1,0:T(8,128)(2,1)}), bf16[16,16,3584]{2,1,0:T(8,128)(2,1)S(1)}, u32[]{:S(2)}, u32[]{:S(2)}) %all-to-all-start.4) | async-done | bytes 1835040 | tf_op jit(solution)/shard_map/all_to_all | solution.py:145
  155.9 1.9 fusion.13
  157.9 21.6 %all_to_all.50 = bf16[16,1,16]{2,1,0:T(2,128)(2,1)S(1)} all-to-all(bf16[16,1,16]{2,1,0:T(2,128)(2,1)S(1)} %convert_element_type.247), channel_id=1, replica_groups=mesh['wide'=16,'narrow'=16,'tp'=4] {'narrow'}, dimensions={0} | all-to-all | bytes 1024 | tf_op jit(solution)/shard_map/all_to_all | solution.py:188
  179.7 0.6 copy.154
  180.3 5.6 %all-to-all-start.8 = ((bf16[16,6,2]{1,2,0:T(2,128)(2,1)}), bf16[16,6,2]{1,2,0:T(2,128)(2,1)S(1)}, u32[]{:S(2)}, u32[]{:S(2)}) async-start(bf16[16,6,2]{1,2,0:T(2,128)(2,1)} %copy.154), calls=%async_computation.8 | async-start | bytes 16384 | tf_op jit(solution)/shard_map/all_to_all | solution.py:205
  186.0 6.9 %all-to-all-done.8 = bf16[16,6,2]{1,2,0:T(2,128)(2,1)S(1)} async-done(((bf16[16,6,2]{1,2,0:T(2,128)(2,1)}), bf16[16,6,2]{1,2,0:T(2,128)(2,1)S(1)}, u32[]{:S(2)}, u32[]{:S(2)}) %all-to-all-start.8) | async-done | bytes 416 | tf_op jit(solution)/shard_map/all_to_all | solution.py:205
  193.0 0.2 fusion.15
  193.2 0.1 copy.143
  193.3 10.1 %all_to_all.51 = bf16[16,6,2]{1,2,0:T(2,128)(2,1)S(1)} all-to-all(bf16[16,6,2]{1,2,0:T(2,128)(2,1)S(1)} %copy.143), channel_id=1, replica_groups=mesh['wide'=16,'narrow'=16,'tp'=4] {'wide'}, dimensions={0} | all-to-all | bytes 768 | tf_op jit(solution)/shard_map/all_to_all | solution.py:119
  203.9 13.8 %all_to_all.52 = bf16[16,1,16]{2,1,0:T(2,128)(2,1)S(1)} all-to-all(bf16[16,1,16]{2,1,0:T(2,128)(2,1)S(1)} %copy.146), channel_id=1, replica_groups=mesh['wide'=16,'narrow'=16,'tp'=4] {'narrow'}, dimensions={0} | all-to-all | bytes 1024 | tf_op jit(solution)/shard_map/all_to_all | solution.py:152
  217.8 0.7 fusion.3
  218.5 0.5 copy-done.1
  219.0 2.0 fusion
  220.9 3.7 all-to-all-start.5
  224.8 0.1 copy.162
  225.0 0.2 eq.145.clone
  225.1 0.2 eq.146
  225.3 0.2 and.83.clone
  225.5 0.2 and.84
  225.7 79.5 %all-to-all-done.5 = bf16[16,16,3584]{2,1,0:T(8,128)(2,1)S(1)} async-done(((bf16[16,16,3584]{2,1,0:T(8,128)(2,1)}), bf16[16,16,3584]{2,1,0:T(8,128)(2,1)S(1)}, u32[]{:S(2)}, u32[]{:S(2)}) %all-to-all-start.5) | async-done | bytes 1835040 | tf_op jit(solution)/shard_map/all_to_all | solution.py:181
  305.1 0.4 convolution_convert_fusion.1
  305.6 1.3 copy.151
  306.9 9.0 %all-to-all-start.6 = ((bf16[16,6,3584]{2,1,0:T(8,128)(2,1)}), bf16[16,6,3584]{2,1,0:T(8,128)(2,1)S(1)}, u32[]{:S(2)}, u32[]{:S(2)}) async-start(bf16[16,6,3584]{2,1,0:T(8,128)(2,1)} %copy.151), calls=%async_computation.6 | async-start | bytes 1835008 | tf_op jit(solution)/shard_map/all_to_all | solution.py:198
  316.0 1.3 dynamic-slice
  318.0 23.3 %all-to-all-done.6 = bf16[16,6,3584]{2,1,0:T(8,128)(2,1)S(1)} async-done(((bf16[16,6,3584]{2,1,0:T(8,128)(2,1)}), bf16[16,6,3584]{2,1,0:T(8,128)(2,1)S(1)}, u32[]{:S(2)}, u32[]{:S(2)}) %all-to-all-start.6) | async-done | bytes 688160 | tf_op jit(solution)/shard_map/all_to_all | solution.py:198
  341.2 0.9 fusion.1
  342.1 1.2 copy.158
  343.4 8.7 %all-reduce = bf16[16,32]{0,1:T(8,128)(2,1)S(1)} all-reduce(bf16[16,32]{0,1:T(8,128)(2,1)S(1)} %broadcast_bitcast_fusion), channel_id=3, replica_groups=mesh['wide'=16,'narrow'=16,'tp'=4] {'tp'}, use_global_device_ids=true, to_apply=%region_18.19.clone | all-reduce | flops 512 | bytes 2048
  352.1 0.6 dynamic-slice_convert_fusion
  352.7 13.8 %reduce-scatter.4.cloned.1.call-done = bf16[896,16]{1,0:T(8,128)(2,1)} async-done(((bf16[3584,16]{1,0:T(8,128)(2,1)}), bf16[896,16]{1,0:T(8,128)(2,1)}) %reduce-scatter.4.cloned.1.call-update) | async-done | bytes 28688
  366.5 1.7 copy.159
  (66 shorter events, 2.6 us)
Async XLA Ops:
  7.2 210.6 %copy-start = (bf16[1,1,3584,128]{3,2,1,0:T(8,128)(2,1)S(1)}, bf16[1,1,3584,128]{3,2,1,0:T(8,128)(2,1)}, u32[]{:S(2)}) copy-start(bf16[1,1,3584,128]{3,2,1,0:T(8,128)(2,1)} %param.11) | copy-start | bytes 2752516
  9.5 24.8 %all-to-all-start = ((s32[16,6,2]{1,2,0:T(2,128)}), s32[16,6,2]{1,2,0:T(2,128)S(1)}, u32[]{:S(2)}, u32[]{:S(2)}) async-start(s32[16,6,2]{1,2,0:T(2,128)} %copy.133), calls=%async_computation | async-start | bytes 32768 | tf_op jit(solution)/shard_map/all_to_all | solution.py:118
  34.3 29.2 %all-to-all-start.3 = ((bf16[16,6,3584]{2,1,0:T(8,128)(2,1)}), bf16[16,6,3584]{2,1,0:T(8,128)(2,1)S(1)}, u32[]{:S(2)}, u32[]{:S(2)}) async-start(bf16[16,6,3584]{2,1,0:T(8,128)(2,1)} %reshape.195), calls=%async_computation.3 | async-start | bytes 1835008 | tf_op jit(solution)/shard_map/all_to_all | solution.py:117
  65.5 9.8 %copy-start.2 = (bf16[1,1,256,2,128]{4,3,2,1,0:T(2,128)(2,1)S(1)}, bf16[1,1,256,2,128]{4,3,2,1,0:T(2,128)(2,1)}, u32[]{:S(2)}) copy-start(bf16[1,1,256,2,128]{4,3,2,1,0:T(2,128)(2,1)} %param.10) | copy-start | bytes 393220
  65.5 90.4 %all-to-all-start.4 = ((bf16[16,16,3584]{2,1,0:T(8,128)(2,1)}), bf16[16,16,3584]{2,1,0:T(8,128)(2,1)S(1)}, u32[]{:S(2)}, u32[]{:S(2)}) async-start(bf16[16,16,3584]{2,1,0:T(8,128)(2,1)} %pad_maximum_fusion), calls=%async_computation.4 | async-start | bytes 3670016 | tf_op jit(solution)/shard_map/all_to_all | solution.py:145
  75.7 110.2 %copy-start.3 = (bf16[16,8]{0,1:T(8,128)(2,1)S(1)}, bf16[16,8]{0,1:T(8,128)(2,1)}, u32[]{:S(2)}) copy-start(bf16[16,8]{0,1:T(8,128)(2,1)} %param.9) | copy-start | bytes 772
  180.3 12.5 %all-to-all-start.8 = ((bf16[16,6,2]{1,2,0:T(2,128)(2,1)}), bf16[16,6,2]{1,2,0:T(2,128)(2,1)S(1)}, u32[]{:S(2)}, u32[]{:S(2)}) async-start(bf16[16,6,2]{1,2,0:T(2,128)(2,1)} %copy.154), calls=%async_computation.8 | async-start | bytes 16384 | tf_op jit(solution)/shard_map/all_to_all | solution.py:205
  217.8 1.2 copy-start.1
  220.9 84.2 %all-to-all-start.5 = ((bf16[16,16,3584]{2,1,0:T(8,128)(2,1)}), bf16[16,16,3584]{2,1,0:T(8,128)(2,1)S(1)}, u32[]{:S(2)}, u32[]{:S(2)}) async-start(bf16[16,16,3584]{2,1,0:T(8,128)(2,1)} %bitcast.67), calls=%async_computation.5 | async-start | bytes 3670016 | tf_op jit(solution)/shard_map/all_to_all | solution.py:181
  306.9 34.3 %all-to-all-start.6 = ((bf16[16,6,3584]{2,1,0:T(8,128)(2,1)}), bf16[16,6,3584]{2,1,0:T(8,128)(2,1)S(1)}, u32[]{:S(2)}, u32[]{:S(2)}) async-start(bf16[16,6,3584]{2,1,0:T(8,128)(2,1)} %copy.151), calls=%async_computation.6 | async-start | bytes 1835008 | tf_op jit(solution)/shard_map/all_to_all | solution.py:198
  315.9 50.6 %reduce-scatter.4.cloned.1.call-start = ((), (), s32[]{:S(2)}) async-start(), calls=%async_computation.10 | async-start | bytes 1146880
Sparse Core Ops, SparseCore 0:
  343.5 22.9 reduce-scatter.3
where the time goes:
time: 376 us; the launch traced here: 375 us
  waiting for transfers between devices  233 us (62%)
  blocking collectives  54.2 us (14%)
  starting transfers between devices  49.4 us (13%)
  between operations  15 us (4%)
  local copies, waits for them, and re-layouts  11.8 us (3%)
  matrix products  7.53 us (2%)
  other arithmetic  4.08 us (1%)
    all_to_all x1, waiting for transfers between devices, per_device(): lax.all_to_all(jnp.concatenate([forward_rows] * HALVES, axis=0), 'narrow'...  80.1 us
    all_to_all x1, waiting for transfers between devices, per_device(): lax.all_to_all(input_term.reshape(lane_count, lane_cap, model_width), 'na...  79.5 us
    all_to_all x1, waiting for transfers between devices, per_device(): lax.all_to_all(send_rows, 'wide', split_axis=0, concat_axis=0, tiled=True)  24.9 us
    all_to_all x1, waiting for transfers between devices, per_device(): lax.all_to_all(row_input.reshape(wide_count, group_cap, model_width).asty...  23.3 us
    all_to_all x1, blocking collectives, per_device(): lax.all_to_all(score_term.reshape(lane_count, lane_cap), 'narrow', split_...  21.6 us
    all_to_all x1, starting transfers between devices, per_device(): lax.all_to_all(slot_lane, 'wide', split_axis=0, concat_axis=0, tiled=True)  17.4 us
    all_to_all x1, blocking collectives, per_device(): lax.all_to_all(jnp.concatenate([forward_gate] * HALVES, axis=0), 'narrow'...  13.8 us
    unnamed x2, waiting for transfers between devices  13.8 us
  transfers between devices with their start and end apart: 7, of which 7 were waited for; matrix products, arithmetic and copies ran while one was open for 2% of the time, Pallas kernels for 0%

commit v1 on v0

v1 whole, which is shorter than its diff:
```python
import jax
import jax.numpy as jnp
from jax import lax
from jax.experimental import pallas as pl
from jax.experimental.pallas import tpu as pltpu
from jax.sharding import PartitionSpec as P

LIMIT = 4
HALVES = 2
BLOCK = 8
TILE = 128


def nn(left, right):
    return lax.dot_general(
        left, right, (((1,), (0,)), ((), ())), preferred_element_type=jnp.float32
    )


def nt(left, right):
    return lax.dot_general(
        left, right, (((1,), (1,)), ((), ())), preferred_element_type=jnp.float32
    )


def iota(shape, axis):
    return lax.broadcasted_iota(jnp.int32, shape, axis)


def bits(mask):
    return jnp.where(mask, 1.0, 0.0).astype(jnp.bfloat16)


def call(kernel, outs, args, flops=0, size=1 << 20):
    return pl.pallas_call(
        kernel,
        out_shape=outs,
        in_specs=[pl.BlockSpec(memory_space=pltpu.VMEM)] * len(args),
        out_specs=jax.tree.map(lambda _: pl.BlockSpec(memory_space=pltpu.VMEM), outs),
        compiler_params=pltpu.CompilerParams(vmem_limit_bytes=40 << 20),
        cost_estimate=pl.CostEstimate(flops=flops, bytes_accessed=size, transcendentals=0),
    )(*args)


def shape(*dims, dtype=jnp.bfloat16):
    return jax.ShapeDtypeStruct(dims, dtype)


def pack_down_kernel(down_ref, *refs):
    out_refs, ready_ref = refs[:-1], refs[-1]
    ready_ref[...] = jnp.zeros_like(ready_ref)
    count = len(out_refs)
    width = down_ref.shape[1] // count
    me = lax.axis_index("tp")
    for step, out_ref in enumerate(out_refs):
        to = lax.rem(me + step, count)
        out_ref[...] = down_ref[:, pl.ds(pl.multiple_of(to * width, TILE), width)]


def pack_rest_kernel(gate_ref, up_ref, preact_ref, *refs):
    out_refs, ready_ref = refs[:-1], refs[-1]
    ready_ref[...] = jnp.zeros_like(ready_ref)
    count = len(out_refs)
    width = gate_ref.shape[0] // count
    me = lax.axis_index("tp")
    for step, out_ref in enumerate(out_refs):
        to = lax.rem(me + step, count)
        rows = pl.ds(pl.multiple_of(to * width, TILE), width)
        out_ref[0:width, :] = gate_ref[rows, :]
        out_ref[width : 2 * width, :] = up_ref[rows, :]
        out_ref[2 * width :, :] = preact_ref[...]


def spread(group_cap, rows):
    r, c = iota((rows, rows), 0), iota((rows, rows), 1)
    return bits((r // BLOCK == c // BLOCK) & (r % BLOCK == group_cap))


def collect(group_cap, rows):
    r, c = iota((rows, rows), 0), iota((rows, rows), 1)
    return bits(
        (r // BLOCK == c // BLOCK) & (c % BLOCK == group_cap) & (r % BLOCK < group_cap)
    )


def own_span(rows, width):
    r, c = iota((rows, rows), 0), iota((rows, rows), 1)
    return c // width == r % BLOCK


def first_kernel(group_cap, width, ids_ref, gates_ref, rows_ref, ready_ref, send_ref, place_ref):
    top, tokens = ids_ref.shape
    rows = send_ref.shape[0]
    groups = rows // BLOCK
    columns = send_ref.shape[1]
    ids = ids_ref[...]
    gates = gates_ref[...].astype(jnp.float32)
    member = jnp.zeros((groups, tokens), jnp.float32)
    table = jnp.zeros((groups * width, tokens), jnp.float32)
    for k in range(top):
        one = ids[k : k + 1, :]
        member = jnp.where(one // width == iota((groups, tokens), 0), 1.0, member)
        table = jnp.where(one == iota((groups * width, tokens), 0), gates[k : k + 1, :], table)
    earlier = bits(iota((tokens, tokens), 0) < iota((tokens, tokens), 1))
    rank = nn(member.astype(jnp.bfloat16), earlier)
    rank = jnp.where((member > 0) & (rank < group_cap), rank, 100.0)
    grow = bits(iota((rows, groups), 0) // BLOCK == iota((rows, groups), 1))
    place = nn(grow, rank.astype(jnp.bfloat16)) == (
        iota((rows, tokens), 0) % BLOCK
    ).astype(jnp.float32)
    place = bits(place)
    place_ref[...] = place
    columns_at = pl.ds(pl.multiple_of(lax.axis_index("tp") * columns, TILE), columns)
    send_ref[...] = nn(place, rows_ref[:, columns_at]).astype(jnp.bfloat16)
    r, c = iota((rows, groups * width), 0), iota((rows, groups * width), 1)
    paired = nt(place, table.astype(jnp.bfloat16))
    paired = jnp.where(r // BLOCK == c // width, paired, 0.0).astype(jnp.bfloat16)
    a, b = iota((groups * width, rows), 0), iota((groups * width, rows), 1)
    repeated = nn(paired, bits(a % width == b % width))
    repeated = jnp.where(own_span(rows, width), repeated, 0.0).astype(jnp.bfloat16)
    notes = nn(spread(group_cap, rows), repeated)
    first = send_ref[:, 0:rows].astype(jnp.float32)
    send_ref[:, 0:rows] = (first + notes).astype(jnp.bfloat16)


def second_kernel(group_cap, width, lane_cap, got_ref, *refs):
    out_ref, gated_ref = refs[-2:]
    rows = got_ref.shape[0]
    got = got_ref[...]
    notes = nn(collect(group_cap, rows), got[:, 0:rows])
    notes = jnp.where(own_span(rows, width), notes, 0.0).astype(jnp.bfloat16)
    slots = width * lane_cap
    a, b = iota((rows, slots), 0), iota((rows, slots), 1)
    gate = nn(notes, bits((a % width == b // lane_cap) & (a < group_cap * width)))
    hit = gate != 0.0
    rank = nn(bits(iota((rows, rows), 1) < iota((rows, rows), 0)), bits(hit))
    place = hit & (rank == (b % lane_cap).astype(jnp.float32))
    gated_ref[...] = jnp.where(place, gate, 0.0).astype(jnp.bfloat16)
    turned = jnp.transpose(jnp.where(place, 1.0, 0.0)).astype(jnp.bfloat16)
    moved = nn(turned, got).astype(jnp.bfloat16)
    for half in range(HALVES):
        out_ref[half] = moved


def partial_kernel(rows_ref, *refs):
    out_ref = refs[-1]
    rows = rows_ref[...]
    blocks = [block_ref[...] for block_ref in refs[:-1]]
    out_ref[...] = nt(rows, jnp.concatenate(blocks, axis=0)).astype(jnp.bfloat16)


def cycle_sum(terms):
    count = len(terms)
    while count > 1:
        count //= 2
        terms = [terms[i] + terms[i + count] for i in range(count)]
    return terms[0]


def expert_kernel(count, *refs):
    parts, blocks, out_ref = refs[:count], refs[count : 2 * count], refs[-1]
    slots = out_ref.shape[0]
    columns = out_ref.shape[1] - TILE
    hidden = parts[0].shape[1] // count
    grads, weights, scores = [], [], []
    for at in range(count):
        pieces = []
        for step in range(count):
            source = (at - step) % count
            pieces.append(
                parts[step][:, source * hidden : (source + 1) * hidden].astype(jnp.float32)
            )
        back = cycle_sum(pieces)
        gate_pre = blocks[at][2 * columns : 2 * columns + slots, :].astype(jnp.float32)
        up_pre = blocks[at][2 * columns + slots :, :].astype(jnp.float32)
        sigmoid_value = jax.nn.sigmoid(gate_pre)
        swish_value = gate_pre * sigmoid_value
        slope = sigmoid_value * (1.0 + gate_pre * (1.0 - sigmoid_value))
        up_part = swish_value * back
        scores.append(up_part * up_pre)
        grads.append((back * up_pre * slope).astype(jnp.bfloat16))
        grads.append(up_part.astype(jnp.bfloat16))
        weights.append(blocks[at][0:columns, :])
        weights.append(blocks[at][columns : 2 * columns, :])
    total = nt(jnp.concatenate(grads, axis=1), jnp.concatenate(weights, axis=1))
    out_ref[:, 0:columns] = total.astype(jnp.bfloat16)
    score = jnp.sum(cycle_sum(scores), axis=1, keepdims=True)
    out_ref[:, columns:] = jnp.broadcast_to(score, (slots, TILE)).astype(jnp.bfloat16)


def rows_kernel(group_cap, width, lane_cap, gated_ref, back_ref, out_ref):
    rows, columns = out_ref.shape
    gated = gated_ref[...]
    both = jnp.concatenate([gated, gated], axis=1)
    out_ref[...] = nn(both, back_ref[:, 0:columns]).astype(jnp.bfloat16)
    place = bits(both != 0)
    slots = both.shape[1]
    a, b = iota((slots, TILE), 0), iota((slots, TILE), 1)
    score = back_ref[:, columns:].astype(jnp.float32)
    score = jnp.where((a // lane_cap) % width == b % width, score, 0.0).astype(jnp.bfloat16)
    score = nn(place, score)
    score = jnp.where(own_span(rows, width), score, 0.0).astype(jnp.bfloat16)
    notes = nn(spread(group_cap, rows), score)
    first = out_ref[:, 0:rows].astype(jnp.float32)
    out_ref[:, 0:rows] = (first + notes).astype(jnp.bfloat16)


def last_kernel(group_cap, width, ids_ref, place_ref, home_ref, tokens_ref, gates_ref):
    top, tokens = ids_ref.shape
    rows = home_ref.shape[0]
    ids = ids_ref[...]
    home = home_ref[...]
    place = jnp.transpose(place_ref[...].astype(jnp.float32)).astype(jnp.bfloat16)
    tokens_ref[...] = nn(place, home).astype(jnp.bfloat16)
    notes = nn(collect(group_cap, rows), home[:, 0:rows])
    notes = jnp.where(own_span(rows, width), notes, 0.0).astype(jnp.bfloat16)
    a, b = iota((rows, rows), 0), iota((rows, rows), 1)
    wide = nn(notes, bits((a % width == b % width) & (a < group_cap * width)))
    wide = jnp.where(a // BLOCK == b // width, wide, 0.0).astype(jnp.bfloat16)
    score = jnp.transpose(nn(place, wide))
    at = iota((rows, tokens), 0)
    for k in range(top):
        gates_ref[k : k + 1, :] = jnp.sum(
            jnp.where(ids[k : k + 1, :] == at, score, 0.0), axis=0, keepdims=True
        )


def exchange(values, axis):
    return lax.all_to_all(values, axis, split_axis=0, concat_axis=0, tiled=True)


def shift(values, step, count):
    return lax.ppermute(
        values, "tp", [(source, (source + step) % count) for source in range(count)]
    )


def per_device(d_out, expert_ids, gate_values, stored_preacts, w_gate, w_up, w_down):
    wide_count = lax.axis_size("wide")
    lane_count = lax.axis_size("narrow")
    split_count = lax.axis_size("tp")
    group_width = lane_count // HALVES
    token_count, model_width = d_out.shape
    slot_count = stored_preacts.shape[2]
    hidden_width = stored_preacts.shape[4]
    lane_cap = slot_count // lane_count
    group_cap = min(token_count, max(1, 3 * token_count * LIMIT // (2 * wide_count)))
    columns = model_width // split_count
    rows = wide_count * BLOCK
    lanes = group_width * lane_cap
    ids = expert_ids.T

    down_packed = call(
        pack_down_kernel,
        [shape(hidden_width, columns)] * split_count + [shape(BLOCK, TILE)],
        (w_down[0, 0],),
    )
    downs = [down_packed[0]] + [
        shift(down_packed[step], step, split_count) for step in range(1, split_count)
    ]
    rest_packed = call(
        pack_rest_kernel,
        [shape(2 * columns + 2 * slot_count, hidden_width)] * split_count + [shape(BLOCK, TILE)],
        (
            w_gate[0, 0],
            w_up[0, 0],
            stored_preacts[0, 0].transpose(1, 0, 2).reshape(2 * slot_count, hidden_width),
        ),
        size=4 << 20,
    )
    blocks = [rest_packed[0]] + [
        shift(rest_packed[step], step, split_count) for step in range(1, split_count)
    ]

    send, place = call(
        lambda *refs: first_kernel(group_cap, group_width, *refs),
        [shape(rows, columns), shape(rows, token_count)],
        (ids, gate_values.T, d_out, down_packed[-1]),
    )
    got = exchange(send.reshape(wide_count, BLOCK, columns), "wide").reshape(rows, columns)
    forward, gated = call(
        lambda *refs: second_kernel(group_cap, group_width, lane_cap, *refs),
        [shape(HALVES, lanes, columns), shape(rows, lanes)],
        (got, rest_packed[-1], *downs[1:]),
    )
    slot_rows = exchange(forward.reshape(lane_count, lane_cap, columns), "narrow").reshape(
        slot_count, columns
    )
    partial = call(
        partial_kernel,
        shape(slot_count, split_count * hidden_width),
        (slot_rows, *downs),
    )
    parts = [partial] + [shift(partial, step, split_count) for step in range(1, split_count)]
    terms = call(
        lambda *refs: expert_kernel(split_count, *refs),
        shape(slot_count, columns + TILE),
        (*parts, *blocks),
    )
    back = exchange(terms.reshape(lane_count, lane_cap, columns + TILE), "narrow").reshape(
        slot_count, columns + TILE
    )
    row_input = call(
        lambda *refs: rows_kernel(group_cap, group_width, lane_cap, *refs),
        shape(rows, columns),
        (gated, back),
    )
    home = exchange(row_input.reshape(wide_count, BLOCK, columns), "wide").reshape(rows, columns)
    d_tokens, d_gates = call(
        lambda *refs: last_kernel(group_cap, group_width, *refs),
        [
            shape(token_count, columns),
            shape(expert_ids.shape[1], token_count, dtype=jnp.float32),
        ],
        (ids, place, home),
    )
    return (d_tokens, d_gates.T)


def solution(mesh):
    return jax.shard_map(
        per_device,
        mesh=mesh,
        in_specs=(
            P(("wide", "narrow"), None),
            P(("wide", "narrow"), None),
            P(("wide", "narrow"), None),
            P("wide", "narrow", None, None, "tp"),
            P("wide", "narrow", None, "tp"),
            P("wide", "narrow", None, "tp"),
            P("wide", "narrow", "tp", None),
        ),
        out_specs=(P(("wide", "narrow"), "tp"), P(("wide", "narrow"), None)),
        check_vma=False,
    )
```

time: 376 us -> 158 us (0.42)
  waiting for transfers between devices: 233 us -> 21.5 us
  between operations: 15 us -> 0.81 us
  blocking collectives: 54.2 us -> 63.3 us
  Pallas kernels: 0 us -> 7.83 us
  starting transfers between devices: 49.4 us -> 57.2 us
  matrix products: 7.53 us -> 0 us
  local copies, waits for them, and re-layouts: 11.8 us -> 6.39 us
  other arithmetic: 4.08 us -> 0 us
    all_to_all x6 -> x2, waiting for transfers between devices: 219 us -> 9.73 us  [exchange(): return lax.all_to_all(values, axis, split_axis=0, concat_axis=0, tiled=True)]
    ppermute x0 -> x9, starting transfers between devices: none -> 29.7 us  [shift(): lax.ppermute(values, 'tp', [(source, (source + step) % count) for source...]
    all_to_all x6 -> x2, starting transfers between devices: 49.3 us -> 27.5 us  [exchange(): return lax.all_to_all(values, axis, split_axis=0, concat_axis=0, tiled=True)]
    all_to_all x3 -> x2, blocking collectives: 45.5 us -> 63.3 us  [exchange(): return lax.all_to_all(values, axis, split_axis=0, concat_axis=0, tiled=True)]
    unnamed x2 -> x0, waiting for transfers between devices: 13.8 us -> none
    ppermute x0 -> x9, waiting for transfers between devices: none -> 11.8 us  [shift(): lax.ppermute(values, 'tp', [(source, (source + step) % count) for source...]
    unnamed x1 -> x0, blocking collectives: 8.71 us -> none
    pallas_call x0 -> x8, Pallas kernels: none -> 7.83 us  [call(): pl.pallas_call(kernel, out_shape=outs, in_specs=[pl.BlockSpec(memory_spac...]
  transfers between devices with their start and end apart: 7 -> 11, of which waited for: 7 -> 5; matrix products, arithmetic and copies ran while one was open for 2% -> 0% of each run, Pallas kernels for 0% -> 1%
where the time goes in v1:
time: 158 us; the launch traced here: 157 us
  blocking collectives  63.3 us (40%)
  starting transfers between devices  57.2 us (36%)
  waiting for transfers between devices  21.5 us (14%)
  Pallas kernels  7.83 us (5%)
  local copies, waits for them, and re-layouts  6.39 us (4%)
    all_to_all x2, blocking collectives, exchange(): return lax.all_to_all(values, axis, split_axis=0, concat_axis=0, tiled=True)  63.3 us
    ppermute x9, starting transfers between devices, shift(): lax.ppermute(values, 'tp', [(source, (source + step) % count) for source...  29.7 us
    all_to_all x2, starting transfers between devices, exchange(): return lax.all_to_all(values, axis, split_axis=0, concat_axis=0, tiled=True)  27.5 us
    ppermute x9, waiting for transfers between devices, shift(): lax.ppermute(values, 'tp', [(source, (source + step) % count) for source...  11.8 us
    all_to_all x2, waiting for transfers between devices, exchange(): return lax.all_to_all(values, axis, split_axis=0, concat_axis=0, tiled=True)  9.73 us
    pallas_call x8, Pallas kernels, call(): pl.pallas_call(kernel, out_shape=outs, in_specs=[pl.BlockSpec(memory_spac...  7.83 us
    unnamed x18, local copies, waits for them, and re-layouts  6.37 us
  transfers between devices with their start and end apart: 11, of which 5 were waited for; matrix products, arithmetic and copies ran while one was open for 0% of the time, Pallas kernels for 1%

profile of v1, /device:TPU:1, one launch (start us, length us, event | category | flops | bytes accessed | tf_op | source)
XLA Modules:
  0.0 157.1 jit_solution(461995619711242848)
XLA Ops:
  0.6 0.0 copy-start
  0.6 1.2 copy-done
  1.8 0.0 copy-start.1
  1.8 0.1 shard_map.86
  1.9 0.0 copy-start.4
  1.9 0.7 copy-done.4
  2.6 0.0 copy-start.3
  2.6 0.9 copy-done.3
  3.5 0.7 copy-done.5
  4.2 1.4 shard_map.87
  5.6 0.0 copy-start.8
  5.6 17.6 %all-to-all-start = ((bf16[16,8,896]{2,1,0:T(8,128)(2,1)}), bf16[16,8,896]{2,1,0:T(8,128)(2,1)S(1)}, u32[]{:S(2)}, u32[]{:S(2)}) async-start(bf16[16,8,896]{2,1,0:T(8,128)(2,1)} %bitcast.3), calls=%async_computation | async-start | bytes 458752 | tf_op jit(solution)/shard_map/all_to_all | solution.py:229
  23.2 1.9 %collective-permute-start = (bf16[128,896]{1,0:T(8,128)(2,1)S(1)}, bf16[128,896]{1,0:T(8,128)(2,1)S(1)}, u32[]{:S(2)}, u32[]{:S(2)}) collective-permute-start(bf16[128,896]{1,0:T(8,128)(2,1)S(1)} %get-tuple-element.22), channel_id=1, source_target_pairs={{0,1},{1,2},{2,3},{3,0},{4,5},{5,6},{6,7},{7,4},{8,9},{9,10},{10,1... | collective-permute-start | bytes 688136 | tf_op jit(solution)/shard_map/ppermute | solution.py:233
  25.1 1.9 %collective-permute-start.1 = (bf16[128,896]{1,0:T(8,128)(2,1)S(1)}, bf16[128,896]{1,0:T(8,128)(2,1)S(1)}, u32[]{:S(2)}, u32[]{:S(2)}) collective-permute-start(bf16[128,896]{1,0:T(8,128)(2,1)S(1)} %get-tuple-element.23), channel_id=1, source_target_pairs={{0,2},{1,3},{2,0},{3,1},{4,6},{5,7},{6,4},{7,5},{8,10},{9,11},{10,... | collective-permute-start | bytes 688136 | tf_op jit(solution)/shard_map/ppermute | solution.py:233
  27.1 4.6 %collective-permute-start.2 = (bf16[128,896]{1,0:T(8,128)(2,1)S(1)}, bf16[128,896]{1,0:T(8,128)(2,1)S(1)}, u32[]{:S(2)}, u32[]{:S(2)}) collective-permute-start(bf16[128,896]{1,0:T(8,128)(2,1)S(1)} %get-tuple-element.24), channel_id=1, source_target_pairs={{0,3},{1,0},{2,1},{3,2},{4,7},{5,4},{6,5},{7,6},{8,11},{9,8},{10,9... | collective-permute-start | bytes 688136 | tf_op jit(solution)/shard_map/ppermute | solution.py:233
  31.6 0.0 copy-done.8
  31.7 0.0 copy-done.1
  31.7 0.0 copy-start.2
  31.7 1.2 copy-done.2
  32.9 1.0 shard_map.88
  33.9 0.0 copy-start.6
  33.9 0.9 copy-done.6
  34.7 0.8 copy-done.7
  35.5 2.7 %collective-permute-done.refs_2_.refs_1_ = bf16[128,896]{1,0:T(8,128)(2,1)S(1)} collective-permute-done((bf16[128,896]{1,0:T(8,128)(2,1)S(1)}, bf16[128,896]{1,0:T(8,128)(2,1)S(1)}, u32[]{:S(2)}, u32[]{:S(2)}) %collective-permute-start) | collective-permute-done | bytes 229408 | tf_op jit(solution)/shard_map/ppermute | solution.py:233
  38.2 0.0 collective-permute-done.1.refs_3_.refs_2_
  38.2 2.2 %collective-permute-done.2.refs_4_.refs_3_ = bf16[128,896]{1,0:T(8,128)(2,1)S(1)} collective-permute-done((bf16[128,896]{1,0:T(8,128)(2,1)S(1)}, bf16[128,896]{1,0:T(8,128)(2,1)S(1)}, u32[]{:S(2)}, u32[]{:S(2)}) %collective-permute-start.2) | collective-permute-done | bytes 229408 | tf_op jit(solution)/shard_map/ppermute | solution.py:233
  40.4 0.0 all-to-all-done
  40.4 1.4 shard_map.89
  41.9 9.9 %all-to-all-start.1 = ((bf16[16,16,896]{2,1,0:T(8,128)(2,1)}), bf16[16,16,896]{2,1,0:T(8,128)(2,1)S(1)}, u32[]{:S(2)}, u32[]{:S(2)}) async-start(bf16[16,16,896]{2,1,0:T(8,128)(2,1)} %bitcast.10), calls=%async_computation.1 | async-start | bytes 917504 | tf_op jit(solution)/shard_map/all_to_all | solution.py:229
  51.8 4.7 %collective-permute-start.6 = (bf16[2304,128]{1,0:T(8,128)(2,1)}, bf16[2304,128]{1,0:T(8,128)(2,1)S(1)}, u32[]{:S(2)}, u32[]{:S(2)}) collective-permute-start(bf16[2304,128]{1,0:T(8,128)(2,1)} %get-tuple-element.29), channel_id=1, source_target_pairs={{0,1},{1,2},{2,3},{3,0},{4,5},{5,6},{6,7},{7,4},{8,9},{9,10},{10,1... | collective-permute-start | bytes 1769480 | tf_op jit(solution)/shard_map/ppermute | solution.py:233
  56.5 3.1 %collective-permute-start.7 = (bf16[2304,128]{1,0:T(8,128)(2,1)}, bf16[2304,128]{1,0:T(8,128)(2,1)S(1)}, u32[]{:S(2)}, u32[]{:S(2)}) collective-permute-start(bf16[2304,128]{1,0:T(8,128)(2,1)} %copy-done.7), channel_id=1, source_target_pairs={{0,2},{1,3},{2,0},{3,1},{4,6},{5,7},{6,4},{7,5},{8,10},{9,11},{10,... | collective-permute-start | bytes 1769480 | tf_op jit(solution)/shard_map/ppermute | solution.py:233
  59.6 3.2 %collective-permute-start.8 = (bf16[2304,128]{1,0:T(8,128)(2,1)}, bf16[2304,128]{1,0:T(8,128)(2,1)}, u32[]{:S(2)}, u32[]{:S(2)}) collective-permute-start(bf16[2304,128]{1,0:T(8,128)(2,1)} %copy-done.6), channel_id=1, source_target_pairs={{0,3},{1,0},{2,1},{3,2},{4,7},{5,4},{6,5},{7,6},{8,11},{9,8},{10,9... | collective-permute-start | bytes 1769480 | tf_op jit(solution)/shard_map/ppermute | solution.py:233
  62.8 9.7 %all-to-all-done.1 = bf16[16,16,896]{2,1,0:T(8,128)(2,1)S(1)} async-done(((bf16[16,16,896]{2,1,0:T(8,128)(2,1)}), bf16[16,16,896]{2,1,0:T(8,128)(2,1)S(1)}, u32[]{:S(2)}, u32[]{:S(2)}) %all-to-all-start.1) | async-done | bytes 458784 | tf_op jit(solution)/shard_map/all_to_all | solution.py:229
  72.5 0.5 shard_map.90.refs_0_
  73.0 5.0 %collective-permute-start.5 = (bf16[256,512]{1,0:T(8,128)(2,1)S(1)}, bf16[256,512]{1,0:T(8,128)(2,1)S(1)}, u32[]{:S(2)}, u32[]{:S(2)}) collective-permute-start(bf16[256,512]{1,0:T(8,128)(2,1)S(1)} %shard_map.90.refs_0_), channel_id=1, source_target_pairs={{0,3},{1,0},{2,1},{3,2},{4,7},{5,4},{6,5},{7,6},{8,11},{9,8},{10,9... | collective-permute-start | bytes 786440 | tf_op jit(solution)/shard_map/ppermute | solution.py:233
  78.0 3.4 %collective-permute-start.4 = (bf16[256,512]{1,0:T(8,128)(2,1)S(1)}, bf16[256,512]{1,0:T(8,128)(2,1)S(1)}, u32[]{:S(2)}, u32[]{:S(2)}) collective-permute-start(bf16[256,512]{1,0:T(8,128)(2,1)S(1)} %shard_map.90.refs_0_), channel_id=1, source_target_pairs={{0,2},{1,3},{2,0},{3,1},{4,6},{5,7},{6,4},{7,5},{8,10},{9,11},{10,... | collective-permute-start | bytes 786440 | tf_op jit(solution)/shard_map/ppermute | solution.py:233
  81.4 0.0 collective-permute-done.6.refs_5_
  81.4 1.9 %collective-permute-start.3 = (bf16[256,512]{1,0:T(8,128)(2,1)S(1)}, bf16[256,512]{1,0:T(8,128)(2,1)S(1)}, u32[]{:S(2)}, u32[]{:S(2)}) collective-permute-start(bf16[256,512]{1,0:T(8,128)(2,1)S(1)} %shard_map.90.refs_0_), channel_id=1, source_target_pairs={{0,1},{1,2},{2,3},{3,0},{4,5},{5,6},{6,7},{7,4},{8,9},{9,10},{10,1... | collective-permute-start | bytes 786440 | tf_op jit(solution)/shard_map/ppermute | solution.py:233
  83.4 0.0 collective-permute-done.7.refs_6_
  83.4 1.3 collective-permute-done.8.refs_7_
  84.7 5.6 %collective-permute-done.5.refs_3_ = bf16[256,512]{1,0:T(8,128)(2,1)S(1)} collective-permute-done((bf16[256,512]{1,0:T(8,128)(2,1)S(1)}, bf16[256,512]{1,0:T(8,128)(2,1)S(1)}, u32[]{:S(2)}, u32[]{:S(2)}) %collective-permute-start.5) | collective-permute-done | bytes 262176 | tf_op jit(solution)/shard_map/ppermute | solution.py:233
  90.2 0.0 collective-permute-done.4.refs_2_
  90.2 0.0 collective-permute-done.3.refs_1_
  90.3 1.9 %shard_map.91 = bf16[256,1024]{1,0:T(8,128)(2,1)S(1)} custom-call(bf16[256,512]{1,0:T(8,128)(2,1)S(1)} %shard_map.90.refs_0_, bf16[256,512]{1,0:T(8,128)(2,1)S(1)} %collective-permute-done.3.refs_1_, bf16[256,512]{1,0:T(8,128)(2,1)S(1)} %collective-permute-done.4.refs_2_, bf16[256,512]{1,0:T(8,128)(2,1)S(1)} %collective-permute-done.5.refs_3_, ...), custom_call_target="tpu_custom_call" | custom-call | bytes 1048576 | tf_op jit(solution)/shard_map/pallas_call | solution.py:35
  92.1 39.1 %all_to_all.20 = bf16[16,16,1024]{2,1,0:T(8,128)(2,1)S(1)} all-to-all(bf16[16,16,1024]{2,1,0:T(8,128)(2,1)S(1)} %bitcast.18), channel_id=1, replica_groups=mesh['wide'=16,'narrow'=16,'tp'=4] {'narrow'}, dimensions={0} | all-to-all | bytes 1048576 | tf_op jit(solution)/shard_map/all_to_all | solution.py:229
  131.3 0.4 shard_map.92
  131.6 24.2 %all_to_all.21 = bf16[16,8,896]{2,1,0:T(8,128)(2,1)S(1)} all-to-all(bf16[16,8,896]{2,1,0:T(8,128)(2,1)S(1)} %bitcast.24), channel_id=1, replica_groups=mesh['wide'=16,'narrow'=16,'tp'=4] {'wide'}, dimensions={0} | all-to-all | bytes 458752 | tf_op jit(solution)/shard_map/all_to_all | solution.py:229
  155.9 1.2 shard_map.93
  (3 shorter events, 0.0 us)
Async XLA Ops:
  0.6 1.2 copy-start
  1.8 29.9 %copy-start.1 = (bf16[1,1,3584,128]{3,2,1,0:T(8,128)(2,1)S(1)}, bf16[1,1,3584,128]{3,2,1,0:T(8,128)(2,1)}, u32[]{:S(2)}) copy-start(bf16[1,1,3584,128]{3,2,1,0:T(8,128)(2,1)} %param.11) | copy-start | bytes 2752516
  1.9 0.8 copy-start.4
  2.6 0.9 copy-start.3
  3.5 0.7 copy-start.5
  5.6 26.0 %copy-start.8 = (bf16[1,1,256,2,128]{4,3,2,1,0:T(2,128)(2,1)S(1)}, bf16[1,1,256,2,128]{4,3,2,1,0:T(2,128)(2,1)}, u32[]{:S(2)}) copy-start(bf16[1,1,256,2,128]{4,3,2,1,0:T(2,128)(2,1)} %param.10) | copy-start | bytes 393220
  5.6 34.8 %all-to-all-start = ((bf16[16,8,896]{2,1,0:T(8,128)(2,1)}), bf16[16,8,896]{2,1,0:T(8,128)(2,1)S(1)}, u32[]{:S(2)}, u32[]{:S(2)}) async-start(bf16[16,8,896]{2,1,0:T(8,128)(2,1)} %bitcast.3), calls=%async_computation | async-start | bytes 458752 | tf_op jit(solution)/shard_map/all_to_all | solution.py:229
  23.2 15.0 %collective-permute-start = (bf16[128,896]{1,0:T(8,128)(2,1)S(1)}, bf16[128,896]{1,0:T(8,128)(2,1)S(1)}, u32[]{:S(2)}, u32[]{:S(2)}) collective-permute-start(bf16[128,896]{1,0:T(8,128)(2,1)S(1)} %get-tuple-element.22), channel_id=1, source_target_pairs={{0,1},{1,2},{2,3},{3,0},{4,5},{5,6},{6,7},{7,4},{8,9},{9,10},{10,1... | collective-permute-start | bytes 688136 | tf_op jit(solution)/shard_map/ppermute | solution.py:233
  25.1 13.1 %collective-permute-start.1 = (bf16[128,896]{1,0:T(8,128)(2,1)S(1)}, bf16[128,896]{1,0:T(8,128)(2,1)S(1)}, u32[]{:S(2)}, u32[]{:S(2)}) collective-permute-start(bf16[128,896]{1,0:T(8,128)(2,1)S(1)} %get-tuple-element.23), channel_id=1, source_target_pairs={{0,2},{1,3},{2,0},{3,1},{4,6},{5,7},{6,4},{7,5},{8,10},{9,11},{10,... | collective-permute-start | bytes 688136 | tf_op jit(solution)/shard_map/ppermute | solution.py:233
  27.1 13.4 %collective-permute-start.2 = (bf16[128,896]{1,0:T(8,128)(2,1)S(1)}, bf16[128,896]{1,0:T(8,128)(2,1)S(1)}, u32[]{:S(2)}, u32[]{:S(2)}) collective-permute-start(bf16[128,896]{1,0:T(8,128)(2,1)S(1)} %get-tuple-element.24), channel_id=1, source_target_pairs={{0,3},{1,0},{2,1},{3,2},{4,7},{5,4},{6,5},{7,6},{8,11},{9,8},{10,9... | collective-permute-start | bytes 688136 | tf_op jit(solution)/shard_map/ppermute | solution.py:233
  31.7 1.2 copy-start.2
  33.9 0.9 copy-start.6
  34.7 0.8 copy-start.7
  41.9 30.6 %all-to-all-start.1 = ((bf16[16,16,896]{2,1,0:T(8,128)(2,1)}), bf16[16,16,896]{2,1,0:T(8,128)(2,1)S(1)}, u32[]{:S(2)}, u32[]{:S(2)}) async-start(bf16[16,16,896]{2,1,0:T(8,128)(2,1)} %bitcast.10), calls=%async_computation.1 | async-start | bytes 917504 | tf_op jit(solution)/shard_map/all_to_all | solution.py:229
  51.8 29.7 %collective-permute-start.6 = (bf16[2304,128]{1,0:T(8,128)(2,1)}, bf16[2304,128]{1,0:T(8,128)(2,1)S(1)}, u32[]{:S(2)}, u32[]{:S(2)}) collective-permute-start(bf16[2304,128]{1,0:T(8,128)(2,1)} %get-tuple-element.29), channel_id=1, source_target_pairs={{0,1},{1,2},{2,3},{3,0},{4,5},{5,6},{6,7},{7,4},{8,9},{9,10},{10,1... | collective-permute-start | bytes 1769480 | tf_op jit(solution)/shard_map/ppermute | solution.py:233
  56.5 26.8 %collective-permute-start.7 = (bf16[2304,128]{1,0:T(8,128)(2,1)}, bf16[2304,128]{1,0:T(8,128)(2,1)S(1)}, u32[]{:S(2)}, u32[]{:S(2)}) collective-permute-start(bf16[2304,128]{1,0:T(8,128)(2,1)} %copy-done.7), channel_id=1, source_target_pairs={{0,2},{1,3},{2,0},{3,1},{4,6},{5,7},{6,4},{7,5},{8,10},{9,11},{10,... | collective-permute-start | bytes 1769480 | tf_op jit(solution)/shard_map/ppermute | solution.py:233
  59.6 25.1 %collective-permute-start.8 = (bf16[2304,128]{1,0:T(8,128)(2,1)}, bf16[2304,128]{1,0:T(8,128)(2,1)}, u32[]{:S(2)}, u32[]{:S(2)}) collective-permute-start(bf16[2304,128]{1,0:T(8,128)(2,1)} %copy-done.6), channel_id=1, source_target_pairs={{0,3},{1,0},{2,1},{3,2},{4,7},{5,4},{6,5},{7,6},{8,11},{9,8},{10,9... | collective-permute-start | bytes 1769480 | tf_op jit(solution)/shard_map/ppermute | solution.py:233
  73.0 17.3 %collective-permute-start.5 = (bf16[256,512]{1,0:T(8,128)(2,1)S(1)}, bf16[256,512]{1,0:T(8,128)(2,1)S(1)}, u32[]{:S(2)}, u32[]{:S(2)}) collective-permute-start(bf16[256,512]{1,0:T(8,128)(2,1)S(1)} %shard_map.90.refs_0_), channel_id=1, source_target_pairs={{0,3},{1,0},{2,1},{3,2},{4,7},{5,4},{6,5},{7,6},{8,11},{9,8},{10,9... | collective-permute-start | bytes 786440 | tf_op jit(solution)/shard_map/ppermute | solution.py:233
  78.0 12.3 %collective-permute-start.4 = (bf16[256,512]{1,0:T(8,128)(2,1)S(1)}, bf16[256,512]{1,0:T(8,128)(2,1)S(1)}, u32[]{:S(2)}, u32[]{:S(2)}) collective-permute-start(bf16[256,512]{1,0:T(8,128)(2,1)S(1)} %shard_map.90.refs_0_), channel_id=1, source_target_pairs={{0,2},{1,3},{2,0},{3,1},{4,6},{5,7},{6,4},{7,5},{8,10},{9,11},{10,... | collective-permute-start | bytes 786440 | tf_op jit(solution)/shard_map/ppermute | solution.py:233
  81.4 8.8 %collective-permute-start.3 = (bf16[256,512]{1,0:T(8,128)(2,1)S(1)}, bf16[256,512]{1,0:T(8,128)(2,1)S(1)}, u32[]{:S(2)}, u32[]{:S(2)}) collective-permute-start(bf16[256,512]{1,0:T(8,128)(2,1)S(1)} %shard_map.90.refs_0_), channel_id=1, source_target_pairs={{0,1},{1,2},{2,3},{3,0},{4,5},{5,6},{6,7},{7,4},{8,9},{9,10},{10,1... | collective-permute-start | bytes 786440 | tf_op jit(solution)/shard_map/ppermute | solution.py:233

commit v2 on v1

--- a/solution.py
+++ b/solution.py
@@ -31,13 +31,15 @@
     return jnp.where(mask, 1.0, 0.0).astype(jnp.bfloat16)
 
 
-def call(kernel, outs, args, flops=0, size=1 << 20):
+def call(kernel, outs, args, flops=0, size=1 << 20, spaces=None, scratch=(), vmem=16):
+    spaces = spaces or [pltpu.VMEM] * len(args)
     return pl.pallas_call(
         kernel,
         out_shape=outs,
-        in_specs=[pl.BlockSpec(memory_space=pltpu.VMEM)] * len(args),
+        in_specs=[pl.BlockSpec(memory_space=space) for space in spaces],
         out_specs=jax.tree.map(lambda _: pl.BlockSpec(memory_space=pltpu.VMEM), outs),
-        compiler_params=pltpu.CompilerParams(vmem_limit_bytes=40 << 20),
+        scratch_shapes=list(scratch),
+        compiler_params=pltpu.CompilerParams(vmem_limit_bytes=vmem << 20),
         cost_estimate=pl.CostEstimate(flops=flops, bytes_accessed=size, transcendentals=0),
     )(*args)
 
@@ -46,29 +48,30 @@
     return jax.ShapeDtypeStruct(dims, dtype)
 
 
-def pack_down_kernel(down_ref, *refs):
+def pack_down_kernel(steps, count, down_ref, after_ref, *out_refs):
+    width = down_ref.shape[1] // count
+    me = lax.axis_index("tp")
+    for step, out_ref in zip(steps, out_refs):
+        to = lax.rem(me + step, count)
+        out_ref[...] = down_ref[:, pl.ds(pl.multiple_of(to * width, TILE), width)]
+
+
+def pack_rest_kernel(gate_ref, up_ref, down_ref, *refs):
     out_refs, ready_ref = refs[:-1], refs[-1]
     ready_ref[...] = jnp.zeros_like(ready_ref)
     count = len(out_refs)
-    width = down_ref.shape[1] // count
-    me = lax.axis_index("tp")
-    for step, out_ref in enumerate(out_refs):
-        to = lax.rem(me + step, count)
-        out_ref[...] = down_ref[:, pl.ds(pl.multiple_of(to * width, TILE), width)]
-
-
-def pack_rest_kernel(gate_ref, up_ref, preact_ref, *refs):
-    out_refs, ready_ref = refs[:-1], refs[-1]
-    ready_ref[...] = jnp.zeros_like(ready_ref)
-    count = len(out_refs)
-    width = gate_ref.shape[0] // count
+    width, hidden = gate_ref.shape[0] // count, gate_ref.shape[1]
     me = lax.axis_index("tp")
     for step, out_ref in enumerate(out_refs):
         to = lax.rem(me + step, count)
         rows = pl.ds(pl.multiple_of(to * width, TILE), width)
         out_ref[0:width, :] = gate_ref[rows, :]
         out_ref[width : 2 * width, :] = up_ref[rows, :]
-        out_ref[2 * width :, :] = preact_ref[...]
+        if out_ref.shape[0] > 2 * width:
+            for tile in range(width // TILE):
+                lanes = pl.ds(pl.multiple_of(to * width + tile * TILE, TILE), TILE)
+                first = 2 * width + tile * hidden
+                out_ref[first : first + hidden, :] = down_ref[:, lanes]
 
 
 def spread(group_cap, rows):
@@ -88,11 +91,23 @@
     return c // width == r % BLOCK
 
 
-def first_kernel(group_cap, width, ids_ref, gates_ref, rows_ref, ready_ref, send_ref, place_ref):
+def first_kernel(
+    group_cap, width, ids_hbm, gates_hbm, rows_hbm, send_ref, place_ref, ids_ref, gates_ref, rows_ref, sems
+):
+    columns = send_ref.shape[1]
+    columns_at = pl.ds(pl.multiple_of(lax.axis_index("tp") * columns, TILE), columns)
+    copies = [
+        pltpu.make_async_copy(ids_hbm, ids_ref, sems.at[0]),
+        pltpu.make_async_copy(gates_hbm, gates_ref, sems.at[1]),
+        pltpu.make_async_copy(rows_hbm.at[:, columns_at], rows_ref, sems.at[2]),
+    ]
+    for copy in copies:
+        copy.start()
+    for copy in copies:
+        copy.wait()
     top, tokens = ids_ref.shape
     rows = send_ref.shape[0]
     groups = rows // BLOCK
-    columns = send_ref.shape[1]
     ids = ids_ref[...]
     gates = gates_ref[...].astype(jnp.float32)
     member = jnp.zeros((groups, tokens), jnp.float32)
@@ -110,8 +125,7 @@
     ).astype(jnp.float32)
     place = bits(place)
     place_ref[...] = place
-    columns_at = pl.ds(pl.multiple_of(lax.axis_index("tp") * columns, TILE), columns)
-    send_ref[...] = nn(place, rows_ref[:, columns_at]).astype(jnp.bfloat16)
+    send_ref[...] = nn(place, rows_ref[...]).astype(jnp.bfloat16)
     r, c = iota((rows, groups * width), 0), iota((rows, groups * width), 1)
     paired = nt(place, table.astype(jnp.bfloat16))
     paired = jnp.where(r // BLOCK == c // width, paired, 0.0).astype(jnp.bfloat16)
@@ -143,9 +157,19 @@
 
 
 def partial_kernel(rows_ref, *refs):
-    out_ref = refs[-1]
+    refs, out_ref = refs[:-2], refs[-1]
     rows = rows_ref[...]
-    blocks = [block_ref[...] for block_ref in refs[:-1]]
+    columns = rows_ref.shape[1]
+    blocks = []
+    for block_ref in refs:
+        if block_ref.shape[1] == columns:
+            blocks.append(block_ref[...])
+            continue
+        hidden = (block_ref.shape[0] - 2 * columns) * TILE // columns
+        firsts = [2 * columns + tile * hidden for tile in range(columns // TILE)]
+        blocks.append(
+            jnp.concatenate([block_ref[first : first + hidden, :] for first in firsts], axis=1)
+        )
     out_ref[...] = nt(rows, jnp.concatenate(blocks, axis=0)).astype(jnp.bfloat16)
 
 
@@ -158,7 +182,8 @@
 
 
 def expert_kernel(count, *refs):
-    parts, blocks, out_ref = refs[:count], refs[count : 2 * count], refs[-1]
+    parts, blocks, preacts_ref, out_ref = refs[:count], refs[count : 2 * count], *refs[-2:]
+    me = lax.axis_index("tp")
     slots = out_ref.shape[0]
     columns = out_ref.shape[1] - TILE
     hidden = parts[0].shape[1] // count
@@ -171,8 +196,9 @@
                 parts[step][:, source * hidden : (source + 1) * hidden].astype(jnp.float32)
             )
         back = cycle_sum(pieces)
-        gate_pre = blocks[at][2 * columns : 2 * columns + slots, :].astype(jnp.float32)
-        up_pre = blocks[at][2 * columns + slots :, :].astype(jnp.float32)
+        block = lax.rem(me + count - at, count)
+        gate_pre = preacts_ref[block, 0:slots, :].astype(jnp.float32)
+        up_pre = preacts_ref[block, slots : 2 * slots, :].astype(jnp.float32)
         sigmoid_value = jax.nn.sigmoid(gate_pre)
         swish_value = gate_pre * sigmoid_value
         slope = sigmoid_value * (1.0 + gate_pre * (1.0 - sigmoid_value))
@@ -235,6 +261,13 @@
     )
 
 
+def shift_all(values):
+    count = len(values)
+    order = sorted(range(1, count), key=lambda step: min(step, count - step))
+    moved = {step: shift(values[step], step, count) for step in order}
+    return [values[0]] + [moved[step] for step in range(1, count)]
+
+
 def per_device(d_out, expert_ids, gate_values, stored_preacts, w_gate, w_up, w_down):
     wide_count = lax.axis_size("wide")
     lane_count = lax.axis_size("narrow")
@@ -250,38 +283,50 @@
     lanes = group_width * lane_cap
     ids = expert_ids.T
 
-    down_packed = call(
-        pack_down_kernel,
-        [shape(hidden_width, columns)] * split_count + [shape(BLOCK, TILE)],
-        (w_down[0, 0],),
-    )
-    downs = [down_packed[0]] + [
-        shift(down_packed[step], step, split_count) for step in range(1, split_count)
-    ]
-    rest_packed = call(
-        pack_rest_kernel,
-        [shape(2 * columns + 2 * slot_count, hidden_width)] * split_count + [shape(BLOCK, TILE)],
-        (
-            w_gate[0, 0],
-            w_up[0, 0],
-            stored_preacts[0, 0].transpose(1, 0, 2).reshape(2 * slot_count, hidden_width),
-        ),
-        size=4 << 20,
-    )
-    blocks = [rest_packed[0]] + [
-        shift(rest_packed[step], step, split_count) for step in range(1, split_count)
-    ]
-
     send, place = call(
         lambda *refs: first_kernel(group_cap, group_width, *refs),
         [shape(rows, columns), shape(rows, token_count)],
-        (ids, gate_values.T, d_out, down_packed[-1]),
-    )
+        (ids, gate_values.T, d_out),
+        spaces=[pltpu.HBM] * 3,
+        vmem=60,
+        scratch=[
+            pltpu.VMEM(ids.shape, ids.dtype),
+            pltpu.VMEM(ids.shape, gate_values.dtype),
+            pltpu.VMEM((token_count, columns), d_out.dtype),
+            pltpu.SemaphoreType.DMA((3,)),
+        ],
+    )
+    half = split_count // 2
+    steps = [step for step in range(split_count) if step != half]
+    down_packed = call(
+        lambda *refs: pack_down_kernel(steps, split_count, *refs),
+        [shape(hidden_width, columns)] * len(steps),
+        (w_down[0, 0], place),
+        spaces=[pltpu.VMEM, pl.ANY],
+    )
+    downs = {
+        step: shift(block, step, split_count) if step else block
+        for step, block in zip(steps, down_packed)
+    }
+    sizes = [(3 if step == half else 2) * columns for step in range(split_count)]
+    rest_packed = call(
+        pack_rest_kernel,
+        [shape(size, hidden_width) for size in sizes] + [shape(BLOCK, TILE)],
+        (w_gate[0, 0], w_up[0, 0], w_down[0, 0]),
+        size=4 << 20,
+    )
+    blocks = shift_all(rest_packed[:-1])
+    downs[half] = blocks[half]
+    preacts = lax.all_gather(
+        stored_preacts[0, 0].transpose(1, 0, 2).reshape(2 * slot_count, hidden_width), "tp"
+    )
+
     got = exchange(send.reshape(wide_count, BLOCK, columns), "wide").reshape(rows, columns)
     forward, gated = call(
         lambda *refs: second_kernel(group_cap, group_width, lane_cap, *refs),
         [shape(HALVES, lanes, columns), shape(rows, lanes)],
-        (got, rest_packed[-1], *downs[1:]),
+        (got, rest_packed[-1], downs[1], downs[split_count - 1]),
+        spaces=[pltpu.VMEM] + [pl.ANY] * 3,
     )
     slot_rows = exchange(forward.reshape(lane_count, lane_cap, columns), "narrow").reshape(
         slot_count, columns
@@ -289,13 +334,15 @@
     partial = call(
         partial_kernel,
         shape(slot_count, split_count * hidden_width),
-        (slot_rows, *downs),
-    )
-    parts = [partial] + [shift(partial, step, split_count) for step in range(1, split_count)]
+        (slot_rows, *(downs[step] for step in range(split_count)), preacts),
+        spaces=[pltpu.VMEM] * (split_count + 1) + [pl.ANY],
+    )
+    parts = shift_all([partial] * split_count)
     terms = call(
         lambda *refs: expert_kernel(split_count, *refs),
         shape(slot_count, columns + TILE),
-        (*parts, *blocks),
+        (*parts, *blocks, preacts),
+        vmem=24,
     )
     back = exchange(terms.reshape(lane_count, lane_cap, columns + TILE), "narrow").reshape(
         slot_count, columns + TILE

time: 158 us -> 165 us (1.044)
  blocking collectives: 63.3 us -> 84.7 us
  waiting for transfers between devices: 21.5 us -> 8.74 us
  starting transfers between devices: 57.2 us -> 55.4 us
    all_gather x0 -> x1, blocking collectives: none -> 26.7 us  [per_device(): lax.all_gather(stored_preacts[0, 0].transpose(1, 0, 2).reshape(2 * slot_c...]
    all_to_all x2, waiting for transfers between devices: 9.73 us -> 0.01 us  [exchange(): return lax.all_to_all(values, axis, split_axis=0, concat_axis=0, tiled=True)]
    all_to_all x2, blocking collectives: 63.3 us -> 58 us  [exchange(): return lax.all_to_all(values, axis, split_axis=0, concat_axis=0, tiled=True)]
    ppermute x9 -> x8, waiting for transfers between devices: 11.8 us -> 8.73 us  [shift(): lax.ppermute(values, 'tp', [(source, (source + step) % count) for source...]
    ppermute x9 -> x8, starting transfers between devices: 29.7 us -> 27.2 us  [shift(): lax.ppermute(values, 'tp', [(source, (source + step) % count) for source...]
    unnamed x18 -> x22, local copies, waits for them, and re-layouts: 6.37 us -> 5.78 us
  transfers between devices with their start and end apart: 11 -> 10, of which waited for: 5 -> 3; matrix products, arithmetic and copies ran while one was open for 0% -> 0% of each run, Pallas kernels for 1% -> 1%
where the time goes in v2:
time: 165 us; the launch traced here: 163 us
  blocking collectives  84.7 us (51%)
  starting transfers between devices  55.4 us (34%)
  waiting for transfers between devices  8.74 us (5%)
  Pallas kernels  7.9 us (5%)
  local copies, waits for them, and re-layouts  5.8 us (4%)
    all_to_all x2, blocking collectives, exchange(): return lax.all_to_all(values, axis, split_axis=0, concat_axis=0, tiled=True)  58 us
    all_to_all x2, starting transfers between devices, exchange(): return lax.all_to_all(values, axis, split_axis=0, concat_axis=0, tiled=True)  28.3 us
    ppermute x8, starting transfers between devices, shift(): lax.ppermute(values, 'tp', [(source, (source + step) % count) for source...  27.2 us
    all_gather x1, blocking collectives, per_device(): lax.all_gather(stored_preacts[0, 0].transpose(1, 0, 2).reshape(2 * slot_c...  26.7 us
    ppermute x8, waiting for transfers between devices, shift(): lax.ppermute(values, 'tp', [(source, (source + step) % count) for source...  8.73 us
    pallas_call x8, Pallas kernels, call(): pl.pallas_call(kernel, out_shape=outs, in_specs=[pl.BlockSpec(memory_spac...  7.9 us
    unnamed x22, local copies, waits for them, and re-layouts  5.78 us
  transfers between devices with their start and end apart: 10, of which 3 were waited for; matrix products, arithmetic and copies ran while one was open for 0% of the time, Pallas kernels for 1%

profile of v2, /device:TPU:1, one launch (start us, length us, event | category | flops | bytes accessed | tf_op | source)
XLA Modules:
  0.0 163.4 jit_solution(11946058587172581254)
XLA Ops:
  0.6 2.2 %shard_map.86 = (bf16[128,896]{1,0:T(8,128)(2,1)}, bf16[128,16]{1,0:T(8,128)(2,1)}) custom-call(s32[8,16]{1,0:T(8,128)} %bitcast.28, bf16[8,16]{1,0:T(8,128)(2,1)} %bitcast.33, bf16[16,3584]{1,0:T(8,128)(2,1)} %refs_2_.1), custom_call_target="tpu_custom_call" | custom-call | bytes 1048576 | tf_op jit(solution)/shard_map/pallas_call | solution.py:36
  2.9 0.0 copy-start.6
  2.9 17.5 %all-to-all-start = ((bf16[16,8,896]{2,1,0:T(8,128)(2,1)}), bf16[16,8,896]{2,1,0:T(8,128)(2,1)S(1)}, u32[]{:S(2)}, u32[]{:S(2)}) async-start(bf16[16,8,896]{2,1,0:T(8,128)(2,1)} %bitcast.31), calls=%async_computation | async-start | bytes 458752 | tf_op jit(solution)/shard_map/all_to_all | solution.py:255
  20.4 0.0 copy-done.6
  20.4 0.0 copy-start
  20.4 1.2 copy-done
  21.5 0.1 shard_map.88
  21.6 0.0 copy-start.4
  21.6 0.7 copy-done.4
  22.3 1.9 %collective-permute-start = (bf16[128,896]{1,0:T(8,128)(2,1)S(1)}, bf16[128,896]{1,0:T(8,128)(2,1)S(1)}, u32[]{:S(2)}, u32[]{:S(2)}) collective-permute-start(bf16[128,896]{1,0:T(8,128)(2,1)S(1)} %get-tuple-element.19), channel_id=1, source_target_pairs={{0,1},{1,2},{2,3},{3,0},{4,5},{5,6},{6,7},{7,4},{8,9},{9,10},{10,1... | collective-permute-start | bytes 688136 | tf_op jit(solution)/shard_map/ppermute | solution.py:259
  24.2 4.6 %collective-permute-start.1 = (bf16[128,896]{1,0:T(8,128)(2,1)S(1)}, bf16[128,896]{1,0:T(8,128)(2,1)S(1)}, u32[]{:S(2)}, u32[]{:S(2)}) collective-permute-start(bf16[128,896]{1,0:T(8,128)(2,1)S(1)} %get-tuple-element.20), channel_id=1, source_target_pairs={{0,3},{1,0},{2,1},{3,2},{4,7},{5,4},{6,5},{7,6},{8,11},{9,8},{10,9... | collective-permute-start | bytes 688136 | tf_op jit(solution)/shard_map/ppermute | solution.py:259
  28.8 0.0 copy-done.1
  28.8 0.0 copy-start.2
  28.8 1.2 copy-done.2
  30.0 1.2 copy-done.3
  31.2 1.3 shard_map.87
  32.5 0.0 collective-permute-done.refs_2_.refs_1_
  32.5 0.7 collective-permute-done.1.refs_3_
  33.2 0.0 all-to-all-done
  33.2 1.4 shard_map.89
  34.7 0.6 copy-done.7
  35.3 10.8 %all-to-all-start.1 = ((bf16[16,16,896]{2,1,0:T(8,128)(2,1)}), bf16[16,16,896]{2,1,0:T(8,128)(2,1)S(1)}, u32[]{:S(2)}, u32[]{:S(2)}) async-start(bf16[16,16,896]{2,1,0:T(8,128)(2,1)} %bitcast.7), calls=%async_computation.1 | async-start | bytes 917504 | tf_op jit(solution)/shard_map/all_to_all | solution.py:255
  46.1 4.4 %collective-permute-start.2 = (bf16[2688,128]{1,0:T(8,128)(2,1)}, bf16[2688,128]{1,0:T(8,128)(2,1)S(1)}, u32[]{:S(2)}, u32[]{:S(2)}) collective-permute-start(bf16[2688,128]{1,0:T(8,128)(2,1)} %get-tuple-element.24), channel_id=1, source_target_pairs={{0,2},{1,3},{2,0},{3,1},{4,6},{5,7},{6,4},{7,5},{8,10},{9,11},{10,... | collective-permute-start | bytes 2064392 | tf_op jit(solution)/shard_map/ppermute | solution.py:259
  50.4 2.7 %collective-permute-start.6 = (bf16[1792,128]{1,0:T(8,128)(2,1)}, bf16[1792,128]{1,0:T(8,128)(2,1)S(1)}, u32[]{:S(2)}, u32[]{:S(2)}) collective-permute-start(bf16[1792,128]{1,0:T(8,128)(2,1)} %get-tuple-element.26), channel_id=1, source_target_pairs={{0,1},{1,2},{2,3},{3,0},{4,5},{5,6},{6,7},{7,4},{8,9},{9,10},{10,1... | collective-permute-start | bytes 1376264 | tf_op jit(solution)/shard_map/ppermute | solution.py:259
  53.2 3.8 %collective-permute-start.7 = (bf16[1792,128]{1,0:T(8,128)(2,1)}, bf16[1792,128]{1,0:T(8,128)(2,1)S(1)}, u32[]{:S(2)}, u32[]{:S(2)}) collective-permute-start(bf16[1792,128]{1,0:T(8,128)(2,1)} %get-tuple-element.27), channel_id=1, source_target_pairs={{0,3},{1,0},{2,1},{3,2},{4,7},{5,4},{6,5},{7,6},{8,11},{9,8},{10,9... | collective-permute-start | bytes 1376264 | tf_op jit(solution)/shard_map/ppermute | solution.py:259
  56.9 0.0 copy-done.10
  57.0 26.7 %all_gather.3.refs_4_.refs_8_ = bf16[4,512,128]{2,1,0:T(8,128)(2,1)S(1)} all-gather(bf16[1,512,128]{2,1,0:T(8,128)(2,1)S(1)} %bitcast.30), channel_id=1, replica_groups=mesh['wide'=16,'narrow'=16,'tp'=4] {'tp'}, dimensions={0}, use_global_device_ids=true | all-gather | bytes 655360 | tf_op jit(solution)/shard_map/all_gather | solution.py:320
  83.7 0.0 collective-permute-done.2.refs_2_.refs_6_
  83.7 0.0 all-to-all-done.1
  83.7 0.9 copy-done.5
  84.6 0.5 shard_map.90.refs_0_
  85.1 3.6 %collective-permute-start.3 = (bf16[256,512]{1,0:T(8,128)(2,1)S(1)}, bf16[256,512]{1,0:T(8,128)(2,1)S(1)}, u32[]{:S(2)}, u32[]{:S(2)}) collective-permute-start(bf16[256,512]{1,0:T(8,128)(2,1)S(1)} %shard_map.90.refs_0_), channel_id=1, source_target_pairs={{0,1},{1,2},{2,3},{3,0},{4,5},{5,6},{6,7},{7,4},{8,9},{9,10},{10,1... | collective-permute-start | bytes 786440 | tf_op jit(solution)/shard_map/ppermute | solution.py:259
  88.7 4.0 %collective-permute-start.4 = (bf16[256,512]{1,0:T(8,128)(2,1)S(1)}, bf16[256,512]{1,0:T(8,128)(2,1)S(1)}, u32[]{:S(2)}, u32[]{:S(2)}) collective-permute-start(bf16[256,512]{1,0:T(8,128)(2,1)S(1)} %shard_map.90.refs_0_), channel_id=1, source_target_pairs={{0,2},{1,3},{2,0},{3,1},{4,6},{5,7},{6,4},{7,5},{8,10},{9,11},{10,... | collective-permute-start | bytes 786440 | tf_op jit(solution)/shard_map/ppermute | solution.py:259
  92.7 2.2 %collective-permute-start.5 = (bf16[256,512]{1,0:T(8,128)(2,1)S(1)}, bf16[256,512]{1,0:T(8,128)(2,1)S(1)}, u32[]{:S(2)}, u32[]{:S(2)}) collective-permute-start(bf16[256,512]{1,0:T(8,128)(2,1)S(1)} %shard_map.90.refs_0_), channel_id=1, source_target_pairs={{0,3},{1,0},{2,1},{3,2},{4,7},{5,4},{6,5},{7,6},{8,11},{9,8},{10,9... | collective-permute-start | bytes 786440 | tf_op jit(solution)/shard_map/ppermute | solution.py:259
  94.9 0.0 collective-permute-done.6.refs_5_
  94.9 0.0 collective-permute-done.7.refs_7_
  95.0 0.0 collective-permute-done.3.refs_1_
  95.0 5.7 %collective-permute-done.4.refs_2_ = bf16[256,512]{1,0:T(8,128)(2,1)S(1)} collective-permute-done((bf16[256,512]{1,0:T(8,128)(2,1)S(1)}, bf16[256,512]{1,0:T(8,128)(2,1)S(1)}, u32[]{:S(2)}, u32[]{:S(2)}) %collective-permute-start.4) | collective-permute-done | bytes 262176 | tf_op jit(solution)/shard_map/ppermute | solution.py:259
  100.7 2.2 %collective-permute-done.5.refs_3_ = bf16[256,512]{1,0:T(8,128)(2,1)S(1)} collective-permute-done((bf16[256,512]{1,0:T(8,128)(2,1)S(1)}, bf16[256,512]{1,0:T(8,128)(2,1)S(1)}, u32[]{:S(2)}, u32[]{:S(2)}) %collective-permute-start.5) | collective-permute-done | bytes 262176 | tf_op jit(solution)/shard_map/ppermute | solution.py:259
  102.9 0.8 shard_map.91
  103.8 0.0 copy-start.8
  103.8 33.0 %all_to_all.20 = bf16[16,16,1024]{2,1,0:T(8,128)(2,1)S(1)} all-to-all(bf16[16,16,1024]{2,1,0:T(8,128)(2,1)S(1)} %bitcast.21), channel_id=1, replica_groups=mesh['wide'=16,'narrow'=16,'tp'=4] {'narrow'}, dimensions={0} | all-to-all | bytes 1048576 | tf_op jit(solution)/shard_map/all_to_all | solution.py:255
  136.8 0.0 copy-done.8
  136.8 0.4 shard_map.92
  137.2 0.0 copy-start.9
  137.2 25.0 %all_to_all.21 = bf16[16,8,896]{2,1,0:T(8,128)(2,1)S(1)} all-to-all(bf16[16,8,896]{2,1,0:T(8,128)(2,1)S(1)} %bitcast.24), channel_id=1, replica_groups=mesh['wide'=16,'narrow'=16,'tp'=4] {'wide'}, dimensions={0} | all-to-all | bytes 458752 | tf_op jit(solution)/shard_map/all_to_all | solution.py:255
  162.2 0.0 copy-done.9
  162.2 1.2 shard_map.93
  (6 shorter events, 0.0 us)
Async XLA Ops:
  2.9 17.5 %copy-start.6 = (bf16[128,16]{1,0:T(8,128)(2,1)S(1)}, bf16[128,16]{1,0:T(8,128)(2,1)}, u32[]{:S(2)}) copy-start(bf16[128,16]{1,0:T(8,128)(2,1)} %get-tuple-element.16.refs_1_) | copy-start | bytes 12292
  2.9 30.4 %all-to-all-start = ((bf16[16,8,896]{2,1,0:T(8,128)(2,1)}), bf16[16,8,896]{2,1,0:T(8,128)(2,1)S(1)}, u32[]{:S(2)}, u32[]{:S(2)}) async-start(bf16[16,8,896]{2,1,0:T(8,128)(2,1)} %bitcast.31), calls=%async_computation | async-start | bytes 458752 | tf_op jit(solution)/shard_map/all_to_all | solution.py:255
  20.4 1.2 copy-start
  21.5 7.3 %copy-start.1 = (bf16[1,1,128,3584]{3,2,1,0:T(8,128)(2,1)S(1)}, bf16[1,1,128,3584]{3,2,1,0:T(8,128)(2,1)}, u32[]{:S(2)}) copy-start(bf16[1,1,128,3584]{3,2,1,0:T(8,128)(2,1)} %param.13) | copy-start | bytes 2752516
  21.6 0.7 copy-start.4
  22.3 10.2 %collective-permute-start = (bf16[128,896]{1,0:T(8,128)(2,1)S(1)}, bf16[128,896]{1,0:T(8,128)(2,1)S(1)}, u32[]{:S(2)}, u32[]{:S(2)}) collective-permute-start(bf16[128,896]{1,0:T(8,128)(2,1)S(1)} %get-tuple-element.19), channel_id=1, source_target_pairs={{0,1},{1,2},{2,3},{3,0},{4,5},{5,6},{6,7},{7,4},{8,9},{9,10},{10,1... | collective-permute-start | bytes 688136 | tf_op jit(solution)/shard_map/ppermute | solution.py:259
  24.2 9.0 %collective-permute-start.1 = (bf16[128,896]{1,0:T(8,128)(2,1)S(1)}, bf16[128,896]{1,0:T(8,128)(2,1)S(1)}, u32[]{:S(2)}, u32[]{:S(2)}) collective-permute-start(bf16[128,896]{1,0:T(8,128)(2,1)S(1)} %get-tuple-element.20), channel_id=1, source_target_pairs={{0,3},{1,0},{2,1},{3,2},{4,7},{5,4},{6,5},{7,6},{8,11},{9,8},{10,9... | collective-permute-start | bytes 688136 | tf_op jit(solution)/shard_map/ppermute | solution.py:259
  28.8 1.2 copy-start.2
  30.0 1.2 copy-start.3
  34.7 0.6 copy-start.7
  35.3 21.7 %copy-start.10 = (bf16[1,1,256,2,128]{4,3,2,1,0:T(2,128)(2,1)S(1)}, bf16[1,1,256,2,128]{4,3,2,1,0:T(2,128)(2,1)}, u32[]{:S(2)}) copy-start(bf16[1,1,256,2,128]{4,3,2,1,0:T(2,128)(2,1)} %param.10) | copy-start | bytes 393220
  35.3 48.4 %all-to-all-start.1 = ((bf16[16,16,896]{2,1,0:T(8,128)(2,1)}), bf16[16,16,896]{2,1,0:T(8,128)(2,1)S(1)}, u32[]{:S(2)}, u32[]{:S(2)}) async-start(bf16[16,16,896]{2,1,0:T(8,128)(2,1)} %bitcast.7), calls=%async_computation.1 | async-start | bytes 917504 | tf_op jit(solution)/shard_map/all_to_all | solution.py:255
  46.1 37.6 %collective-permute-start.2 = (bf16[2688,128]{1,0:T(8,128)(2,1)}, bf16[2688,128]{1,0:T(8,128)(2,1)S(1)}, u32[]{:S(2)}, u32[]{:S(2)}) collective-permute-start(bf16[2688,128]{1,0:T(8,128)(2,1)} %get-tuple-element.24), channel_id=1, source_target_pairs={{0,2},{1,3},{2,0},{3,1},{4,6},{5,7},{6,4},{7,5},{8,10},{9,11},{10,... | collective-permute-start | bytes 2064392 | tf_op jit(solution)/shard_map/ppermute | solution.py:259
  50.4 44.5 %collective-permute-start.6 = (bf16[1792,128]{1,0:T(8,128)(2,1)}, bf16[1792,128]{1,0:T(8,128)(2,1)S(1)}, u32[]{:S(2)}, u32[]{:S(2)}) collective-permute-start(bf16[1792,128]{1,0:T(8,128)(2,1)} %get-tuple-element.26), channel_id=1, source_target_pairs={{0,1},{1,2},{2,3},{3,0},{4,5},{5,6},{6,7},{7,4},{8,9},{9,10},{10,1... | collective-permute-start | bytes 1376264 | tf_op jit(solution)/shard_map/ppermute | solution.py:259
  53.2 41.8 %collective-permute-start.7 = (bf16[1792,128]{1,0:T(8,128)(2,1)}, bf16[1792,128]{1,0:T(8,128)(2,1)S(1)}, u32[]{:S(2)}, u32[]{:S(2)}) collective-permute-start(bf16[1792,128]{1,0:T(8,128)(2,1)} %get-tuple-element.27), channel_id=1, source_target_pairs={{0,3},{1,0},{2,1},{3,2},{4,7},{5,4},{6,5},{7,6},{8,11},{9,8},{10,9... | collective-permute-start | bytes 1376264 | tf_op jit(solution)/shard_map/ppermute | solution.py:259
  83.7 0.9 copy-start.5
  85.1 9.9 %collective-permute-start.3 = (bf16[256,512]{1,0:T(8,128)(2,1)S(1)}, bf16[256,512]{1,0:T(8,128)(2,1)S(1)}, u32[]{:S(2)}, u32[]{:S(2)}) collective-permute-start(bf16[256,512]{1,0:T(8,128)(2,1)S(1)} %shard_map.90.refs_0_), channel_id=1, source_target_pairs={{0,1},{1,2},{2,3},{3,0},{4,5},{5,6},{6,7},{7,4},{8,9},{9,10},{10,1... | collective-permute-start | bytes 786440 | tf_op jit(solution)/shard_map/ppermute | solution.py:259
  88.7 12.0 %collective-permute-start.4 = (bf16[256,512]{1,0:T(8,128)(2,1)S(1)}, bf16[256,512]{1,0:T(8,128)(2,1)S(1)}, u32[]{:S(2)}, u32[]{:S(2)}) collective-permute-start(bf16[256,512]{1,0:T(8,128)(2,1)S(1)} %shard_map.90.refs_0_), channel_id=1, source_target_pairs={{0,2},{1,3},{2,0},{3,1},{4,6},{5,7},{6,4},{7,5},{8,10},{9,11},{10,... | collective-permute-start | bytes 786440 | tf_op jit(solution)/shard_map/ppermute | solution.py:259
  92.7 10.2 %collective-permute-start.5 = (bf16[256,512]{1,0:T(8,128)(2,1)S(1)}, bf16[256,512]{1,0:T(8,128)(2,1)S(1)}, u32[]{:S(2)}, u32[]{:S(2)}) collective-permute-start(bf16[256,512]{1,0:T(8,128)(2,1)S(1)} %shard_map.90.refs_0_), channel_id=1, source_target_pairs={{0,3},{1,0},{2,1},{3,2},{4,7},{5,4},{6,5},{7,6},{8,11},{9,8},{10,9... | collective-permute-start | bytes 786440 | tf_op jit(solution)/shard_map/ppermute | solution.py:259
  103.8 33.0 %copy-start.8 = (bf16[128,128]{1,0:T(8,128)(2,1)S(1)}, bf16[128,128]{1,0:T(8,128)(2,1)}, u32[]{:S(2)}) copy-start(bf16[128,128]{1,0:T(8,128)(2,1)} %copy-done.7) | copy-start | bytes 98308
  137.2 25.0 %copy-start.9 = (s32[16,8]{0,1:T(8,128)S(1)}, s32[16,8]{0,1:T(8,128)}, u32[]{:S(2)}) copy-start(s32[16,8]{0,1:T(8,128)} %param.8) | copy-start | bytes 1540

commit v3 on v1

--- a/solution.py
+++ b/solution.py
@@ -31,13 +31,17 @@
     return jnp.where(mask, 1.0, 0.0).astype(jnp.bfloat16)
 
 
-def call(kernel, outs, args, flops=0, size=1 << 20):
+def call(kernel, outs, args, flops=0, size=1 << 20, spaces=None, out_spaces=None, scratch=(), vmem=16):
+    spaces = spaces or [pltpu.VMEM] * len(args)
     return pl.pallas_call(
         kernel,
         out_shape=outs,
-        in_specs=[pl.BlockSpec(memory_space=pltpu.VMEM)] * len(args),
-        out_specs=jax.tree.map(lambda _: pl.BlockSpec(memory_space=pltpu.VMEM), outs),
-        compiler_params=pltpu.CompilerParams(vmem_limit_bytes=40 << 20),
+        in_specs=[pl.BlockSpec(memory_space=space) for space in spaces],
+        out_specs=[pl.BlockSpec(memory_space=space) for space in out_spaces]
+        if out_spaces
+        else jax.tree.map(lambda _: pl.BlockSpec(memory_space=pltpu.VMEM), outs),
+        scratch_shapes=list(scratch),
+        compiler_params=pltpu.CompilerParams(vmem_limit_bytes=vmem << 20),
         cost_estimate=pl.CostEstimate(flops=flops, bytes_accessed=size, transcendentals=0),
     )(*args)
 
@@ -46,20 +50,7 @@
     return jax.ShapeDtypeStruct(dims, dtype)
 
 
-def pack_down_kernel(down_ref, *refs):
-    out_refs, ready_ref = refs[:-1], refs[-1]
-    ready_ref[...] = jnp.zeros_like(ready_ref)
-    count = len(out_refs)
-    width = down_ref.shape[1] // count
-    me = lax.axis_index("tp")
-    for step, out_ref in enumerate(out_refs):
-        to = lax.rem(me + step, count)
-        out_ref[...] = down_ref[:, pl.ds(pl.multiple_of(to * width, TILE), width)]
-
-
-def pack_rest_kernel(gate_ref, up_ref, preact_ref, *refs):
-    out_refs, ready_ref = refs[:-1], refs[-1]
-    ready_ref[...] = jnp.zeros_like(ready_ref)
+def pack_rest_kernel(gate_ref, up_ref, preact_ref, after_ref, *out_refs):
     count = len(out_refs)
     width = gate_ref.shape[0] // count
     me = lax.axis_index("tp")
@@ -71,6 +62,13 @@
         out_ref[2 * width :, :] = preact_ref[...]
 
 
+def join_kernel(*refs):
+    out_ref = refs[-1]
+    hidden = refs[0].shape[0]
+    for at, block_ref in enumerate(refs[:-1]):
+        out_ref[at * hidden : (at + 1) * hidden, :] = block_ref[...]
+
+
 def spread(group_cap, rows):
     r, c = iota((rows, rows), 0), iota((rows, rows), 1)
     return bits((r // BLOCK == c // BLOCK) & (r % BLOCK == group_cap))
@@ -88,11 +86,34 @@
     return c // width == r % BLOCK
 
 
-def first_kernel(group_cap, width, ids_ref, gates_ref, rows_ref, ready_ref, send_ref, place_ref):
+def first_kernel(group_cap, width, count, ids_hbm, gates_hbm, rows_hbm, down_hbm, *refs):
+    send_ref, place_ref = refs[:2]
+    down_refs = refs[2 : 2 + count]
+    ids_ref, gates_ref, rows_ref, sems = refs[2 + count :]
+    columns = send_ref.shape[1]
+    me = lax.axis_index("tp")
+
+    def columns_of(index):
+        return pl.ds(pl.multiple_of(index * columns, TILE), columns)
+
+    loads = [
+        pltpu.make_async_copy(ids_hbm, ids_ref, sems.at[0]),
+        pltpu.make_async_copy(gates_hbm, gates_ref, sems.at[1]),
+        pltpu.make_async_copy(rows_hbm.at[:, columns_of(me)], rows_ref, sems.at[2]),
+    ]
+    packs = [
+        pltpu.make_async_copy(
+            down_hbm.at[:, columns_of(lax.rem(me + step, count))], down_ref, sems.at[3 + step]
+        )
+        for step, down_ref in enumerate(down_refs)
+    ]
+    for copy in loads + packs:
+        copy.start()
+    for copy in loads:
+        copy.wait()
     top, tokens = ids_ref.shape
     rows = send_ref.shape[0]
     groups = rows // BLOCK
-    columns = send_ref.shape[1]
     ids = ids_ref[...]
     gates = gates_ref[...].astype(jnp.float32)
     member = jnp.zeros((groups, tokens), jnp.float32)
@@ -110,8 +131,7 @@
     ).astype(jnp.float32)
     place = bits(place)
     place_ref[...] = place
-    columns_at = pl.ds(pl.multiple_of(lax.axis_index("tp") * columns, TILE), columns)
-    send_ref[...] = nn(place, rows_ref[:, columns_at]).astype(jnp.bfloat16)
+    send_ref[...] = nn(place, rows_ref[...]).astype(jnp.bfloat16)
     r, c = iota((rows, groups * width), 0), iota((rows, groups * width), 1)
     paired = nt(place, table.astype(jnp.bfloat16))
     paired = jnp.where(r // BLOCK == c // width, paired, 0.0).astype(jnp.bfloat16)
@@ -121,6 +141,8 @@
     notes = nn(spread(group_cap, rows), repeated)
     first = send_ref[:, 0:rows].astype(jnp.float32)
     send_ref[:, 0:rows] = (first + notes).astype(jnp.bfloat16)
+    for copy in packs:
+        copy.wait()
 
 
 def second_kernel(group_cap, width, lane_cap, got_ref, *refs):
@@ -142,11 +164,8 @@
         out_ref[half] = moved
 
 
-def partial_kernel(rows_ref, *refs):
-    out_ref = refs[-1]
-    rows = rows_ref[...]
-    blocks = [block_ref[...] for block_ref in refs[:-1]]
-    out_ref[...] = nt(rows, jnp.concatenate(blocks, axis=0)).astype(jnp.bfloat16)
+def partial_kernel(rows_ref, down_ref, out_ref):
+    out_ref[...] = nt(rows_ref[...], down_ref[...]).astype(jnp.bfloat16)
 
 
 def cycle_sum(terms):
@@ -235,6 +254,13 @@
     )
 
 
+def shift_all(values):
+    count = len(values)
+    order = sorted(range(1, count), key=lambda step: min(step, count - step))
+    moved = {step: shift(values[step], step, count) for step in order}
+    return [values[0]] + [moved[step] for step in range(1, count)]
+
+
 def per_device(d_out, expert_ids, gate_values, stored_preacts, w_gate, w_up, w_down):
     wide_count = lax.axis_size("wide")
     lane_count = lax.axis_size("narrow")
@@ -250,52 +276,63 @@
     lanes = group_width * lane_cap
     ids = expert_ids.T
 
-    down_packed = call(
-        pack_down_kernel,
-        [shape(hidden_width, columns)] * split_count + [shape(BLOCK, TILE)],
-        (w_down[0, 0],),
-    )
-    downs = [down_packed[0]] + [
-        shift(down_packed[step], step, split_count) for step in range(1, split_count)
-    ]
+    send, place, *down_packed = call(
+        lambda *refs: first_kernel(group_cap, group_width, split_count, *refs),
+        [shape(rows, columns), shape(rows, token_count)]
+        + [shape(hidden_width, columns)] * split_count,
+        (ids, gate_values.T, d_out, w_down[0, 0]),
+        spaces=[pltpu.HBM] * 4,
+        out_spaces=[pltpu.VMEM] * 2 + [pltpu.HBM] * split_count,
+        vmem=60,
+        scratch=[
+            pltpu.VMEM(ids.shape, ids.dtype),
+            pltpu.VMEM(ids.shape, gate_values.dtype),
+            pltpu.VMEM((token_count, columns), d_out.dtype),
+            pltpu.SemaphoreType.DMA((3 + split_count,)),
+        ],
+    )
+    downs = shift_all(down_packed)
+    down_cols = call(
+        join_kernel,
+        shape(split_count * hidden_width, columns),
+        downs,
+        size=1 << 20,
+        flops=20 * 10**9,
+    )
+
+    got = exchange(send.reshape(wide_count, BLOCK, columns), "wide").reshape(rows, columns)
+    forward, gated = call(
+        lambda *refs: second_kernel(group_cap, group_width, lane_cap, *refs),
+        [shape(HALVES, lanes, columns), shape(rows, lanes)],
+        (got,),
+    )
     rest_packed = call(
         pack_rest_kernel,
-        [shape(2 * columns + 2 * slot_count, hidden_width)] * split_count + [shape(BLOCK, TILE)],
+        [shape(2 * columns + 2 * slot_count, hidden_width)] * split_count,
         (
             w_gate[0, 0],
             w_up[0, 0],
             stored_preacts[0, 0].transpose(1, 0, 2).reshape(2 * slot_count, hidden_width),
+            gated,
         ),
         size=4 << 20,
-    )
-    blocks = [rest_packed[0]] + [
-        shift(rest_packed[step], step, split_count) for step in range(1, split_count)
-    ]
-
-    send, place = call(
-        lambda *refs: first_kernel(group_cap, group_width, *refs),
-        [shape(rows, columns), shape(rows, token_count)],
-        (ids, gate_values.T, d_out, down_packed[-1]),
-    )
-    got = exchange(send.reshape(wide_count, BLOCK, columns), "wide").reshape(rows, columns)
-    forward, gated = call(
-        lambda *refs: second_kernel(group_cap, group_width, lane_cap, *refs),
-        [shape(HALVES, lanes, columns), shape(rows, lanes)],
-        (got, rest_packed[-1], *downs[1:]),
-    )
+        spaces=[pltpu.VMEM] * 3 + [pl.ANY],
+    )
+    blocks = shift_all(rest_packed)
     slot_rows = exchange(forward.reshape(lane_count, lane_cap, columns), "narrow").reshape(
         slot_count, columns
     )
     partial = call(
         partial_kernel,
         shape(slot_count, split_count * hidden_width),
-        (slot_rows, *downs),
-    )
-    parts = [partial] + [shift(partial, step, split_count) for step in range(1, split_count)]
+        (slot_rows, down_cols),
+    )
+    parts = shift_all([partial] * split_count)
     terms = call(
         lambda *refs: expert_kernel(split_count, *refs),
         shape(slot_count, columns + TILE),
         (*parts, *blocks),
+        vmem=24,
     )
     back = exchange(terms.reshape(lane_count, lane_cap, columns + TILE), "narrow").reshape(
         slot_count, columns + TILE

time: 158 us -> 175 us (1.11)
  Pallas kernels: 7.83 us -> 37.6 us
  blocking collectives: 63.3 us -> 54.7 us
  local copies, waits for them, and re-layouts: 6.39 us -> 0.05 us
  starting transfers between devices: 57.2 us -> 59.1 us
    pallas_call x8, Pallas kernels: 7.83 us -> 37.6 us  [call(): pl.pallas_call(kernel, out_shape=outs, in_specs=[pl.BlockSpec(memory_spac...]
    all_to_all x2, blocking collectives: 63.3 us -> 54.7 us  [exchange(): return lax.all_to_all(values, axis, split_axis=0, concat_axis=0, tiled=True)]
    unnamed x18 -> x12, local copies, waits for them, and re-layouts: 6.37 us -> 0.03 us
    ppermute x9, starting transfers between devices: 29.7 us -> 31.9 us  [shift(): lax.ppermute(values, 'tp', [(source, (source + step) % count) for source...]
  transfers between devices with their start and end apart: 11 -> 11, of which waited for: 5 -> 4; matrix products, arithmetic and copies ran while one was open for 0% -> 0% of each run, Pallas kernels for 1% -> 3%
where the time goes in v3:
time: 175 us; the launch traced here: 173 us
  starting transfers between devices  59.1 us (34%)
  blocking collectives  54.7 us (31%)
  Pallas kernels  37.6 us (21%)
  waiting for transfers between devices  20.9 us (12%)
    all_to_all x2, blocking collectives, exchange(): return lax.all_to_all(values, axis, split_axis=0, concat_axis=0, tiled=True)  54.7 us
    pallas_call x8, Pallas kernels, call(): pl.pallas_call(kernel, out_shape=outs, in_specs=[pl.BlockSpec(memory_spac...  37.6 us
    ppermute x9, starting transfers between devices, shift(): lax.ppermute(values, 'tp', [(source, (source + step) % count) for source...  31.9 us
    all_to_all x2, starting transfers between devices, exchange(): return lax.all_to_all(values, axis, split_axis=0, concat_axis=0, tiled=True)  27.2 us
    ppermute x9, waiting for transfers between devices, shift(): lax.ppermute(values, 'tp', [(source, (source + step) % count) for source...  10.7 us
    all_to_all x2, waiting for transfers between devices, exchange(): return lax.all_to_all(values, axis, split_axis=0, concat_axis=0, tiled=True)  10.2 us
  transfers between devices with their start and end apart: 11, of which 4 were waited for; matrix products, arithmetic and copies ran while one was open for 0% of the time, Pallas kernels for 3%

profile of v3, /device:TPU:1, one launch (start us, length us, event | category | flops | bytes accessed | tf_op | source)
XLA Modules:
  0.0 173.2 jit_solution(14406904565631486911)
XLA Ops:
  0.6 0.0 copy-start.5
  0.6 29.7 %shard_map.86 = (bf16[128,896]{1,0:T(8,128)(2,1)}, bf16[128,16]{1,0:T(8,128)(2,1)}, bf16[128,896]{1,0:T(8,128)(2,1)}, bf16[128,896]{1,0:T(8,128)(2,1)}, bf16[128...) custom-call(s32[8,16]{1,0:T(8,128)} %bitcast.27, bf16[8,16]{1,0:T(8,128)(2,1)} %bitcast.32, bf16[16,3584]{1,0:T(8,128)(2,1)} %refs_2_.1, ...), custom_call_target="tpu_custom_call" | custom-call | bytes 1048576 | tf_op jit(solution)/shard_map/pallas_call | solution.py:36
  30.3 0.0 copy-start
  30.3 0.0 copy-start.1
  30.3 17.6 %all-to-all-start = ((bf16[16,8,896]{2,1,0:T(8,128)(2,1)}), bf16[16,8,896]{2,1,0:T(8,128)(2,1)S(1)}, u32[]{:S(2)}, u32[]{:S(2)}) async-start(bf16[16,8,896]{2,1,0:T(8,128)(2,1)} %bitcast.30), calls=%async_computation | async-start | bytes 458752 | tf_op jit(solution)/shard_map/all_to_all | solution.py:248
  48.0 1.9 %collective-permute-start = (bf16[128,896]{1,0:T(8,128)(2,1)}, bf16[128,896]{1,0:T(8,128)(2,1)}, u32[]{:S(2)}, u32[]{:S(2)}) collective-permute-start(bf16[128,896]{1,0:T(8,128)(2,1)} %get-tuple-element.21), channel_id=1, source_target_pairs={{0,1},{1,2},{2,3},{3,0},{4,5},{5,6},{6,7},{7,4},{8,9},{9,10},{10,1... | collective-permute-start | bytes 688136 | tf_op jit(solution)/shard_map/ppermute | solution.py:252
  49.9 1.9 %collective-permute-start.1 = (bf16[128,896]{1,0:T(8,128)(2,1)}, bf16[128,896]{1,0:T(8,128)(2,1)}, u32[]{:S(2)}, u32[]{:S(2)}) collective-permute-start(bf16[128,896]{1,0:T(8,128)(2,1)} %get-tuple-element.22), channel_id=1, source_target_pairs={{0,2},{1,3},{2,0},{3,1},{4,6},{5,7},{6,4},{7,5},{8,10},{9,11},{10,... | collective-permute-start | bytes 688136 | tf_op jit(solution)/shard_map/ppermute | solution.py:252
  51.8 4.6 %collective-permute-start.2 = (bf16[128,896]{1,0:T(8,128)(2,1)}, bf16[128,896]{1,0:T(8,128)(2,1)}, u32[]{:S(2)}, u32[]{:S(2)}) collective-permute-start(bf16[128,896]{1,0:T(8,128)(2,1)} %get-tuple-element.23), channel_id=1, source_target_pairs={{0,3},{1,0},{2,1},{3,2},{4,7},{5,4},{6,5},{7,6},{8,11},{9,8},{10,9... | collective-permute-start | bytes 688136 | tf_op jit(solution)/shard_map/ppermute | solution.py:252
  56.4 0.0 copy-done.5
  56.4 2.7 %all-to-all-done = bf16[16,8,896]{2,1,0:T(8,128)(2,1)S(1)} async-done(((bf16[16,8,896]{2,1,0:T(8,128)(2,1)}), bf16[16,8,896]{2,1,0:T(8,128)(2,1)S(1)}, u32[]{:S(2)}, u32[]{:S(2)}) %all-to-all-start) | async-done | bytes 229408 | tf_op jit(solution)/shard_map/all_to_all | solution.py:248
  59.1 1.4 shard_map.87
  60.6 9.6 %all-to-all-start.1 = ((bf16[16,16,896]{2,1,0:T(8,128)(2,1)}), bf16[16,16,896]{2,1,0:T(8,128)(2,1)S(1)}, u32[]{:S(2)}, u32[]{:S(2)}) async-start(bf16[16,16,896]{2,1,0:T(8,128)(2,1)} %bitcast.5), calls=%async_computation.1 | async-start | bytes 917504 | tf_op jit(solution)/shard_map/all_to_all | solution.py:248
  70.2 0.0 copy-done
  70.2 0.0 copy-done.1
  70.2 0.0 copy-start.4
  70.2 1.3 shard_map.90
  71.5 3.1 %collective-permute-start.6 = (bf16[2304,128]{1,0:T(8,128)(2,1)}, bf16[2304,128]{1,0:T(8,128)(2,1)S(1)}, u32[]{:S(2)}, u32[]{:S(2)}) collective-permute-start(bf16[2304,128]{1,0:T(8,128)(2,1)} %get-tuple-element.25), channel_id=1, source_target_pairs={{0,1},{1,2},{2,3},{3,0},{4,5},{5,6},{6,7},{7,4},{8,9},{9,10},{10,1... | collective-permute-start | bytes 1769480 | tf_op jit(solution)/shard_map/ppermute | solution.py:252
  74.7 4.4 %collective-permute-start.7 = (bf16[2304,128]{1,0:T(8,128)(2,1)}, bf16[2304,128]{1,0:T(8,128)(2,1)S(1)}, u32[]{:S(2)}, u32[]{:S(2)}) collective-permute-start(bf16[2304,128]{1,0:T(8,128)(2,1)} %get-tuple-element.26), channel_id=1, source_target_pairs={{0,2},{1,3},{2,0},{3,1},{4,6},{5,7},{6,4},{7,5},{8,10},{9,11},{10,... | collective-permute-start | bytes 1769480 | tf_op jit(solution)/shard_map/ppermute | solution.py:252
  79.0 0.0 collective-permute-done.refs_1_
  79.0 3.1 %collective-permute-start.8 = (bf16[2304,128]{1,0:T(8,128)(2,1)}, bf16[2304,128]{1,0:T(8,128)(2,1)}, u32[]{:S(2)}, u32[]{:S(2)}) collective-permute-start(bf16[2304,128]{1,0:T(8,128)(2,1)} %get-tuple-element.27), channel_id=1, source_target_pairs={{0,3},{1,0},{2,1},{3,2},{4,7},{5,4},{6,5},{7,6},{8,11},{9,8},{10,9... | collective-permute-start | bytes 1769480 | tf_op jit(solution)/shard_map/ppermute | solution.py:252
  82.1 0.0 collective-permute-done.1.refs_2_
  82.1 0.0 collective-permute-done.2.refs_3_
  82.1 0.0 copy-done.4
  82.1 1.2 shard_map.88.down_ref
  83.4 7.5 %all-to-all-done.1 = bf16[16,16,896]{2,1,0:T(8,128)(2,1)S(1)} async-done(((bf16[16,16,896]{2,1,0:T(8,128)(2,1)}), bf16[16,16,896]{2,1,0:T(8,128)(2,1)S(1)}, u32[]{:S(2)}, u32[]{:S(2)}) %all-to-all-start.1) | async-done | bytes 458784 | tf_op jit(solution)/shard_map/all_to_all | solution.py:248
  90.9 0.5 shard_map.89.refs_0_
  91.4 8.0 %collective-permute-start.5 = (bf16[256,512]{1,0:T(8,128)(2,1)S(1)}, bf16[256,512]{1,0:T(8,128)(2,1)S(1)}, u32[]{:S(2)}, u32[]{:S(2)}) collective-permute-start(bf16[256,512]{1,0:T(8,128)(2,1)S(1)} %shard_map.89.refs_0_), channel_id=1, source_target_pairs={{0,3},{1,0},{2,1},{3,2},{4,7},{5,4},{6,5},{7,6},{8,11},{9,8},{10,9... | collective-permute-start | bytes 786440 | tf_op jit(solution)/shard_map/ppermute | solution.py:252
  99.4 2.4 %collective-permute-start.4 = (bf16[256,512]{1,0:T(8,128)(2,1)S(1)}, bf16[256,512]{1,0:T(8,128)(2,1)S(1)}, u32[]{:S(2)}, u32[]{:S(2)}) collective-permute-start(bf16[256,512]{1,0:T(8,128)(2,1)S(1)} %shard_map.89.refs_0_), channel_id=1, source_target_pairs={{0,2},{1,3},{2,0},{3,1},{4,6},{5,7},{6,4},{7,5},{8,10},{9,11},{10,... | collective-permute-start | bytes 786440 | tf_op jit(solution)/shard_map/ppermute | solution.py:252
  101.8 0.0 collective-permute-done.6.refs_5_
  101.9 2.5 %collective-permute-start.3 = (bf16[256,512]{1,0:T(8,128)(2,1)S(1)}, bf16[256,512]{1,0:T(8,128)(2,1)S(1)}, u32[]{:S(2)}, u32[]{:S(2)}) collective-permute-start(bf16[256,512]{1,0:T(8,128)(2,1)S(1)} %shard_map.89.refs_0_), channel_id=1, source_target_pairs={{0,1},{1,2},{2,3},{3,0},{4,5},{5,6},{6,7},{7,4},{8,9},{9,10},{10,1... | collective-permute-start | bytes 786440 | tf_op jit(solution)/shard_map/ppermute | solution.py:252
  104.4 0.0 collective-permute-done.7.refs_6_
  104.4 0.0 collective-permute-done.8.refs_7_
  104.4 6.4 %collective-permute-done.5.refs_3_ = bf16[256,512]{1,0:T(8,128)(2,1)S(1)} collective-permute-done((bf16[256,512]{1,0:T(8,128)(2,1)S(1)}, bf16[256,512]{1,0:T(8,128)(2,1)S(1)}, u32[]{:S(2)}, u32[]{:S(2)}) %collective-permute-start.5) | collective-permute-done | bytes 262176 | tf_op jit(solution)/shard_map/ppermute | solution.py:252
  110.8 0.0 collective-permute-done.4.refs_2_
  110.8 4.2 %collective-permute-done.3.refs_1_ = bf16[256,512]{1,0:T(8,128)(2,1)S(1)} collective-permute-done((bf16[256,512]{1,0:T(8,128)(2,1)S(1)}, bf16[256,512]{1,0:T(8,128)(2,1)S(1)}, u32[]{:S(2)}, u32[]{:S(2)}) %collective-permute-start.3) | collective-permute-done | bytes 262176 | tf_op jit(solution)/shard_map/ppermute | solution.py:252
  115.0 1.9 %shard_map.91 = bf16[256,1024]{1,0:T(8,128)(2,1)S(1)} custom-call(bf16[256,512]{1,0:T(8,128)(2,1)S(1)} %shard_map.89.refs_0_, bf16[256,512]{1,0:T(8,128)(2,1)S(1)} %collective-permute-done.3.refs_1_, bf16[256,512]{1,0:T(8,128)(2,1)S(1)} %collective-permute-done.4.refs_2_, bf16[256,512]{1,0:T(8,128)(2,1)S(1)} %collective-permute-done.5.refs_3_, ...), custom_call_target="tpu_custom_call" | custom-call | bytes 1048576 | tf_op jit(solution)/shard_map/pallas_call | solution.py:36
  116.9 34.0 %all_to_all.20 = bf16[16,16,1024]{2,1,0:T(8,128)(2,1)S(1)} all-to-all(bf16[16,16,1024]{2,1,0:T(8,128)(2,1)S(1)} %bitcast.18), channel_id=1, replica_groups=mesh['wide'=16,'narrow'=16,'tp'=4] {'narrow'}, dimensions={0} | all-to-all | bytes 1048576 | tf_op jit(solution)/shard_map/all_to_all | solution.py:248
  150.9 0.4 shard_map.92
  151.3 0.0 copy-start.2
  151.3 0.0 copy-start.3
  151.3 20.7 %all_to_all.21 = bf16[16,8,896]{2,1,0:T(8,128)(2,1)S(1)} all-to-all(bf16[16,8,896]{2,1,0:T(8,128)(2,1)S(1)} %bitcast.23), channel_id=1, replica_groups=mesh['wide'=16,'narrow'=16,'tp'=4] {'wide'}, dimensions={0} | all-to-all | bytes 458752 | tf_op jit(solution)/shard_map/all_to_all | solution.py:248
  172.0 0.0 copy-done.2
  172.0 0.0 copy-done.3
  172.0 1.2 shard_map.93
  (1 shorter events, 0.0 us)
Async XLA Ops:
  0.6 55.8 %copy-start.5 = (bf16[1,1,256,2,128]{4,3,2,1,0:T(2,128)(2,1)S(1)}, bf16[1,1,256,2,128]{4,3,2,1,0:T(2,128)(2,1)}, u32[]{:S(2)}) copy-start(bf16[1,1,256,2,128]{4,3,2,1,0:T(2,128)(2,1)} %param.10) | copy-start | bytes 393220
  30.3 39.9 %copy-start = (bf16[1,1,3584,128]{3,2,1,0:T(8,128)(2,1)S(1)}, bf16[1,1,3584,128]{3,2,1,0:T(8,128)(2,1)}, u32[]{:S(2)}) copy-start(bf16[1,1,3584,128]{3,2,1,0:T(8,128)(2,1)} %param.11) | copy-start | bytes 2752516
  30.3 39.9 %copy-start.1 = (bf16[1,1,3584,128]{3,2,1,0:T(8,128)(2,1)S(1)}, bf16[1,1,3584,128]{3,2,1,0:T(8,128)(2,1)}, u32[]{:S(2)}) copy-start(bf16[1,1,3584,128]{3,2,1,0:T(8,128)(2,1)} %param.12) | copy-start | bytes 2752516
  30.3 28.8 %all-to-all-start = ((bf16[16,8,896]{2,1,0:T(8,128)(2,1)}), bf16[16,8,896]{2,1,0:T(8,128)(2,1)S(1)}, u32[]{:S(2)}, u32[]{:S(2)}) async-start(bf16[16,8,896]{2,1,0:T(8,128)(2,1)} %bitcast.30), calls=%async_computation | async-start | bytes 458752 | tf_op jit(solution)/shard_map/all_to_all | solution.py:248
  48.0 31.1 %collective-permute-start = (bf16[128,896]{1,0:T(8,128)(2,1)}, bf16[128,896]{1,0:T(8,128)(2,1)}, u32[]{:S(2)}, u32[]{:S(2)}) collective-permute-start(bf16[128,896]{1,0:T(8,128)(2,1)} %get-tuple-element.21), channel_id=1, source_target_pairs={{0,1},{1,2},{2,3},{3,0},{4,5},{5,6},{6,7},{7,4},{8,9},{9,10},{10,1... | collective-permute-start | bytes 688136 | tf_op jit(solution)/shard_map/ppermute | solution.py:252
  49.9 32.2 %collective-permute-start.1 = (bf16[128,896]{1,0:T(8,128)(2,1)}, bf16[128,896]{1,0:T(8,128)(2,1)}, u32[]{:S(2)}, u32[]{:S(2)}) collective-permute-start(bf16[128,896]{1,0:T(8,128)(2,1)} %get-tuple-element.22), channel_id=1, source_target_pairs={{0,2},{1,3},{2,0},{3,1},{4,6},{5,7},{6,4},{7,5},{8,10},{9,11},{10,... | collective-permute-start | bytes 688136 | tf_op jit(solution)/shard_map/ppermute | solution.py:252
  51.8 30.3 %collective-permute-start.2 = (bf16[128,896]{1,0:T(8,128)(2,1)}, bf16[128,896]{1,0:T(8,128)(2,1)}, u32[]{:S(2)}, u32[]{:S(2)}) collective-permute-start(bf16[128,896]{1,0:T(8,128)(2,1)} %get-tuple-element.23), channel_id=1, source_target_pairs={{0,3},{1,0},{2,1},{3,2},{4,7},{5,4},{6,5},{7,6},{8,11},{9,8},{10,9... | collective-permute-start | bytes 688136 | tf_op jit(solution)/shard_map/ppermute | solution.py:252
  60.6 30.4 %all-to-all-start.1 = ((bf16[16,16,896]{2,1,0:T(8,128)(2,1)}), bf16[16,16,896]{2,1,0:T(8,128)(2,1)S(1)}, u32[]{:S(2)}, u32[]{:S(2)}) async-start(bf16[16,16,896]{2,1,0:T(8,128)(2,1)} %bitcast.5), calls=%async_computation.1 | async-start | bytes 917504 | tf_op jit(solution)/shard_map/all_to_all | solution.py:248
  70.2 11.9 %copy-start.4 = (bf16[128,896]{1,0:T(8,128)(2,1)S(1)}, bf16[128,896]{1,0:T(8,128)(2,1)}, u32[]{:S(2)}) copy-start(bf16[128,896]{1,0:T(8,128)(2,1)} %get-tuple-element.20.refs_0_) | copy-start | bytes 688132
  71.5 30.3 %collective-permute-start.6 = (bf16[2304,128]{1,0:T(8,128)(2,1)}, bf16[2304,128]{1,0:T(8,128)(2,1)S(1)}, u32[]{:S(2)}, u32[]{:S(2)}) collective-permute-start(bf16[2304,128]{1,0:T(8,128)(2,1)} %get-tuple-element.25), channel_id=1, source_target_pairs={{0,1},{1,2},{2,3},{3,0},{4,5},{5,6},{6,7},{7,4},{8,9},{9,10},{10,1... | collective-permute-start | bytes 1769480 | tf_op jit(solution)/shard_map/ppermute | solution.py:252
  74.7 29.7 %collective-permute-start.7 = (bf16[2304,128]{1,0:T(8,128)(2,1)}, bf16[2304,128]{1,0:T(8,128)(2,1)S(1)}, u32[]{:S(2)}, u32[]{:S(2)}) collective-permute-start(bf16[2304,128]{1,0:T(8,128)(2,1)} %get-tuple-element.26), channel_id=1, source_target_pairs={{0,2},{1,3},{2,0},{3,1},{4,6},{5,7},{6,4},{7,5},{8,10},{9,11},{10,... | collective-permute-start | bytes 1769480 | tf_op jit(solution)/shard_map/ppermute | solution.py:252
  79.0 25.4 %collective-permute-start.8 = (bf16[2304,128]{1,0:T(8,128)(2,1)}, bf16[2304,128]{1,0:T(8,128)(2,1)}, u32[]{:S(2)}, u32[]{:S(2)}) collective-permute-start(bf16[2304,128]{1,0:T(8,128)(2,1)} %get-tuple-element.27), channel_id=1, source_target_pairs={{0,3},{1,0},{2,1},{3,2},{4,7},{5,4},{6,5},{7,6},{8,11},{9,8},{10,9... | collective-permute-start | bytes 1769480 | tf_op jit(solution)/shard_map/ppermute | solution.py:252
  91.4 19.4 %collective-permute-start.5 = (bf16[256,512]{1,0:T(8,128)(2,1)S(1)}, bf16[256,512]{1,0:T(8,128)(2,1)S(1)}, u32[]{:S(2)}, u32[]{:S(2)}) collective-permute-start(bf16[256,512]{1,0:T(8,128)(2,1)S(1)} %shard_map.89.refs_0_), channel_id=1, source_target_pairs={{0,3},{1,0},{2,1},{3,2},{4,7},{5,4},{6,5},{7,6},{8,11},{9,8},{10,9... | collective-permute-start | bytes 786440 | tf_op jit(solution)/shard_map/ppermute | solution.py:252
  99.4 11.4 %collective-permute-start.4 = (bf16[256,512]{1,0:T(8,128)(2,1)S(1)}, bf16[256,512]{1,0:T(8,128)(2,1)S(1)}, u32[]{:S(2)}, u32[]{:S(2)}) collective-permute-start(bf16[256,512]{1,0:T(8,128)(2,1)S(1)} %shard_map.89.refs_0_), channel_id=1, source_target_pairs={{0,2},{1,3},{2,0},{3,1},{4,6},{5,7},{6,4},{7,5},{8,10},{9,11},{10,... | collective-permute-start | bytes 786440 | tf_op jit(solution)/shard_map/ppermute | solution.py:252
  101.9 13.2 %collective-permute-start.3 = (bf16[256,512]{1,0:T(8,128)(2,1)S(1)}, bf16[256,512]{1,0:T(8,128)(2,1)S(1)}, u32[]{:S(2)}, u32[]{:S(2)}) collective-permute-start(bf16[256,512]{1,0:T(8,128)(2,1)S(1)} %shard_map.89.refs_0_), channel_id=1, source_target_pairs={{0,1},{1,2},{2,3},{3,0},{4,5},{5,6},{6,7},{7,4},{8,9},{9,10},{10,1... | collective-permute-start | bytes 786440 | tf_op jit(solution)/shard_map/ppermute | solution.py:252
  151.3 20.7 %copy-start.2 = (bf16[128,16]{1,0:T(8,128)(2,1)S(1)}, bf16[128,16]{1,0:T(8,128)(2,1)}, u32[]{:S(2)}) copy-start(bf16[128,16]{1,0:T(8,128)(2,1)} %get-tuple-element.16.refs_1_) | copy-start | bytes 12292
  151.3 20.7 %copy-start.3 = (s32[16,8]{0,1:T(8,128)S(1)}, s32[16,8]{0,1:T(8,128)}, u32[]{:S(2)}) copy-start(s32[16,8]{0,1:T(8,128)} %param.8) | copy-start | bytes 1540

commit v4 on v3

--- a/solution.py
+++ b/solution.py
@@ -282,7 +282,7 @@
         + [shape(hidden_width, columns)] * split_count,
         (ids, gate_values.T, d_out, w_down[0, 0]),
         spaces=[pltpu.HBM] * 4,
-        out_spaces=[pltpu.VMEM] * 2 + [pltpu.HBM] * split_count,
+        out_spaces=[pltpu.VMEM] * (2 + split_count),
         vmem=60,
         scratch=[
             pltpu.VMEM(ids.shape, ids.dtype),

time: 175 us -> 148 us (0.85)
  Pallas kernels: 37.6 us -> 10.6 us
    pallas_call x8, Pallas kernels: 37.6 us -> 10.6 us  [call(): pl.pallas_call(kernel, out_shape=outs, in_specs=[pl.BlockSpec(memory_spac...]
where the time goes in v4:
time: 148 us; the launch traced here: 146 us
  starting transfers between devices  59.1 us (40%)
  blocking collectives  54.6 us (37%)
  waiting for transfers between devices  20.9 us (14%)
  Pallas kernels  10.6 us (7%)
    all_to_all x2, blocking collectives, exchange(): return lax.all_to_all(values, axis, split_axis=0, concat_axis=0, tiled=True)  54.6 us
    ppermute x9, starting transfers between devices, shift(): lax.ppermute(values, 'tp', [(source, (source + step) % count) for source...  31.9 us
    all_to_all x2, starting transfers between devices, exchange(): return lax.all_to_all(values, axis, split_axis=0, concat_axis=0, tiled=True)  27.2 us
    ppermute x9, waiting for transfers between devices, shift(): lax.ppermute(values, 'tp', [(source, (source + step) % count) for source...  10.7 us
    pallas_call x8, Pallas kernels, call(): pl.pallas_call(kernel, out_shape=outs, in_specs=[pl.BlockSpec(memory_spac...  10.6 us
    all_to_all x2, waiting for transfers between devices, exchange(): return lax.all_to_all(values, axis, split_axis=0, concat_axis=0, tiled=True)  10.2 us
  transfers between devices with their start and end apart: 11, of which 4 were waited for; matrix products, arithmetic and copies ran while one was open for 0% of the time, Pallas kernels for 3%

profile of v4, /device:TPU:1, one launch (start us, length us, event | category | flops | bytes accessed | tf_op | source)
XLA Modules:
  0.0 146.2 jit_solution(14376698606166276864)
XLA Ops:
  0.6 0.0 copy-start.5
  0.6 2.6 %shard_map.86 = (bf16[128,896]{1,0:T(8,128)(2,1)}, bf16[128,16]{1,0:T(8,128)(2,1)}, bf16[128,896]{1,0:T(8,128)(2,1)}, bf16[128,896]{1,0:T(8,128)(2,1)}, bf16[128...) custom-call(s32[8,16]{1,0:T(8,128)} %bitcast.27, bf16[8,16]{1,0:T(8,128)(2,1)} %bitcast.32, bf16[16,3584]{1,0:T(8,128)(2,1)} %refs_2_.1, ...), custom_call_target="tpu_custom_call" | custom-call | bytes 1048576 | tf_op jit(solution)/shard_map/pallas_call | solution.py:36
  3.3 0.0 copy-start
  3.3 0.0 copy-start.1
  3.3 17.6 %all-to-all-start = ((bf16[16,8,896]{2,1,0:T(8,128)(2,1)}), bf16[16,8,896]{2,1,0:T(8,128)(2,1)S(1)}, u32[]{:S(2)}, u32[]{:S(2)}) async-start(bf16[16,8,896]{2,1,0:T(8,128)(2,1)} %bitcast.30), calls=%async_computation | async-start | bytes 458752 | tf_op jit(solution)/shard_map/all_to_all | solution.py:248
  20.9 1.9 %collective-permute-start = (bf16[128,896]{1,0:T(8,128)(2,1)}, bf16[128,896]{1,0:T(8,128)(2,1)}, u32[]{:S(2)}, u32[]{:S(2)}) collective-permute-start(bf16[128,896]{1,0:T(8,128)(2,1)} %get-tuple-element.21), channel_id=1, source_target_pairs={{0,1},{1,2},{2,3},{3,0},{4,5},{5,6},{6,7},{7,4},{8,9},{9,10},{10,1... | collective-permute-start | bytes 688136 | tf_op jit(solution)/shard_map/ppermute | solution.py:252
  22.8 1.9 %collective-permute-start.1 = (bf16[128,896]{1,0:T(8,128)(2,1)}, bf16[128,896]{1,0:T(8,128)(2,1)}, u32[]{:S(2)}, u32[]{:S(2)}) collective-permute-start(bf16[128,896]{1,0:T(8,128)(2,1)} %get-tuple-element.22), channel_id=1, source_target_pairs={{0,2},{1,3},{2,0},{3,1},{4,6},{5,7},{6,4},{7,5},{8,10},{9,11},{10,... | collective-permute-start | bytes 688136 | tf_op jit(solution)/shard_map/ppermute | solution.py:252
  24.8 4.6 %collective-permute-start.2 = (bf16[128,896]{1,0:T(8,128)(2,1)}, bf16[128,896]{1,0:T(8,128)(2,1)}, u32[]{:S(2)}, u32[]{:S(2)}) collective-permute-start(bf16[128,896]{1,0:T(8,128)(2,1)} %get-tuple-element.23), channel_id=1, source_target_pairs={{0,3},{1,0},{2,1},{3,2},{4,7},{5,4},{6,5},{7,6},{8,11},{9,8},{10,9... | collective-permute-start | bytes 688136 | tf_op jit(solution)/shard_map/ppermute | solution.py:252
  29.3 0.0 copy-done.5
  29.4 2.7 %all-to-all-done = bf16[16,8,896]{2,1,0:T(8,128)(2,1)S(1)} async-done(((bf16[16,8,896]{2,1,0:T(8,128)(2,1)}), bf16[16,8,896]{2,1,0:T(8,128)(2,1)S(1)}, u32[]{:S(2)}, u32[]{:S(2)}) %all-to-all-start) | async-done | bytes 229408 | tf_op jit(solution)/shard_map/all_to_all | solution.py:248
  32.1 1.4 shard_map.87
  33.5 9.6 %all-to-all-start.1 = ((bf16[16,16,896]{2,1,0:T(8,128)(2,1)}), bf16[16,16,896]{2,1,0:T(8,128)(2,1)S(1)}, u32[]{:S(2)}, u32[]{:S(2)}) async-start(bf16[16,16,896]{2,1,0:T(8,128)(2,1)} %bitcast.5), calls=%async_computation.1 | async-start | bytes 917504 | tf_op jit(solution)/shard_map/all_to_all | solution.py:248
  43.1 0.0 copy-done
  43.1 0.0 copy-done.1
  43.2 0.0 copy-start.4
  43.2 1.3 shard_map.90
  44.5 3.1 %collective-permute-start.6 = (bf16[2304,128]{1,0:T(8,128)(2,1)}, bf16[2304,128]{1,0:T(8,128)(2,1)S(1)}, u32[]{:S(2)}, u32[]{:S(2)}) collective-permute-start(bf16[2304,128]{1,0:T(8,128)(2,1)} %get-tuple-element.25), channel_id=1, source_target_pairs={{0,1},{1,2},{2,3},{3,0},{4,5},{5,6},{6,7},{7,4},{8,9},{9,10},{10,1... | collective-permute-start | bytes 1769480 | tf_op jit(solution)/shard_map/ppermute | solution.py:252
  47.6 4.4 %collective-permute-start.7 = (bf16[2304,128]{1,0:T(8,128)(2,1)}, bf16[2304,128]{1,0:T(8,128)(2,1)S(1)}, u32[]{:S(2)}, u32[]{:S(2)}) collective-permute-start(bf16[2304,128]{1,0:T(8,128)(2,1)} %get-tuple-element.26), channel_id=1, source_target_pairs={{0,2},{1,3},{2,0},{3,1},{4,6},{5,7},{6,4},{7,5},{8,10},{9,11},{10,... | collective-permute-start | bytes 1769480 | tf_op jit(solution)/shard_map/ppermute | solution.py:252
  52.0 0.0 collective-permute-done.refs_1_
  52.0 3.1 %collective-permute-start.8 = (bf16[2304,128]{1,0:T(8,128)(2,1)}, bf16[2304,128]{1,0:T(8,128)(2,1)}, u32[]{:S(2)}, u32[]{:S(2)}) collective-permute-start(bf16[2304,128]{1,0:T(8,128)(2,1)} %get-tuple-element.27), channel_id=1, source_target_pairs={{0,3},{1,0},{2,1},{3,2},{4,7},{5,4},{6,5},{7,6},{8,11},{9,8},{10,9... | collective-permute-start | bytes 1769480 | tf_op jit(solution)/shard_map/ppermute | solution.py:252
  55.1 0.0 collective-permute-done.1.refs_2_
  55.1 0.0 collective-permute-done.2.refs_3_
  55.1 0.0 copy-done.4
  55.1 1.2 shard_map.88.down_ref
  56.3 7.5 %all-to-all-done.1 = bf16[16,16,896]{2,1,0:T(8,128)(2,1)S(1)} async-done(((bf16[16,16,896]{2,1,0:T(8,128)(2,1)}), bf16[16,16,896]{2,1,0:T(8,128)(2,1)S(1)}, u32[]{:S(2)}, u32[]{:S(2)}) %all-to-all-start.1) | async-done | bytes 458784 | tf_op jit(solution)/shard_map/all_to_all | solution.py:248
  63.9 0.5 shard_map.89.refs_0_
  64.3 8.0 %collective-permute-start.5 = (bf16[256,512]{1,0:T(8,128)(2,1)S(1)}, bf16[256,512]{1,0:T(8,128)(2,1)S(1)}, u32[]{:S(2)}, u32[]{:S(2)}) collective-permute-start(bf16[256,512]{1,0:T(8,128)(2,1)S(1)} %shard_map.89.refs_0_), channel_id=1, source_target_pairs={{0,3},{1,0},{2,1},{3,2},{4,7},{5,4},{6,5},{7,6},{8,11},{9,8},{10,9... | collective-permute-start | bytes 786440 | tf_op jit(solution)/shard_map/ppermute | solution.py:252
  72.4 2.4 %collective-permute-start.4 = (bf16[256,512]{1,0:T(8,128)(2,1)S(1)}, bf16[256,512]{1,0:T(8,128)(2,1)S(1)}, u32[]{:S(2)}, u32[]{:S(2)}) collective-permute-start(bf16[256,512]{1,0:T(8,128)(2,1)S(1)} %shard_map.89.refs_0_), channel_id=1, source_target_pairs={{0,2},{1,3},{2,0},{3,1},{4,6},{5,7},{6,4},{7,5},{8,10},{9,11},{10,... | collective-permute-start | bytes 786440 | tf_op jit(solution)/shard_map/ppermute | solution.py:252
  74.8 0.0 collective-permute-done.6.refs_5_
  74.8 2.5 %collective-permute-start.3 = (bf16[256,512]{1,0:T(8,128)(2,1)S(1)}, bf16[256,512]{1,0:T(8,128)(2,1)S(1)}, u32[]{:S(2)}, u32[]{:S(2)}) collective-permute-start(bf16[256,512]{1,0:T(8,128)(2,1)S(1)} %shard_map.89.refs_0_), channel_id=1, source_target_pairs={{0,1},{1,2},{2,3},{3,0},{4,5},{5,6},{6,7},{7,4},{8,9},{9,10},{10,1... | collective-permute-start | bytes 786440 | tf_op jit(solution)/shard_map/ppermute | solution.py:252
  77.3 0.0 collective-permute-done.7.refs_6_
  77.3 0.0 collective-permute-done.8.refs_7_
  77.3 6.4 %collective-permute-done.5.refs_3_ = bf16[256,512]{1,0:T(8,128)(2,1)S(1)} collective-permute-done((bf16[256,512]{1,0:T(8,128)(2,1)S(1)}, bf16[256,512]{1,0:T(8,128)(2,1)S(1)}, u32[]{:S(2)}, u32[]{:S(2)}) %collective-permute-start.5) | collective-permute-done | bytes 262176 | tf_op jit(solution)/shard_map/ppermute | solution.py:252
  83.8 0.0 collective-permute-done.4.refs_2_
  83.8 4.3 %collective-permute-done.3.refs_1_ = bf16[256,512]{1,0:T(8,128)(2,1)S(1)} collective-permute-done((bf16[256,512]{1,0:T(8,128)(2,1)S(1)}, bf16[256,512]{1,0:T(8,128)(2,1)S(1)}, u32[]{:S(2)}, u32[]{:S(2)}) %collective-permute-start.3) | collective-permute-done | bytes 262176 | tf_op jit(solution)/shard_map/ppermute | solution.py:252
  88.0 1.9 %shard_map.91 = bf16[256,1024]{1,0:T(8,128)(2,1)S(1)} custom-call(bf16[256,512]{1,0:T(8,128)(2,1)S(1)} %shard_map.89.refs_0_, bf16[256,512]{1,0:T(8,128)(2,1)S(1)} %collective-permute-done.3.refs_1_, bf16[256,512]{1,0:T(8,128)(2,1)S(1)} %collective-permute-done.4.refs_2_, bf16[256,512]{1,0:T(8,128)(2,1)S(1)} %collective-permute-done.5.refs_3_, ...), custom_call_target="tpu_custom_call" | custom-call | bytes 1048576 | tf_op jit(solution)/shard_map/pallas_call | solution.py:36
  89.9 34.0 %all_to_all.20 = bf16[16,16,1024]{2,1,0:T(8,128)(2,1)S(1)} all-to-all(bf16[16,16,1024]{2,1,0:T(8,128)(2,1)S(1)} %bitcast.18), channel_id=1, replica_groups=mesh['wide'=16,'narrow'=16,'tp'=4] {'narrow'}, dimensions={0} | all-to-all | bytes 1048576 | tf_op jit(solution)/shard_map/all_to_all | solution.py:248
  123.9 0.4 shard_map.92
  124.3 0.0 copy-start.2
  124.3 0.0 copy-start.3
  124.3 20.7 %all_to_all.21 = bf16[16,8,896]{2,1,0:T(8,128)(2,1)S(1)} all-to-all(bf16[16,8,896]{2,1,0:T(8,128)(2,1)S(1)} %bitcast.23), channel_id=1, replica_groups=mesh['wide'=16,'narrow'=16,'tp'=4] {'wide'}, dimensions={0} | all-to-all | bytes 458752 | tf_op jit(solution)/shard_map/all_to_all | solution.py:248
  145.0 0.0 copy-done.2
  145.0 0.0 copy-done.3
  145.0 1.2 shard_map.93
  (1 shorter events, 0.0 us)
Async XLA Ops:
  0.6 28.7 %copy-start.5 = (bf16[1,1,256,2,128]{4,3,2,1,0:T(2,128)(2,1)S(1)}, bf16[1,1,256,2,128]{4,3,2,1,0:T(2,128)(2,1)}, u32[]{:S(2)}) copy-start(bf16[1,1,256,2,128]{4,3,2,1,0:T(2,128)(2,1)} %param.10) | copy-start | bytes 393220
  3.3 39.9 %copy-start = (bf16[1,1,3584,128]{3,2,1,0:T(8,128)(2,1)S(1)}, bf16[1,1,3584,128]{3,2,1,0:T(8,128)(2,1)}, u32[]{:S(2)}) copy-start(bf16[1,1,3584,128]{3,2,1,0:T(8,128)(2,1)} %param.11) | copy-start | bytes 2752516
  3.3 39.9 %copy-start.1 = (bf16[1,1,3584,128]{3,2,1,0:T(8,128)(2,1)S(1)}, bf16[1,1,3584,128]{3,2,1,0:T(8,128)(2,1)}, u32[]{:S(2)}) copy-start(bf16[1,1,3584,128]{3,2,1,0:T(8,128)(2,1)} %param.12) | copy-start | bytes 2752516
  3.3 28.8 %all-to-all-start = ((bf16[16,8,896]{2,1,0:T(8,128)(2,1)}), bf16[16,8,896]{2,1,0:T(8,128)(2,1)S(1)}, u32[]{:S(2)}, u32[]{:S(2)}) async-start(bf16[16,8,896]{2,1,0:T(8,128)(2,1)} %bitcast.30), calls=%async_computation | async-start | bytes 458752 | tf_op jit(solution)/shard_map/all_to_all | solution.py:248
  20.9 31.1 %collective-permute-start = (bf16[128,896]{1,0:T(8,128)(2,1)}, bf16[128,896]{1,0:T(8,128)(2,1)}, u32[]{:S(2)}, u32[]{:S(2)}) collective-permute-start(bf16[128,896]{1,0:T(8,128)(2,1)} %get-tuple-element.21), channel_id=1, source_target_pairs={{0,1},{1,2},{2,3},{3,0},{4,5},{5,6},{6,7},{7,4},{8,9},{9,10},{10,1... | collective-permute-start | bytes 688136 | tf_op jit(solution)/shard_map/ppermute | solution.py:252
  22.8 32.2 %collective-permute-start.1 = (bf16[128,896]{1,0:T(8,128)(2,1)}, bf16[128,896]{1,0:T(8,128)(2,1)}, u32[]{:S(2)}, u32[]{:S(2)}) collective-permute-start(bf16[128,896]{1,0:T(8,128)(2,1)} %get-tuple-element.22), channel_id=1, source_target_pairs={{0,2},{1,3},{2,0},{3,1},{4,6},{5,7},{6,4},{7,5},{8,10},{9,11},{10,... | collective-permute-start | bytes 688136 | tf_op jit(solution)/shard_map/ppermute | solution.py:252
  24.8 30.3 %collective-permute-start.2 = (bf16[128,896]{1,0:T(8,128)(2,1)}, bf16[128,896]{1,0:T(8,128)(2,1)}, u32[]{:S(2)}, u32[]{:S(2)}) collective-permute-start(bf16[128,896]{1,0:T(8,128)(2,1)} %get-tuple-element.23), channel_id=1, source_target_pairs={{0,3},{1,0},{2,1},{3,2},{4,7},{5,4},{6,5},{7,6},{8,11},{9,8},{10,9... | collective-permute-start | bytes 688136 | tf_op jit(solution)/shard_map/ppermute | solution.py:252
  33.5 30.4 %all-to-all-start.1 = ((bf16[16,16,896]{2,1,0:T(8,128)(2,1)}), bf16[16,16,896]{2,1,0:T(8,128)(2,1)S(1)}, u32[]{:S(2)}, u32[]{:S(2)}) async-start(bf16[16,16,896]{2,1,0:T(8,128)(2,1)} %bitcast.5), calls=%async_computation.1 | async-start | bytes 917504 | tf_op jit(solution)/shard_map/all_to_all | solution.py:248
  43.2 11.9 %copy-start.4 = (bf16[128,896]{1,0:T(8,128)(2,1)S(1)}, bf16[128,896]{1,0:T(8,128)(2,1)}, u32[]{:S(2)}) copy-start(bf16[128,896]{1,0:T(8,128)(2,1)} %get-tuple-element.20.refs_0_) | copy-start | bytes 688132
  44.5 30.3 %collective-permute-start.6 = (bf16[2304,128]{1,0:T(8,128)(2,1)}, bf16[2304,128]{1,0:T(8,128)(2,1)S(1)}, u32[]{:S(2)}, u32[]{:S(2)}) collective-permute-start(bf16[2304,128]{1,0:T(8,128)(2,1)} %get-tuple-element.25), channel_id=1, source_target_pairs={{0,1},{1,2},{2,3},{3,0},{4,5},{5,6},{6,7},{7,4},{8,9},{9,10},{10,1... | collective-permute-start | bytes 1769480 | tf_op jit(solution)/shard_map/ppermute | solution.py:252
  47.6 29.7 %collective-permute-start.7 = (bf16[2304,128]{1,0:T(8,128)(2,1)}, bf16[2304,128]{1,0:T(8,128)(2,1)S(1)}, u32[]{:S(2)}, u32[]{:S(2)}) collective-permute-start(bf16[2304,128]{1,0:T(8,128)(2,1)} %get-tuple-element.26), channel_id=1, source_target_pairs={{0,2},{1,3},{2,0},{3,1},{4,6},{5,7},{6,4},{7,5},{8,10},{9,11},{10,... | collective-permute-start | bytes 1769480 | tf_op jit(solution)/shard_map/ppermute | solution.py:252
  52.0 25.3 %collective-permute-start.8 = (bf16[2304,128]{1,0:T(8,128)(2,1)}, bf16[2304,128]{1,0:T(8,128)(2,1)}, u32[]{:S(2)}, u32[]{:S(2)}) collective-permute-start(bf16[2304,128]{1,0:T(8,128)(2,1)} %get-tuple-element.27), channel_id=1, source_target_pairs={{0,3},{1,0},{2,1},{3,2},{4,7},{5,4},{6,5},{7,6},{8,11},{9,8},{10,9... | collective-permute-start | bytes 1769480 | tf_op jit(solution)/shard_map/ppermute | solution.py:252
  64.3 19.4 %collective-permute-start.5 = (bf16[256,512]{1,0:T(8,128)(2,1)S(1)}, bf16[256,512]{1,0:T(8,128)(2,1)S(1)}, u32[]{:S(2)}, u32[]{:S(2)}) collective-permute-start(bf16[256,512]{1,0:T(8,128)(2,1)S(1)} %shard_map.89.refs_0_), channel_id=1, source_target_pairs={{0,3},{1,0},{2,1},{3,2},{4,7},{5,4},{6,5},{7,6},{8,11},{9,8},{10,9... | collective-permute-start | bytes 786440 | tf_op jit(solution)/shard_map/ppermute | solution.py:252
  72.4 11.4 %collective-permute-start.4 = (bf16[256,512]{1,0:T(8,128)(2,1)S(1)}, bf16[256,512]{1,0:T(8,128)(2,1)S(1)}, u32[]{:S(2)}, u32[]{:S(2)}) collective-permute-start(bf16[256,512]{1,0:T(8,128)(2,1)S(1)} %shard_map.89.refs_0_), channel_id=1, source_target_pairs={{0,2},{1,3},{2,0},{3,1},{4,6},{5,7},{6,4},{7,5},{8,10},{9,11},{10,... | collective-permute-start | bytes 786440 | tf_op jit(solution)/shard_map/ppermute | solution.py:252
  74.8 13.2 %collective-permute-start.3 = (bf16[256,512]{1,0:T(8,128)(2,1)S(1)}, bf16[256,512]{1,0:T(8,128)(2,1)S(1)}, u32[]{:S(2)}, u32[]{:S(2)}) collective-permute-start(bf16[256,512]{1,0:T(8,128)(2,1)S(1)} %shard_map.89.refs_0_), channel_id=1, source_target_pairs={{0,1},{1,2},{2,3},{3,0},{4,5},{5,6},{6,7},{7,4},{8,9},{9,10},{10,1... | collective-permute-start | bytes 786440 | tf_op jit(solution)/shard_map/ppermute | solution.py:252
  124.3 20.7 %copy-start.2 = (bf16[128,16]{1,0:T(8,128)(2,1)S(1)}, bf16[128,16]{1,0:T(8,128)(2,1)}, u32[]{:S(2)}) copy-start(bf16[128,16]{1,0:T(8,128)(2,1)} %get-tuple-element.16.refs_1_) | copy-start | bytes 12292
  124.3 20.7 %copy-start.3 = (s32[16,8]{0,1:T(8,128)S(1)}, s32[16,8]{0,1:T(8,128)}, u32[]{:S(2)}) copy-start(s32[16,8]{0,1:T(8,128)} %param.8) | copy-start | bytes 1540

commit v5 on v4

--- a/solution.py
+++ b/solution.py
@@ -176,48 +176,72 @@
     return terms[0]
 
 
-def expert_kernel(count, *refs):
-    parts, blocks, out_ref = refs[:count], refs[count : 2 * count], refs[-1]
-    slots = out_ref.shape[0]
-    columns = out_ref.shape[1] - TILE
-    hidden = parts[0].shape[1] // count
-    grads, weights, scores = [], [], []
+def prepare_kernel(*refs):
+    blocks, (weight_ref, swish_ref, slope_ref, hidden_ref) = refs[:-4], refs[-4:]
+    columns = weight_ref.shape[0]
+    slots = swish_ref.shape[0]
+    for at, block_ref in enumerate(blocks):
+        for part in range(2):
+            first = (2 * at + part) * TILE
+            weight_ref[:, first : first + TILE] = block_ref[part * columns : (part + 1) * columns, :]
+        gate_pre = block_ref[2 * columns : 2 * columns + slots, :].astype(jnp.float32)
+        up_pre = block_ref[2 * columns + slots :, :].astype(jnp.float32)
+        sigmoid_value = jax.nn.sigmoid(gate_pre)
+        swish_value = gate_pre * sigmoid_value
+        lanes = slice(at * TILE, (at + 1) * TILE)
+        swish_ref[:, lanes] = swish_value
+        slope_ref[:, lanes] = up_pre * (sigmoid_value * (1.0 + gate_pre * (1.0 - sigmoid_value)))
+        hidden_ref[:, lanes] = swish_value * up_pre
+
+
+def expert_kernel(count, lane_cap, *refs):
+    parts = refs[:count]
+    weight_ref, swish_ref, slope_ref, hidden_ref, out_ref = refs[count:]
+    slots = parts[0].shape[0]
+    columns = weight_ref.shape[0]
+    grads, scores = [], []
     for at in range(count):
         pieces = []
         for step in range(count):
             source = (at - step) % count
             pieces.append(
-                parts[step][:, source * hidden : (source + 1) * hidden].astype(jnp.float32)
+                parts[step][:, source * TILE : (source + 1) * TILE].astype(jnp.float32)
             )
         back = cycle_sum(pieces)
-        gate_pre = blocks[at][2 * columns : 2 * columns + slots, :].astype(jnp.float32)
-        up_pre = blocks[at][2 * columns + slots :, :].astype(jnp.float32)
-        sigmoid_value = jax.nn.sigmoid(gate_pre)
-        swish_value = gate_pre * sigmoid_value
-        slope = sigmoid_value * (1.0 + gate_pre * (1.0 - sigmoid_value))
-        up_part = swish_value * back
-        scores.append(up_part * up_pre)
-        grads.append((back * up_pre * slope).astype(jnp.bfloat16))
-        grads.append(up_part.astype(jnp.bfloat16))
-        weights.append(blocks[at][0:columns, :])
-        weights.append(blocks[at][columns : 2 * columns, :])
-    total = nt(jnp.concatenate(grads, axis=1), jnp.concatenate(weights, axis=1))
-    out_ref[:, 0:columns] = total.astype(jnp.bfloat16)
+        lanes = slice(at * TILE, (at + 1) * TILE)
+        scores.append(hidden_ref[:, lanes] * back)
+        grads.append((slope_ref[:, lanes] * back).astype(jnp.bfloat16))
+        grads.append((swish_ref[:, lanes] * back).astype(jnp.bfloat16))
+    total = nt(jnp.concatenate(grads, axis=1), weight_ref[...]).astype(jnp.bfloat16)
+    lane_count = slots // lane_cap
+    pieces = [
+        total[:, first : first + TILE].reshape(lane_count, lane_cap, TILE)
+        for first in range(0, columns, TILE)
+    ]
     score = jnp.sum(cycle_sum(scores), axis=1, keepdims=True)
-    out_ref[:, columns:] = jnp.broadcast_to(score, (slots, TILE)).astype(jnp.bfloat16)
+    lane = lax.rem(lax.axis_index("narrow"), lane_count // HALVES)
+    slot, place = iota((slots, TILE), 0), iota((slots, TILE), 1)
+    score = jnp.where(place == lane * lane_cap + slot % lane_cap, score, 0.0)
+    score = jnp.sum(score.reshape(lane_count, lane_cap, TILE), axis=1, keepdims=True)
+    pieces.append(jnp.broadcast_to(score, (lane_count, BLOCK, TILE)).astype(jnp.bfloat16))
+    out_ref[...] = jnp.concatenate(pieces, axis=1)
 
 
 def rows_kernel(group_cap, width, lane_cap, gated_ref, back_ref, out_ref):
     rows, columns = out_ref.shape
     gated = gated_ref[...]
+    lane_count = back_ref.shape[0]
+    pieces = [
+        back_ref[:, tile * lane_cap : (tile + 1) * lane_cap, :].reshape(lane_count * lane_cap, TILE)
+        for tile in range(columns // TILE)
+    ]
     both = jnp.concatenate([gated, gated], axis=1)
-    out_ref[...] = nn(both, back_ref[:, 0:columns]).astype(jnp.bfloat16)
-    place = bits(both != 0)
-    slots = both.shape[1]
-    a, b = iota((slots, TILE), 0), iota((slots, TILE), 1)
-    score = back_ref[:, columns:].astype(jnp.float32)
-    score = jnp.where((a // lane_cap) % width == b % width, score, 0.0).astype(jnp.bfloat16)
-    score = nn(place, score)
+    out_ref[...] = nn(both, jnp.concatenate(pieces, axis=1)).astype(jnp.bfloat16)
+    score = back_ref[...][:, columns // TILE * lane_cap :, :].astype(jnp.float32)
+    score = jnp.sum(jnp.sum(score, axis=0)[0:1, :], axis=0, keepdims=True)
+    score = jnp.where(gated != 0, score, 0.0).astype(jnp.bfloat16)
+    a, b = iota((rows, TILE), 0), iota((rows, TILE), 1)
+    score = nn(score, bits(a // lane_cap == b % width))
     score = jnp.where(own_span(rows, width), score, 0.0).astype(jnp.bfloat16)
     notes = nn(spread(group_cap, rows), score)
     first = out_ref[:, 0:rows].astype(jnp.float32)
@@ -328,15 +352,22 @@
         (slot_rows, down_cols),
     )
     parts = shift_all([partial] * split_count)
+    hidden_all = split_count * hidden_width
+    prepared = call(
+        prepare_kernel,
+        [shape(columns, 2 * hidden_all)]
+        + [shape(slot_count, hidden_all, dtype=jnp.float32)] * 3,
+        blocks,
+        size=8 << 20,
+    )
+    block_rows = columns // TILE * lane_cap + BLOCK
     terms = call(
-        lambda *refs: expert_kernel(split_count, *refs),
-        shape(slot_count, columns + TILE),
-        (*parts, *blocks),
+        lambda *refs: expert_kernel(split_count, lane_cap, *refs),
+        shape(lane_count, block_rows, TILE),
+        (*parts, *prepared),
         vmem=24,
     )
-    back = exchange(terms.reshape(lane_count, lane_cap, columns + TILE), "narrow").reshape(
-        slot_count, columns + TILE
-    )
+    back = exchange(terms, "narrow")
     row_input = call(
         lambda *refs: rows_kernel(group_cap, group_width, lane_cap, *refs),
         shape(rows, columns),

time: 148 us -> 146 us (0.986)
  waiting for transfers between devices: 20.9 us -> 17.5 us
  local copies, waits for them, and re-layouts: 0.05 us -> 1.88 us
    ppermute x9, waiting for transfers between devices: 10.7 us -> 8.53 us  [shift(): lax.ppermute(values, 'tp', [(source, (source + step) % count) for source...]
    pallas_call x8 -> x9, Pallas kernels: 10.6 us -> 11.2 us  [call(): pl.pallas_call(kernel, out_shape=outs, in_specs=[pl.BlockSpec(memory_spac...]
  transfers between devices with their start and end apart: 11 -> 11, of which waited for: 4 -> 5; matrix products, arithmetic and copies ran while one was open for 0% -> 1% of each run, Pallas kernels for 3% -> 4%
where the time goes in v5:
time: 146 us; the launch traced here: 145 us
  starting transfers between devices  58.4 us (40%)
  blocking collectives  54.8 us (38%)
  waiting for transfers between devices  17.5 us (12%)
  Pallas kernels  11.2 us (8%)
  local copies, waits for them, and re-layouts  1.88 us (1%)
    all_to_all x2, blocking collectives, exchange(): return lax.all_to_all(values, axis, split_axis=0, concat_axis=0, tiled=True)  54.8 us
    ppermute x9, starting transfers between devices, shift(): lax.ppermute(values, 'tp', [(source, (source + step) % count) for source...  30.8 us
    all_to_all x2, starting transfers between devices, exchange(): return lax.all_to_all(values, axis, split_axis=0, concat_axis=0, tiled=True)  27.6 us
    pallas_call x9, Pallas kernels, call(): pl.pallas_call(kernel, out_shape=outs, in_specs=[pl.BlockSpec(memory_spac...  11.2 us
    all_to_all x2, waiting for transfers between devices, exchange(): return lax.all_to_all(values, axis, split_axis=0, concat_axis=0, tiled=True)  9 us
    ppermute x9, waiting for transfers between devices, shift(): lax.ppermute(values, 'tp', [(source, (source + step) % count) for source...  8.53 us
  transfers between devices with their start and end apart: 11, of which 5 were waited for; matrix products, arithmetic and copies ran while one was open for 1% of the time, Pallas kernels for 4%

profile of v5, /device:TPU:1, one launch (start us, length us, event | category | flops | bytes accessed | tf_op | source)
XLA Modules:
  0.0 144.7 jit_solution(10288224731702438008)
XLA Ops:
  0.6 0.0 copy-start.1
  0.6 0.0 copy-start
  0.7 2.7 %shard_map.86 = (bf16[128,896]{1,0:T(8,128)(2,1)}, bf16[128,16]{1,0:T(8,128)(2,1)}, bf16[128,896]{1,0:T(8,128)(2,1)}, bf16[128,896]{1,0:T(8,128)(2,1)}, bf16[128...) custom-call(s32[8,16]{1,0:T(8,128)} %bitcast.23, bf16[8,16]{1,0:T(8,128)(2,1)} %bitcast.28, bf16[16,3584]{1,0:T(8,128)(2,1)} %refs_2_.1, ...), custom_call_target="tpu_custom_call" | custom-call | bytes 1048576 | tf_op jit(solution)/shard_map/pallas_call | solution.py:36
  3.4 17.5 %all-to-all-start = ((bf16[16,8,896]{2,1,0:T(8,128)(2,1)}), bf16[16,8,896]{2,1,0:T(8,128)(2,1)S(1)}, u32[]{:S(2)}, u32[]{:S(2)}) async-start(bf16[16,8,896]{2,1,0:T(8,128)(2,1)} %bitcast.26), calls=%async_computation | async-start | bytes 458752 | tf_op jit(solution)/shard_map/all_to_all | solution.py:272
  20.9 1.9 %collective-permute-start = (bf16[128,896]{1,0:T(8,128)(2,1)}, bf16[128,896]{1,0:T(8,128)(2,1)}, u32[]{:S(2)}, u32[]{:S(2)}) collective-permute-start(bf16[128,896]{1,0:T(8,128)(2,1)} %get-tuple-element.25), channel_id=1, source_target_pairs={{0,1},{1,2},{2,3},{3,0},{4,5},{5,6},{6,7},{7,4},{8,9},{9,10},{10,1... | collective-permute-start | bytes 688136 | tf_op jit(solution)/shard_map/ppermute | solution.py:276
  22.8 1.9 %collective-permute-start.1 = (bf16[128,896]{1,0:T(8,128)(2,1)}, bf16[128,896]{1,0:T(8,128)(2,1)}, u32[]{:S(2)}, u32[]{:S(2)}) collective-permute-start(bf16[128,896]{1,0:T(8,128)(2,1)} %get-tuple-element.26), channel_id=1, source_target_pairs={{0,2},{1,3},{2,0},{3,1},{4,6},{5,7},{6,4},{7,5},{8,10},{9,11},{10,... | collective-permute-start | bytes 688136 | tf_op jit(solution)/shard_map/ppermute | solution.py:276
  24.7 4.6 %collective-permute-start.2 = (bf16[128,896]{1,0:T(8,128)(2,1)}, bf16[128,896]{1,0:T(8,128)(2,1)}, u32[]{:S(2)}, u32[]{:S(2)}) collective-permute-start(bf16[128,896]{1,0:T(8,128)(2,1)} %get-tuple-element.27), channel_id=1, source_target_pairs={{0,3},{1,0},{2,1},{3,2},{4,7},{5,4},{6,5},{7,6},{8,11},{9,8},{10,9... | collective-permute-start | bytes 688136 | tf_op jit(solution)/shard_map/ppermute | solution.py:276
  29.3 0.9 copy.9
  30.2 1.8 %all-to-all-done = bf16[16,8,896]{2,1,0:T(8,128)(2,1)S(1)} async-done(((bf16[16,8,896]{2,1,0:T(8,128)(2,1)}), bf16[16,8,896]{2,1,0:T(8,128)(2,1)S(1)}, u32[]{:S(2)}, u32[]{:S(2)}) %all-to-all-start) | async-done | bytes 229408 | tf_op jit(solution)/shard_map/all_to_all | solution.py:272
  32.0 1.4 shard_map.87
  33.4 10.1 %all-to-all-start.1 = ((bf16[16,16,896]{2,1,0:T(8,128)(2,1)}), bf16[16,16,896]{2,1,0:T(8,128)(2,1)S(1)}, u32[]{:S(2)}, u32[]{:S(2)}) async-start(bf16[16,16,896]{2,1,0:T(8,128)(2,1)} %bitcast.5), calls=%async_computation.1 | async-start | bytes 917504 | tf_op jit(solution)/shard_map/all_to_all | solution.py:272
  43.6 0.0 copy-done.1
  43.6 0.0 copy-done
  43.6 1.3 shard_map.90
  44.9 2.6 %collective-permute-start.6 = (bf16[2304,128]{1,0:T(8,128)(2,1)}, bf16[2304,128]{1,0:T(8,128)(2,1)S(1)}, u32[]{:S(2)}, u32[]{:S(2)}) collective-permute-start(bf16[2304,128]{1,0:T(8,128)(2,1)} %get-tuple-element.29), channel_id=1, source_target_pairs={{0,1},{1,2},{2,3},{3,0},{4,5},{5,6},{6,7},{7,4},{8,9},{9,10},{10,1... | collective-permute-start | bytes 1769480 | tf_op jit(solution)/shard_map/ppermute | solution.py:276
  47.6 4.4 %collective-permute-start.7 = (bf16[2304,128]{1,0:T(8,128)(2,1)}, bf16[2304,128]{1,0:T(8,128)(2,1)S(1)}, u32[]{:S(2)}, u32[]{:S(2)}) collective-permute-start(bf16[2304,128]{1,0:T(8,128)(2,1)} %get-tuple-element.30), channel_id=1, source_target_pairs={{0,2},{1,3},{2,0},{3,1},{4,6},{5,7},{6,4},{7,5},{8,10},{9,11},{10,... | collective-permute-start | bytes 1769480 | tf_op jit(solution)/shard_map/ppermute | solution.py:276
  51.9 0.0 collective-permute-done.refs_1_
  51.9 3.1 %collective-permute-start.8 = (bf16[2304,128]{1,0:T(8,128)(2,1)}, bf16[2304,128]{1,0:T(8,128)(2,1)}, u32[]{:S(2)}, u32[]{:S(2)}) collective-permute-start(bf16[2304,128]{1,0:T(8,128)(2,1)} %get-tuple-element.31), channel_id=1, source_target_pairs={{0,3},{1,0},{2,1},{3,2},{4,7},{5,4},{6,5},{7,6},{8,11},{9,8},{10,9... | collective-permute-start | bytes 1769480 | tf_op jit(solution)/shard_map/ppermute | solution.py:276
  55.0 0.0 collective-permute-done.1.refs_2_
  55.0 0.0 collective-permute-done.2.refs_3_
  55.0 0.0 copy-start.4
  55.0 0.9 copy-done.4
  56.0 1.2 shard_map.88.down_ref
  57.2 7.2 %all-to-all-done.1 = bf16[16,16,896]{2,1,0:T(8,128)(2,1)S(1)} async-done(((bf16[16,16,896]{2,1,0:T(8,128)(2,1)}), bf16[16,16,896]{2,1,0:T(8,128)(2,1)S(1)}, u32[]{:S(2)}, u32[]{:S(2)}) %all-to-all-start.1) | async-done | bytes 458784 | tf_op jit(solution)/shard_map/all_to_all | solution.py:272
  64.4 0.5 shard_map.89.refs_0_
  64.9 7.4 %collective-permute-start.5 = (bf16[256,512]{1,0:T(8,128)(2,1)S(1)}, bf16[256,512]{1,0:T(8,128)(2,1)S(1)}, u32[]{:S(2)}, u32[]{:S(2)}) collective-permute-start(bf16[256,512]{1,0:T(8,128)(2,1)S(1)} %shard_map.89.refs_0_), channel_id=1, source_target_pairs={{0,3},{1,0},{2,1},{3,2},{4,7},{5,4},{6,5},{7,6},{8,11},{9,8},{10,9... | collective-permute-start | bytes 786440 | tf_op jit(solution)/shard_map/ppermute | solution.py:276
  72.3 2.2 %collective-permute-start.4 = (bf16[256,512]{1,0:T(8,128)(2,1)S(1)}, bf16[256,512]{1,0:T(8,128)(2,1)S(1)}, u32[]{:S(2)}, u32[]{:S(2)}) collective-permute-start(bf16[256,512]{1,0:T(8,128)(2,1)S(1)} %shard_map.89.refs_0_), channel_id=1, source_target_pairs={{0,2},{1,3},{2,0},{3,1},{4,6},{5,7},{6,4},{7,5},{8,10},{9,11},{10,... | collective-permute-start | bytes 786440 | tf_op jit(solution)/shard_map/ppermute | solution.py:276
  74.5 0.0 collective-permute-done.6.refs_1_
  74.5 2.8 %collective-permute-start.3 = (bf16[256,512]{1,0:T(8,128)(2,1)S(1)}, bf16[256,512]{1,0:T(8,128)(2,1)S(1)}, u32[]{:S(2)}, u32[]{:S(2)}) collective-permute-start(bf16[256,512]{1,0:T(8,128)(2,1)S(1)} %shard_map.89.refs_0_), channel_id=1, source_target_pairs={{0,1},{1,2},{2,3},{3,0},{4,5},{5,6},{6,7},{7,4},{8,9},{9,10},{10,1... | collective-permute-start | bytes 786440 | tf_op jit(solution)/shard_map/ppermute | solution.py:276
  77.3 0.0 collective-permute-done.7.refs_2_
  77.3 0.4 collective-permute-done.8.refs_3_
  77.7 1.7 %shard_map.91 = (bf16[896,1024]{1,0:T(8,128)(2,1)S(1)}, f32[256,512]{1,0:T(8,128)S(1)}, f32[256,512]{1,0:T(8,128)S(1)}, f32[256,512]{1,0:T(8,128)S(1)}) custom-call(bf16[2304,128]{1,0:T(8,128)(2,1)S(1)} %get-tuple-element.28.refs_0_, bf16[2304,128]{1,0:T(8,128)(2,1)S(1)} %collective-permute-done.6.refs_1_, ...), custom_call_target="tpu_custom_call" | custom-call | bytes 8388608 | tf_op jit(solution)/shard_map/pallas_call | solution.py:36
  79.4 5.2 %collective-permute-done.5.refs_3_ = bf16[256,512]{1,0:T(8,128)(2,1)S(1)} collective-permute-done((bf16[256,512]{1,0:T(8,128)(2,1)S(1)}, bf16[256,512]{1,0:T(8,128)(2,1)S(1)}, u32[]{:S(2)}, u32[]{:S(2)}) %collective-permute-start.5) | collective-permute-done | bytes 262176 | tf_op jit(solution)/shard_map/ppermute | solution.py:276
  84.6 0.0 collective-permute-done.4.refs_2_
  84.6 2.9 %collective-permute-done.3.refs_1_ = bf16[256,512]{1,0:T(8,128)(2,1)S(1)} collective-permute-done((bf16[256,512]{1,0:T(8,128)(2,1)S(1)}, bf16[256,512]{1,0:T(8,128)(2,1)S(1)}, u32[]{:S(2)}, u32[]{:S(2)}) %collective-permute-start.3) | collective-permute-done | bytes 262176 | tf_op jit(solution)/shard_map/ppermute | solution.py:276
  87.5 0.8 shard_map.92
  88.3 0.0 copy-start.2
  88.3 0.0 copy-start.3
  88.3 33.3 %all_to_all.20.refs_1_ = bf16[16,120,128]{2,1,0:T(8,128)(2,1)S(1)} all-to-all(bf16[16,120,128]{2,1,0:T(8,128)(2,1)S(1)} %shard_map.92), channel_id=1, replica_groups=mesh['wide'=16,'narrow'=16,'tp'=4] {'narrow'}, dimensions={0} | all-to-all | bytes 983040 | tf_op jit(solution)/shard_map/all_to_all | solution.py:272
  121.6 0.4 shard_map.93
  121.9 21.5 %all_to_all.21 = bf16[16,8,896]{2,1,0:T(8,128)(2,1)S(1)} all-to-all(bf16[16,8,896]{2,1,0:T(8,128)(2,1)S(1)} %bitcast.19), channel_id=1, replica_groups=mesh['wide'=16,'narrow'=16,'tp'=4] {'wide'}, dimensions={0} | all-to-all | bytes 458752 | tf_op jit(solution)/shard_map/all_to_all | solution.py:272
  143.5 0.0 copy-done.2
  143.5 0.0 copy-done.3
  143.5 1.2 shard_map.94
Async XLA Ops:
  0.6 42.9 %copy-start.1 = (bf16[1,1,3584,128]{3,2,1,0:T(8,128)(2,1)S(1)}, bf16[1,1,3584,128]{3,2,1,0:T(8,128)(2,1)}, u32[]{:S(2)}) copy-start(bf16[1,1,3584,128]{3,2,1,0:T(8,128)(2,1)} %param.12) | copy-start | bytes 2752516
  0.6 42.9 %copy-start = (bf16[1,1,3584,128]{3,2,1,0:T(8,128)(2,1)S(1)}, bf16[1,1,3584,128]{3,2,1,0:T(8,128)(2,1)}, u32[]{:S(2)}) copy-start(bf16[1,1,3584,128]{3,2,1,0:T(8,128)(2,1)} %param.11) | copy-start | bytes 2752516
  3.4 28.6 %all-to-all-start = ((bf16[16,8,896]{2,1,0:T(8,128)(2,1)}), bf16[16,8,896]{2,1,0:T(8,128)(2,1)S(1)}, u32[]{:S(2)}, u32[]{:S(2)}) async-start(bf16[16,8,896]{2,1,0:T(8,128)(2,1)} %bitcast.26), calls=%async_computation | async-start | bytes 458752 | tf_op jit(solution)/shard_map/all_to_all | solution.py:272
  20.9 31.1 %collective-permute-start = (bf16[128,896]{1,0:T(8,128)(2,1)}, bf16[128,896]{1,0:T(8,128)(2,1)}, u32[]{:S(2)}, u32[]{:S(2)}) collective-permute-start(bf16[128,896]{1,0:T(8,128)(2,1)} %get-tuple-element.25), channel_id=1, source_target_pairs={{0,1},{1,2},{2,3},{3,0},{4,5},{5,6},{6,7},{7,4},{8,9},{9,10},{10,1... | collective-permute-start | bytes 688136 | tf_op jit(solution)/shard_map/ppermute | solution.py:276
  22.8 32.2 %collective-permute-start.1 = (bf16[128,896]{1,0:T(8,128)(2,1)}, bf16[128,896]{1,0:T(8,128)(2,1)}, u32[]{:S(2)}, u32[]{:S(2)}) collective-permute-start(bf16[128,896]{1,0:T(8,128)(2,1)} %get-tuple-element.26), channel_id=1, source_target_pairs={{0,2},{1,3},{2,0},{3,1},{4,6},{5,7},{6,4},{7,5},{8,10},{9,11},{10,... | collective-permute-start | bytes 688136 | tf_op jit(solution)/shard_map/ppermute | solution.py:276
  24.7 30.3 %collective-permute-start.2 = (bf16[128,896]{1,0:T(8,128)(2,1)}, bf16[128,896]{1,0:T(8,128)(2,1)}, u32[]{:S(2)}, u32[]{:S(2)}) collective-permute-start(bf16[128,896]{1,0:T(8,128)(2,1)} %get-tuple-element.27), channel_id=1, source_target_pairs={{0,3},{1,0},{2,1},{3,2},{4,7},{5,4},{6,5},{7,6},{8,11},{9,8},{10,9... | collective-permute-start | bytes 688136 | tf_op jit(solution)/shard_map/ppermute | solution.py:276
  33.4 30.9 %all-to-all-start.1 = ((bf16[16,16,896]{2,1,0:T(8,128)(2,1)}), bf16[16,16,896]{2,1,0:T(8,128)(2,1)S(1)}, u32[]{:S(2)}, u32[]{:S(2)}) async-start(bf16[16,16,896]{2,1,0:T(8,128)(2,1)} %bitcast.5), calls=%async_computation.1 | async-start | bytes 917504 | tf_op jit(solution)/shard_map/all_to_all | solution.py:272
  44.9 29.6 %collective-permute-start.6 = (bf16[2304,128]{1,0:T(8,128)(2,1)}, bf16[2304,128]{1,0:T(8,128)(2,1)S(1)}, u32[]{:S(2)}, u32[]{:S(2)}) collective-permute-start(bf16[2304,128]{1,0:T(8,128)(2,1)} %get-tuple-element.29), channel_id=1, source_target_pairs={{0,1},{1,2},{2,3},{3,0},{4,5},{5,6},{6,7},{7,4},{8,9},{9,10},{10,1... | collective-permute-start | bytes 1769480 | tf_op jit(solution)/shard_map/ppermute | solution.py:276
  47.6 29.7 %collective-permute-start.7 = (bf16[2304,128]{1,0:T(8,128)(2,1)}, bf16[2304,128]{1,0:T(8,128)(2,1)S(1)}, u32[]{:S(2)}, u32[]{:S(2)}) collective-permute-start(bf16[2304,128]{1,0:T(8,128)(2,1)} %get-tuple-element.30), channel_id=1, source_target_pairs={{0,2},{1,3},{2,0},{3,1},{4,6},{5,7},{6,4},{7,5},{8,10},{9,11},{10,... | collective-permute-start | bytes 1769480 | tf_op jit(solution)/shard_map/ppermute | solution.py:276
  51.9 25.8 %collective-permute-start.8 = (bf16[2304,128]{1,0:T(8,128)(2,1)}, bf16[2304,128]{1,0:T(8,128)(2,1)}, u32[]{:S(2)}, u32[]{:S(2)}) collective-permute-start(bf16[2304,128]{1,0:T(8,128)(2,1)} %get-tuple-element.31), channel_id=1, source_target_pairs={{0,3},{1,0},{2,1},{3,2},{4,7},{5,4},{6,5},{7,6},{8,11},{9,8},{10,9... | collective-permute-start | bytes 1769480 | tf_op jit(solution)/shard_map/ppermute | solution.py:276
  55.0 0.9 copy-start.4
  64.9 19.7 %collective-permute-start.5 = (bf16[256,512]{1,0:T(8,128)(2,1)S(1)}, bf16[256,512]{1,0:T(8,128)(2,1)S(1)}, u32[]{:S(2)}, u32[]{:S(2)}) collective-permute-start(bf16[256,512]{1,0:T(8,128)(2,1)S(1)} %shard_map.89.refs_0_), channel_id=1, source_target_pairs={{0,3},{1,0},{2,1},{3,2},{4,7},{5,4},{6,5},{7,6},{8,11},{9,8},{10,9... | collective-permute-start | bytes 786440 | tf_op jit(solution)/shard_map/ppermute | solution.py:276
  72.3 12.3 %collective-permute-start.4 = (bf16[256,512]{1,0:T(8,128)(2,1)S(1)}, bf16[256,512]{1,0:T(8,128)(2,1)S(1)}, u32[]{:S(2)}, u32[]{:S(2)}) collective-permute-start(bf16[256,512]{1,0:T(8,128)(2,1)S(1)} %shard_map.89.refs_0_), channel_id=1, source_target_pairs={{0,2},{1,3},{2,0},{3,1},{4,6},{5,7},{6,4},{7,5},{8,10},{9,11},{10,... | collective-permute-start | bytes 786440 | tf_op jit(solution)/shard_map/ppermute | solution.py:276
  74.5 13.0 %collective-permute-start.3 = (bf16[256,512]{1,0:T(8,128)(2,1)S(1)}, bf16[256,512]{1,0:T(8,128)(2,1)S(1)}, u32[]{:S(2)}, u32[]{:S(2)}) collective-permute-start(bf16[256,512]{1,0:T(8,128)(2,1)S(1)} %shard_map.89.refs_0_), channel_id=1, source_target_pairs={{0,1},{1,2},{2,3},{3,0},{4,5},{5,6},{6,7},{7,4},{8,9},{9,10},{10,1... | collective-permute-start | bytes 786440 | tf_op jit(solution)/shard_map/ppermute | solution.py:276
  88.3 55.2 %copy-start.2 = (bf16[128,16]{1,0:T(8,128)(2,1)S(1)}, bf16[128,16]{1,0:T(8,128)(2,1)}, u32[]{:S(2)}) copy-start(bf16[128,16]{1,0:T(8,128)(2,1)} %get-tuple-element.20.refs_1_) | copy-start | bytes 12292
  88.3 55.2 %copy-start.3 = (s32[16,8]{0,1:T(8,128)S(1)}, s32[16,8]{0,1:T(8,128)}, u32[]{:S(2)}) copy-start(s32[16,8]{0,1:T(8,128)} %param.8) | copy-start | bytes 1540

commit v6 on v5

--- a/solution.py
+++ b/solution.py
@@ -50,7 +50,7 @@
     return jax.ShapeDtypeStruct(dims, dtype)
 
 
-def pack_rest_kernel(gate_ref, up_ref, preact_ref, after_ref, *out_refs):
+def pack_rest_kernel(gate_ref, up_ref, after_ref, *out_refs):
     count = len(out_refs)
     width = gate_ref.shape[0] // count
     me = lax.axis_index("tp")
@@ -59,14 +59,18 @@
         rows = pl.ds(pl.multiple_of(to * width, TILE), width)
         out_ref[0:width, :] = gate_ref[rows, :]
         out_ref[width : 2 * width, :] = up_ref[rows, :]
-        out_ref[2 * width :, :] = preact_ref[...]
-
-
-def join_kernel(*refs):
-    out_ref = refs[-1]
-    hidden = refs[0].shape[0]
-    for at, block_ref in enumerate(refs[:-1]):
-        out_ref[at * hidden : (at + 1) * hidden, :] = block_ref[...]
+
+
+def join_kernel(down_ref, *refs):
+    block_refs, out_ref = refs[:-1], refs[-1]
+    hidden, columns = down_ref.shape[0], out_ref.shape[1]
+    own = lax.axis_index("tp") * columns
+    out_ref[0:hidden, :] = down_ref[:, pl.ds(pl.multiple_of(own, TILE), columns)]
+    for at, block_ref in enumerate(block_refs, 1):
+        for tile in range(columns // TILE):
+            out_ref[at * hidden : (at + 1) * hidden, tile * TILE : (tile + 1) * TILE] = (
+                block_ref[tile * hidden : (tile + 1) * hidden, :]
+            )
 
 
 def spread(group_cap, rows):
@@ -86,10 +90,12 @@
     return c // width == r % BLOCK
 
 
-def first_kernel(group_cap, width, count, ids_hbm, gates_hbm, rows_hbm, down_hbm, *refs):
+def first_kernel(
+    group_cap, width, count, ids_hbm, gates_hbm, rows_hbm, down_hbm, preacts_hbm, *refs
+):
     send_ref, place_ref = refs[:2]
-    down_refs = refs[2 : 2 + count]
-    ids_ref, gates_ref, rows_ref, sems = refs[2 + count :]
+    block_refs = refs[2 : 1 + count]
+    ids_ref, gates_ref, rows_ref, sems = refs[1 + count :]
     columns = send_ref.shape[1]
     me = lax.axis_index("tp")
 
@@ -101,11 +107,18 @@
         pltpu.make_async_copy(gates_hbm, gates_ref, sems.at[1]),
         pltpu.make_async_copy(rows_hbm.at[:, columns_of(me)], rows_ref, sems.at[2]),
     ]
+    packs = []
+    hidden = down_hbm.shape[0]
+    for step, block_ref in enumerate(block_refs, 1):
+        first = lax.rem(me + step, count) * columns
+        for tile in range(columns // TILE):
+            lanes = pl.ds(pl.multiple_of(first + tile * TILE, TILE), TILE)
+            packs.append((down_hbm.at[:, lanes], block_ref.at[pl.ds(tile * hidden, hidden)]))
+        tail = pl.ds(columns // TILE * hidden, preacts_hbm.shape[0])
+        packs.append((preacts_hbm, block_ref.at[tail]))
     packs = [
-        pltpu.make_async_copy(
-            down_hbm.at[:, columns_of(lax.rem(me + step, count))], down_ref, sems.at[3 + step]
-        )
-        for step, down_ref in enumerate(down_refs)
+        pltpu.make_async_copy(source, target, sems.at[3 + at])
+        for at, (source, target) in enumerate(packs)
     ]
     for copy in loads + packs:
         copy.start()
@@ -176,22 +189,27 @@
     return terms[0]
 
 
-def prepare_kernel(*refs):
-    blocks, (weight_ref, swish_ref, slope_ref, hidden_ref) = refs[:-4], refs[-4:]
+def prepare_kernel(count, preacts_ref, *refs):
+    blocks, early = refs[:count], refs[count : 2 * count - 1]
+    weight_ref, swish_ref, slope_ref, hidden_ref = refs[2 * count - 1 :]
     columns = weight_ref.shape[0]
     slots = swish_ref.shape[0]
     for at, block_ref in enumerate(blocks):
         for part in range(2):
             first = (2 * at + part) * TILE
             weight_ref[:, first : first + TILE] = block_ref[part * columns : (part + 1) * columns, :]
-        gate_pre = block_ref[2 * columns : 2 * columns + slots, :].astype(jnp.float32)
-        up_pre = block_ref[2 * columns + slots :, :].astype(jnp.float32)
-        sigmoid_value = jax.nn.sigmoid(gate_pre)
-        swish_value = gate_pre * sigmoid_value
-        lanes = slice(at * TILE, (at + 1) * TILE)
-        swish_ref[:, lanes] = swish_value
-        slope_ref[:, lanes] = up_pre * (sigmoid_value * (1.0 + gate_pre * (1.0 - sigmoid_value)))
-        hidden_ref[:, lanes] = swish_value * up_pre
+    tail = early[0].shape[0] - 2 * slots
+    raw = jnp.concatenate(
+        [preacts_ref[...]] + [block_ref[tail:, :] for block_ref in early], axis=1
+    )
+    slot, row = iota((slots, 2 * slots), 0), iota((slots, 2 * slots), 1)
+    gate_pre = nn(bits(row == 2 * slot), raw)
+    up_pre = nn(bits(row == 2 * slot + 1), raw)
+    sigmoid_value = jax.nn.sigmoid(gate_pre)
+    swish_value = gate_pre * sigmoid_value
+    swish_ref[...] = swish_value
+    slope_ref[...] = up_pre * (sigmoid_value * (1.0 + gate_pre * (1.0 - sigmoid_value)))
+    hidden_ref[...] = swish_value * up_pre
 
 
 def expert_kernel(count, lane_cap, *refs):
@@ -300,28 +318,32 @@
     lanes = group_width * lane_cap
     ids = expert_ids.T
 
-    send, place, *down_packed = call(
+    preacts = stored_preacts[0, 0].reshape(2 * slot_count, hidden_width)
+    tiles = columns // TILE
+    early_rows = tiles * hidden_width + 2 * slot_count
+    others = split_count - 1
+    send, place, *early = call(
         lambda *refs: first_kernel(group_cap, group_width, split_count, *refs),
         [shape(rows, columns), shape(rows, token_count)]
-        + [shape(hidden_width, columns)] * split_count,
-        (ids, gate_values.T, d_out, w_down[0, 0]),
-        spaces=[pltpu.HBM] * 4,
-        out_spaces=[pltpu.VMEM] * (2 + split_count),
+        + [shape(early_rows, hidden_width)] * others,
+        (ids, gate_values.T, d_out, w_down[0, 0], preacts),
+        spaces=[pltpu.HBM] * 5,
+        out_spaces=[pltpu.VMEM] * (2 + others),
         vmem=60,
         scratch=[
             pltpu.VMEM(ids.shape, ids.dtype),
             pltpu.VMEM(ids.shape, gate_values.dtype),
             pltpu.VMEM((token_count, columns), d_out.dtype),
-            pltpu.SemaphoreType.DMA((3 + split_count,)),
+            pltpu.SemaphoreType.DMA((3 + others * (tiles + 1),)),
         ],
     )
-    downs = shift_all(down_packed)
+    early = shift_all([None] + early)[1:]
     down_cols = call(
         join_kernel,
         shape(split_count * hidden_width, columns),
-        downs,
+        (w_down[0, 0], *early),
         size=1 << 20,
-        flops=20 * 10**9,
+        flops=18 * 10**9,
     )
 
     got = exchange(send.reshape(wide_count, BLOCK, columns), "wide").reshape(rows, columns)
@@ -332,15 +354,14 @@
     )
     rest_packed = call(
         pack_rest_kernel,
-        [shape(2 * columns + 2 * slot_count, hidden_width)] * split_count,
+        [shape(2 * columns, hidden_width)] * split_count,
         (
             w_gate[0, 0],
             w_up[0, 0],
-            stored_preacts[0, 0].transpose(1, 0, 2).reshape(2 * slot_count, hidden_width),
             gated,
         ),
         size=4 << 20,
-        spaces=[pltpu.VMEM] * 3 + [pl.ANY],
+        spaces=[pltpu.VMEM] * 2 + [pl.ANY],
     )
     blocks = shift_all(rest_packed)
     slot_rows = exchange(forward.reshape(lane_count, lane_cap, columns), "narrow").reshape(
@@ -354,10 +375,10 @@
     parts = shift_all([partial] * split_count)
     hidden_all = split_count * hidden_width
     prepared = call(
-        prepare_kernel,
+        lambda *refs: prepare_kernel(split_count, *refs),
         [shape(columns, 2 * hidden_all)]
         + [shape(slot_count, hidden_all, dtype=jnp.float32)] * 3,
-        blocks,
+        (preacts, *blocks, *early),
         size=8 << 20,
     )
     block_rows = columns // TILE * lane_cap + BLOCK

time: 146 us -> 145 us (level)
  waiting for transfers between devices: 17.5 us -> 13.6 us
  starting transfers between devices: 58.4 us -> 60.5 us
    ppermute x9, waiting for transfers between devices: 8.53 us -> 4.26 us  [shift(): lax.ppermute(values, 'tp', [(source, (source + step) % count) for source...]
    ppermute x9, starting transfers between devices: 30.8 us -> 33.2 us  [shift(): lax.ppermute(values, 'tp', [(source, (source + step) % count) for source...]
  transfers between devices with their start and end apart: 11 -> 11, of which waited for: 5 -> 4; matrix products, arithmetic and copies ran while one was open for 1% -> 0% of each run, Pallas kernels for 4% -> 4%
where the time goes in v6:
time: 145 us; the launch traced here: 143 us
  starting transfers between devices  60.5 us (42%)
  blocking collectives  54.4 us (38%)
  waiting for transfers between devices  13.6 us (9%)
  Pallas kernels  11.6 us (8%)
  local copies, waits for them, and re-layouts  1.59 us (1%)
    all_to_all x2, blocking collectives, exchange(): return lax.all_to_all(values, axis, split_axis=0, concat_axis=0, tiled=True)  54.4 us
    ppermute x9, starting transfers between devices, shift(): lax.ppermute(values, 'tp', [(source, (source + step) % count) for source...  33.2 us
    all_to_all x2, starting transfers between devices, exchange(): return lax.all_to_all(values, axis, split_axis=0, concat_axis=0, tiled=True)  27.2 us
    pallas_call x9, Pallas kernels, call(): pl.pallas_call(kernel, out_shape=outs, in_specs=[pl.BlockSpec(memory_spac...  11.6 us
    all_to_all x2, waiting for transfers between devices, exchange(): return lax.all_to_all(values, axis, split_axis=0, concat_axis=0, tiled=True)  9.37 us
    ppermute x9, waiting for transfers between devices, shift(): lax.ppermute(values, 'tp', [(source, (source + step) % count) for source...  4.26 us
  transfers between devices with their start and end apart: 11, of which 4 were waited for; matrix products, arithmetic and copies ran while one was open for 0% of the time, Pallas kernels for 4%

profile of v6, /device:TPU:1, one launch (start us, length us, event | category | flops | bytes accessed | tf_op | source)
XLA Modules:
  0.0 142.6 jit_solution(11549677781709261342)
XLA Ops:
  0.6 0.0 copy-start
  0.6 0.0 copy-start.1
  0.7 3.0 %shard_map.86 = (bf16[128,896]{1,0:T(8,128)(2,1)}, bf16[128,16]{1,0:T(8,128)(2,1)}, bf16[1408,128]{1,0:T(8,128)(2,1)}, bf16[1408,128]{1,0:T(8,128)(2,1)}, bf16[1408,128]{1,0:T(8,128)(2,1)}) custom-call(s32[8,16]{1,0:T(8,128)} %bitcast.24, bf16[8,16]{1,0:T(8,128)(2,1)} %bitcast.27, bf16[16,3584]{1,0:T(8,128)(2,1)} %refs_2_.1, bf16[128,3584]{1,0:T(8,128)(2,1)} %bitcast.17, ...), custom_call_target="tpu_custom_call" | custom-call | bytes 1048576 | tf_op jit(solution)/shard_map/pallas_call | solution.py:36
  3.6 0.0 copy-start.2
  3.6 17.6 %all-to-all-start = ((bf16[16,8,896]{2,1,0:T(8,128)(2,1)}), bf16[16,8,896]{2,1,0:T(8,128)(2,1)S(1)}, u32[]{:S(2)}, u32[]{:S(2)}) async-start(bf16[16,8,896]{2,1,0:T(8,128)(2,1)} %bitcast.26), calls=%async_computation | async-start | bytes 458752 | tf_op jit(solution)/shard_map/all_to_all | solution.py:290
  21.3 1.9 %collective-permute-start = (bf16[1408,128]{1,0:T(8,128)(2,1)}, bf16[1408,128]{1,0:T(8,128)(2,1)}, u32[]{:S(2)}, u32[]{:S(2)}) collective-permute-start(bf16[1408,128]{1,0:T(8,128)(2,1)} %get-tuple-element.23), channel_id=1, source_target_pairs={{0,1},{1,2},{2,3},{3,0},{4,5},{5,6},{6,7},{7,4},{8,9},{9,10},{10,1... | collective-permute-start | bytes 1081352 | tf_op jit(solution)/shard_map/ppermute | solution.py:294
  23.2 1.9 %collective-permute-start.1 = (bf16[1408,128]{1,0:T(8,128)(2,1)}, bf16[1408,128]{1,0:T(8,128)(2,1)}, u32[]{:S(2)}, u32[]{:S(2)}) collective-permute-start(bf16[1408,128]{1,0:T(8,128)(2,1)} %get-tuple-element.24), channel_id=1, source_target_pairs={{0,2},{1,3},{2,0},{3,1},{4,6},{5,7},{6,4},{7,5},{8,10},{9,11},{10,... | collective-permute-start | bytes 1081352 | tf_op jit(solution)/shard_map/ppermute | solution.py:294
  25.1 4.6 %collective-permute-start.2 = (bf16[1408,128]{1,0:T(8,128)(2,1)}, bf16[1408,128]{1,0:T(8,128)(2,1)}, u32[]{:S(2)}, u32[]{:S(2)}) collective-permute-start(bf16[1408,128]{1,0:T(8,128)(2,1)} %get-tuple-element.25), channel_id=1, source_target_pairs={{0,3},{1,0},{2,1},{3,2},{4,7},{5,4},{6,5},{7,6},{8,11},{9,8},{10,9... | collective-permute-start | bytes 1081352 | tf_op jit(solution)/shard_map/ppermute | solution.py:294
  29.7 2.7 %all-to-all-done = bf16[16,8,896]{2,1,0:T(8,128)(2,1)S(1)} async-done(((bf16[16,8,896]{2,1,0:T(8,128)(2,1)}), bf16[16,8,896]{2,1,0:T(8,128)(2,1)S(1)}, u32[]{:S(2)}, u32[]{:S(2)}) %all-to-all-start) | async-done | bytes 229408 | tf_op jit(solution)/shard_map/all_to_all | solution.py:290
  32.4 0.6 shard_map.87
  33.1 0.0 copy-start.4
  33.1 0.8 copy-done.4
  33.8 9.6 %all-to-all-start.1 = ((bf16[16,16,896]{2,1,0:T(8,128)(2,1)}), bf16[16,16,896]{2,1,0:T(8,128)(2,1)S(1)}, u32[]{:S(2)}, u32[]{:S(2)}) async-start(bf16[16,16,896]{2,1,0:T(8,128)(2,1)} %bitcast.23), calls=%async_computation.1 | async-start | bytes 917504 | tf_op jit(solution)/shard_map/all_to_all | solution.py:290
  43.5 0.0 copy-done
  43.5 0.0 copy-done.1
  43.5 1.2 shard_map.90
  44.7 0.8 copy-done.5
  45.5 3.1 %collective-permute-start.6 = (bf16[1792,128]{1,0:T(8,128)(2,1)}, bf16[1792,128]{1,0:T(8,128)(2,1)}, u32[]{:S(2)}, u32[]{:S(2)}) collective-permute-start(bf16[1792,128]{1,0:T(8,128)(2,1)} %get-tuple-element.27), channel_id=1, source_target_pairs={{0,1},{1,2},{2,3},{3,0},{4,5},{5,6},{6,7},{7,4},{8,9},{9,10},{10,1... | collective-permute-start | bytes 1376264 | tf_op jit(solution)/shard_map/ppermute | solution.py:294
  48.6 4.4 %collective-permute-start.7 = (bf16[1792,128]{1,0:T(8,128)(2,1)}, bf16[1792,128]{1,0:T(8,128)(2,1)}, u32[]{:S(2)}, u32[]{:S(2)}) collective-permute-start(bf16[1792,128]{1,0:T(8,128)(2,1)} %get-tuple-element.28), channel_id=1, source_target_pairs={{0,2},{1,3},{2,0},{3,1},{4,6},{5,7},{6,4},{7,5},{8,10},{9,11},{10,... | collective-permute-start | bytes 1376264 | tf_op jit(solution)/shard_map/ppermute | solution.py:294
  53.0 0.0 collective-permute-done.refs_0_.refs_5_
  53.0 0.0 copy-start.3
  53.0 3.2 %collective-permute-start.8 = (bf16[1792,128]{1,0:T(8,128)(2,1)}, bf16[1792,128]{1,0:T(8,128)(2,1)}, u32[]{:S(2)}, u32[]{:S(2)}) collective-permute-start(bf16[1792,128]{1,0:T(8,128)(2,1)} %get-tuple-element.29), channel_id=1, source_target_pairs={{0,3},{1,0},{2,1},{3,2},{4,7},{5,4},{6,5},{7,6},{8,11},{9,8},{10,9... | collective-permute-start | bytes 1376264 | tf_op jit(solution)/shard_map/ppermute | solution.py:294
  56.2 0.0 collective-permute-done.1.refs_1_.refs_6_
  56.2 0.0 collective-permute-done.2.refs_2_.refs_7_
  56.2 0.0 copy-done.2
  56.2 1.3 shard_map.88.down_ref
  57.5 0.0 copy-start.6
  57.6 6.6 %all-to-all-done.1 = bf16[16,16,896]{2,1,0:T(8,128)(2,1)S(1)} async-done(((bf16[16,16,896]{2,1,0:T(8,128)(2,1)}), bf16[16,16,896]{2,1,0:T(8,128)(2,1)S(1)}, u32[]{:S(2)}, u32[]{:S(2)}) %all-to-all-start.1) | async-done | bytes 458784 | tf_op jit(solution)/shard_map/all_to_all | solution.py:290
  64.2 0.5 shard_map.89.refs_0_
  64.7 6.7 %collective-permute-start.3 = (bf16[256,512]{1,0:T(8,128)(2,1)S(1)}, bf16[256,512]{1,0:T(8,128)(2,1)S(1)}, u32[]{:S(2)}, u32[]{:S(2)}) collective-permute-start(bf16[256,512]{1,0:T(8,128)(2,1)S(1)} %shard_map.89.refs_0_), channel_id=1, source_target_pairs={{0,1},{1,2},{2,3},{3,0},{4,5},{5,6},{6,7},{7,4},{8,9},{9,10},{10,1... | collective-permute-start | bytes 786440 | tf_op jit(solution)/shard_map/ppermute | solution.py:294
  71.4 4.4 %collective-permute-start.4 = (bf16[256,512]{1,0:T(8,128)(2,1)S(1)}, bf16[256,512]{1,0:T(8,128)(2,1)S(1)}, u32[]{:S(2)}, u32[]{:S(2)}) collective-permute-start(bf16[256,512]{1,0:T(8,128)(2,1)S(1)} %shard_map.89.refs_0_), channel_id=1, source_target_pairs={{0,2},{1,3},{2,0},{3,1},{4,6},{5,7},{6,4},{7,5},{8,10},{9,11},{10,... | collective-permute-start | bytes 786440 | tf_op jit(solution)/shard_map/ppermute | solution.py:294
  75.8 0.0 collective-permute-done.6.refs_2_
  75.8 3.1 %collective-permute-start.5 = (bf16[256,512]{1,0:T(8,128)(2,1)S(1)}, bf16[256,512]{1,0:T(8,128)(2,1)S(1)}, u32[]{:S(2)}, u32[]{:S(2)}) collective-permute-start(bf16[256,512]{1,0:T(8,128)(2,1)S(1)} %shard_map.89.refs_0_), channel_id=1, source_target_pairs={{0,3},{1,0},{2,1},{3,2},{4,7},{5,4},{6,5},{7,6},{8,11},{9,8},{10,9... | collective-permute-start | bytes 786440 | tf_op jit(solution)/shard_map/ppermute | solution.py:294
  78.9 0.0 collective-permute-done.7.refs_3_
  78.9 0.0 collective-permute-done.8.refs_4_
  78.9 0.0 copy-done.3
  78.9 0.0 copy-done.6
  78.9 2.6 %shard_map.91 = (bf16[896,1024]{1,0:T(8,128)(2,1)S(1)}, f32[256,512]{1,0:T(8,128)S(1)}, f32[256,512]{1,0:T(8,128)S(1)}, f32[256,512]{1,0:T(8,128)S(1)}) custom-call(bf16[512,128]{1,0:T(8,128)(2,1)S(1)} %bitcast.22, bf16[1792,128]{1,0:T(8,128)(2,1)S(1)} %copy-done.6, bf16[1792,128]{1,0:T(8,128)(2,1)} %collective-permute-done.6.refs_2_, ...), custom_call_target="tpu_custom_call" | custom-call | bytes 8388608 | tf_op jit(solution)/shard_map/pallas_call | solution.py:36
  81.6 0.0 collective-permute-done.3.refs_1_
  81.6 1.5 %collective-permute-done.4.refs_2_ = bf16[256,512]{1,0:T(8,128)(2,1)S(1)} collective-permute-done((bf16[256,512]{1,0:T(8,128)(2,1)S(1)}, bf16[256,512]{1,0:T(8,128)(2,1)S(1)}, u32[]{:S(2)}, u32[]{:S(2)}) %collective-permute-start.4) | collective-permute-done | bytes 262176 | tf_op jit(solution)/shard_map/ppermute | solution.py:294
  83.1 2.8 %collective-permute-done.5.refs_3_ = bf16[256,512]{1,0:T(8,128)(2,1)S(1)} collective-permute-done((bf16[256,512]{1,0:T(8,128)(2,1)S(1)}, bf16[256,512]{1,0:T(8,128)(2,1)S(1)}, u32[]{:S(2)}, u32[]{:S(2)}) %collective-permute-start.5) | collective-permute-done | bytes 262176 | tf_op jit(solution)/shard_map/ppermute | solution.py:294
  85.8 0.8 shard_map.92
  86.6 0.0 copy-start.7
  86.6 0.0 copy-start.8
  86.6 30.6 %all_to_all.20.refs_1_ = bf16[16,120,128]{2,1,0:T(8,128)(2,1)S(1)} all-to-all(bf16[16,120,128]{2,1,0:T(8,128)(2,1)S(1)} %shard_map.92), channel_id=1, replica_groups=mesh['wide'=16,'narrow'=16,'tp'=4] {'narrow'}, dimensions={0} | all-to-all | bytes 983040 | tf_op jit(solution)/shard_map/all_to_all | solution.py:290
  117.3 0.4 shard_map.93
  117.6 23.7 %all_to_all.21 = bf16[16,8,896]{2,1,0:T(8,128)(2,1)S(1)} all-to-all(bf16[16,8,896]{2,1,0:T(8,128)(2,1)S(1)} %bitcast.20), channel_id=1, replica_groups=mesh['wide'=16,'narrow'=16,'tp'=4] {'wide'}, dimensions={0} | all-to-all | bytes 458752 | tf_op jit(solution)/shard_map/all_to_all | solution.py:290
  141.4 1.2 shard_map.94
  (3 shorter events, 0.0 us)
Async XLA Ops:
  0.6 42.8 %copy-start = (bf16[1,1,3584,128]{3,2,1,0:T(8,128)(2,1)S(1)}, bf16[1,1,3584,128]{3,2,1,0:T(8,128)(2,1)}, u32[]{:S(2)}) copy-start(bf16[1,1,3584,128]{3,2,1,0:T(8,128)(2,1)} %param.11) | copy-start | bytes 2752516
  0.6 42.8 %copy-start.1 = (bf16[1,1,3584,128]{3,2,1,0:T(8,128)(2,1)S(1)}, bf16[1,1,3584,128]{3,2,1,0:T(8,128)(2,1)}, u32[]{:S(2)}) copy-start(bf16[1,1,3584,128]{3,2,1,0:T(8,128)(2,1)} %param.12) | copy-start | bytes 2752516
  3.6 52.6 %copy-start.2 = (bf16[1,1,128,3584]{3,2,1,0:T(8,128)(2,1)S(1)}, bf16[1,1,128,3584]{3,2,1,0:T(8,128)(2,1)}, u32[]{:S(2)}) copy-start(bf16[1,1,128,3584]{3,2,1,0:T(8,128)(2,1)} %param.13) | copy-start | bytes 2752516
  3.6 28.8 %all-to-all-start = ((bf16[16,8,896]{2,1,0:T(8,128)(2,1)}), bf16[16,8,896]{2,1,0:T(8,128)(2,1)S(1)}, u32[]{:S(2)}, u32[]{:S(2)}) async-start(bf16[16,8,896]{2,1,0:T(8,128)(2,1)} %bitcast.26), calls=%async_computation | async-start | bytes 458752 | tf_op jit(solution)/shard_map/all_to_all | solution.py:290
  21.3 31.7 %collective-permute-start = (bf16[1408,128]{1,0:T(8,128)(2,1)}, bf16[1408,128]{1,0:T(8,128)(2,1)}, u32[]{:S(2)}, u32[]{:S(2)}) collective-permute-start(bf16[1408,128]{1,0:T(8,128)(2,1)} %get-tuple-element.23), channel_id=1, source_target_pairs={{0,1},{1,2},{2,3},{3,0},{4,5},{5,6},{6,7},{7,4},{8,9},{9,10},{10,1... | collective-permute-start | bytes 1081352 | tf_op jit(solution)/shard_map/ppermute | solution.py:294
  23.2 33.0 %collective-permute-start.1 = (bf16[1408,128]{1,0:T(8,128)(2,1)}, bf16[1408,128]{1,0:T(8,128)(2,1)}, u32[]{:S(2)}, u32[]{:S(2)}) collective-permute-start(bf16[1408,128]{1,0:T(8,128)(2,1)} %get-tuple-element.24), channel_id=1, source_target_pairs={{0,2},{1,3},{2,0},{3,1},{4,6},{5,7},{6,4},{7,5},{8,10},{9,11},{10,... | collective-permute-start | bytes 1081352 | tf_op jit(solution)/shard_map/ppermute | solution.py:294
  25.1 31.1 %collective-permute-start.2 = (bf16[1408,128]{1,0:T(8,128)(2,1)}, bf16[1408,128]{1,0:T(8,128)(2,1)}, u32[]{:S(2)}, u32[]{:S(2)}) collective-permute-start(bf16[1408,128]{1,0:T(8,128)(2,1)} %get-tuple-element.25), channel_id=1, source_target_pairs={{0,3},{1,0},{2,1},{3,2},{4,7},{5,4},{6,5},{7,6},{8,11},{9,8},{10,9... | collective-permute-start | bytes 1081352 | tf_op jit(solution)/shard_map/ppermute | solution.py:294
  33.1 0.8 copy-start.4
  33.8 30.4 %all-to-all-start.1 = ((bf16[16,16,896]{2,1,0:T(8,128)(2,1)}), bf16[16,16,896]{2,1,0:T(8,128)(2,1)S(1)}, u32[]{:S(2)}, u32[]{:S(2)}) async-start(bf16[16,16,896]{2,1,0:T(8,128)(2,1)} %bitcast.23), calls=%async_computation.1 | async-start | bytes 917504 | tf_op jit(solution)/shard_map/all_to_all | solution.py:290
  44.7 0.8 copy-start.5
  45.5 30.3 %collective-permute-start.6 = (bf16[1792,128]{1,0:T(8,128)(2,1)}, bf16[1792,128]{1,0:T(8,128)(2,1)}, u32[]{:S(2)}, u32[]{:S(2)}) collective-permute-start(bf16[1792,128]{1,0:T(8,128)(2,1)} %get-tuple-element.27), channel_id=1, source_target_pairs={{0,1},{1,2},{2,3},{3,0},{4,5},{5,6},{6,7},{7,4},{8,9},{9,10},{10,1... | collective-permute-start | bytes 1376264 | tf_op jit(solution)/shard_map/ppermute | solution.py:294
  48.6 30.3 %collective-permute-start.7 = (bf16[1792,128]{1,0:T(8,128)(2,1)}, bf16[1792,128]{1,0:T(8,128)(2,1)}, u32[]{:S(2)}, u32[]{:S(2)}) collective-permute-start(bf16[1792,128]{1,0:T(8,128)(2,1)} %get-tuple-element.28), channel_id=1, source_target_pairs={{0,2},{1,3},{2,0},{3,1},{4,6},{5,7},{6,4},{7,5},{8,10},{9,11},{10,... | collective-permute-start | bytes 1376264 | tf_op jit(solution)/shard_map/ppermute | solution.py:294
  53.0 25.9 %copy-start.3 = (bf16[1,1,256,2,128]{4,3,2,1,0:T(2,128)(2,1)S(1)}, bf16[1,1,256,2,128]{4,3,2,1,0:T(2,128)(2,1)}, u32[]{:S(2)}) copy-start(bf16[1,1,256,2,128]{4,3,2,1,0:T(2,128)(2,1)} %param.10) | copy-start | bytes 393220
  53.0 25.9 %collective-permute-start.8 = (bf16[1792,128]{1,0:T(8,128)(2,1)}, bf16[1792,128]{1,0:T(8,128)(2,1)}, u32[]{:S(2)}, u32[]{:S(2)}) collective-permute-start(bf16[1792,128]{1,0:T(8,128)(2,1)} %get-tuple-element.29), channel_id=1, source_target_pairs={{0,3},{1,0},{2,1},{3,2},{4,7},{5,4},{6,5},{7,6},{8,11},{9,8},{10,9... | collective-permute-start | bytes 1376264 | tf_op jit(solution)/shard_map/ppermute | solution.py:294
  57.5 21.4 %copy-start.6 = (bf16[1792,128]{1,0:T(8,128)(2,1)S(1)}, bf16[1792,128]{1,0:T(8,128)(2,1)}, u32[]{:S(2)}) copy-start(bf16[1792,128]{1,0:T(8,128)(2,1)} %copy-done.5) | copy-start | bytes 1376260
  64.7 16.9 %collective-permute-start.3 = (bf16[256,512]{1,0:T(8,128)(2,1)S(1)}, bf16[256,512]{1,0:T(8,128)(2,1)S(1)}, u32[]{:S(2)}, u32[]{:S(2)}) collective-permute-start(bf16[256,512]{1,0:T(8,128)(2,1)S(1)} %shard_map.89.refs_0_), channel_id=1, source_target_pairs={{0,1},{1,2},{2,3},{3,0},{4,5},{5,6},{6,7},{7,4},{8,9},{9,10},{10,1... | collective-permute-start | bytes 786440 | tf_op jit(solution)/shard_map/ppermute | solution.py:294
  71.4 11.6 %collective-permute-start.4 = (bf16[256,512]{1,0:T(8,128)(2,1)S(1)}, bf16[256,512]{1,0:T(8,128)(2,1)S(1)}, u32[]{:S(2)}, u32[]{:S(2)}) collective-permute-start(bf16[256,512]{1,0:T(8,128)(2,1)S(1)} %shard_map.89.refs_0_), channel_id=1, source_target_pairs={{0,2},{1,3},{2,0},{3,1},{4,6},{5,7},{6,4},{7,5},{8,10},{9,11},{10,... | collective-permute-start | bytes 786440 | tf_op jit(solution)/shard_map/ppermute | solution.py:294
  75.8 10.0 %collective-permute-start.5 = (bf16[256,512]{1,0:T(8,128)(2,1)S(1)}, bf16[256,512]{1,0:T(8,128)(2,1)S(1)}, u32[]{:S(2)}, u32[]{:S(2)}) collective-permute-start(bf16[256,512]{1,0:T(8,128)(2,1)S(1)} %shard_map.89.refs_0_), channel_id=1, source_target_pairs={{0,3},{1,0},{2,1},{3,2},{4,7},{5,4},{6,5},{7,6},{8,11},{9,8},{10,9... | collective-permute-start | bytes 786440 | tf_op jit(solution)/shard_map/ppermute | solution.py:294
  86.6 54.8 %copy-start.7 = (bf16[128,16]{1,0:T(8,128)(2,1)S(1)}, bf16[128,16]{1,0:T(8,128)(2,1)}, u32[]{:S(2)}) copy-start(bf16[128,16]{1,0:T(8,128)(2,1)} %get-tuple-element.19.refs_1_) | copy-start | bytes 12292
  86.6 54.8 %copy-start.8 = (s32[16,8]{0,1:T(8,128)S(1)}, s32[16,8]{0,1:T(8,128)}, u32[]{:S(2)}) copy-start(s32[16,8]{0,1:T(8,128)} %param.8) | copy-start | bytes 1540

commit v7 on v6

--- a/solution.py
+++ b/solution.py
@@ -62,7 +62,7 @@
 
 
 def join_kernel(down_ref, *refs):
-    block_refs, out_ref = refs[:-1], refs[-1]
+    block_refs, out_ref = by_step([down_ref, *refs[:-1]])[1:], refs[-1]
     hidden, columns = down_ref.shape[0], out_ref.shape[1]
     own = lax.axis_index("tp") * columns
     out_ref[0:hidden, :] = down_ref[:, pl.ds(pl.multiple_of(own, TILE), columns)]
@@ -94,8 +94,8 @@
     group_cap, width, count, ids_hbm, gates_hbm, rows_hbm, down_hbm, preacts_hbm, *refs
 ):
     send_ref, place_ref = refs[:2]
-    block_refs = refs[2 : 1 + count]
-    ids_ref, gates_ref, rows_ref, sems = refs[1 + count :]
+    block_hbms = refs[2 : 1 + count]
+    ids_ref, gates_ref, rows_ref, block_refs, sems, out_sems = refs[1 + count :]
     columns = send_ref.shape[1]
     me = lax.axis_index("tp")
 
@@ -109,7 +109,8 @@
     ]
     packs = []
     hidden = down_hbm.shape[0]
-    for step, block_ref in enumerate(block_refs, 1):
+    for step in range(1, count):
+        block_ref = block_refs.at[step - 1]
         first = lax.rem(me + step, count) * columns
         for tile in range(columns // TILE):
             lanes = pl.ds(pl.multiple_of(first + tile * TILE, TILE), TILE)
@@ -144,6 +145,14 @@
     ).astype(jnp.float32)
     place = bits(place)
     place_ref[...] = place
+    for copy in packs:
+        copy.wait()
+    stores = [
+        pltpu.make_async_copy(block_refs.at[at], block_hbm, out_sems.at[at])
+        for at, block_hbm in enumerate(block_hbms)
+    ]
+    for copy in stores:
+        copy.start()
     send_ref[...] = nn(place, rows_ref[...]).astype(jnp.bfloat16)
     r, c = iota((rows, groups * width), 0), iota((rows, groups * width), 1)
     paired = nt(place, table.astype(jnp.bfloat16))
@@ -154,7 +163,7 @@
     notes = nn(spread(group_cap, rows), repeated)
     first = send_ref[:, 0:rows].astype(jnp.float32)
     send_ref[:, 0:rows] = (first + notes).astype(jnp.bfloat16)
-    for copy in packs:
+    for copy in stores:
         copy.wait()
 
 
@@ -190,7 +199,8 @@
 
 
 def prepare_kernel(count, preacts_ref, *refs):
-    blocks, early = refs[:count], refs[count : 2 * count - 1]
+    blocks = by_step(refs[:count])
+    early = by_step([preacts_ref, *refs[count : 2 * count - 1]])
     weight_ref, swish_ref, slope_ref, hidden_ref = refs[2 * count - 1 :]
     columns = weight_ref.shape[0]
     slots = swish_ref.shape[0]
@@ -198,9 +208,9 @@
         for part in range(2):
             first = (2 * at + part) * TILE
             weight_ref[:, first : first + TILE] = block_ref[part * columns : (part + 1) * columns, :]
-    tail = early[0].shape[0] - 2 * slots
+    tail = early[1].shape[0] - 2 * slots
     raw = jnp.concatenate(
-        [preacts_ref[...]] + [block_ref[tail:, :] for block_ref in early], axis=1
+        [preacts_ref[...]] + [block_ref[tail:, :] for block_ref in early[1:]], axis=1
     )
     slot, row = iota((slots, 2 * slots), 0), iota((slots, 2 * slots), 1)
     gate_pre = nn(bits(row == 2 * slot), raw)
@@ -213,7 +223,7 @@
 
 
 def expert_kernel(count, lane_cap, *refs):
-    parts = refs[:count]
+    parts = by_step(refs[:count])
     weight_ref, swish_ref, slope_ref, hidden_ref, out_ref = refs[count:]
     slots = parts[0].shape[0]
     columns = weight_ref.shape[0]
@@ -296,11 +306,18 @@
     )
 
 
+def far_first(count):
+    return [0] + sorted(range(1, count), key=lambda step: -min(step, count - step))
+
+
+def by_step(values):
+    order = far_first(len(values))
+    return [values[order.index(step)] for step in range(len(values))]
+
+
 def shift_all(values):
     count = len(values)
-    order = sorted(range(1, count), key=lambda step: min(step, count - step))
-    moved = {step: shift(values[step], step, count) for step in order}
-    return [values[0]] + [moved[step] for step in range(1, count)]
+    return [values[0]] + [shift(values[step], step, count) for step in range(1, count)]
 
 
 def per_device(d_out, expert_ids, gate_values, stored_preacts, w_gate, w_up, w_down):
@@ -328,16 +345,19 @@
         + [shape(early_rows, hidden_width)] * others,
         (ids, gate_values.T, d_out, w_down[0, 0], preacts),
         spaces=[pltpu.HBM] * 5,
-        out_spaces=[pltpu.VMEM] * (2 + others),
+        out_spaces=[pltpu.VMEM] * 2 + [pltpu.HBM] * others,
         vmem=60,
         scratch=[
             pltpu.VMEM(ids.shape, ids.dtype),
             pltpu.VMEM(ids.shape, gate_values.dtype),
             pltpu.VMEM((token_count, columns), d_out.dtype),
+            pltpu.VMEM((others, early_rows, hidden_width), d_out.dtype),
             pltpu.SemaphoreType.DMA((3 + others * (tiles + 1),)),
+            pltpu.SemaphoreType.DMA((others,)),
         ],
     )
-    early = shift_all([None] + early)[1:]
+    early = shift_all([None] + early)
+    early = [early[step] for step in far_first(split_count)[1:]]
     down_cols = call(
         join_kernel,
         shape(split_count * hidden_width, columns),
@@ -378,14 +398,14 @@
         lambda *refs: prepare_kernel(split_count, *refs),
         [shape(columns, 2 * hidden_all)]
         + [shape(slot_count, hidden_all, dtype=jnp.float32)] * 3,
-        (preacts, *blocks, *early),
+        (preacts, *(blocks[step] for step in far_first(split_count)), *early),
         size=8 << 20,
     )
     block_rows = columns // TILE * lane_cap + BLOCK
     terms = call(
         lambda *refs: expert_kernel(split_count, lane_cap, *refs),
         shape(lane_count, block_rows, TILE),
-        (*parts, *prepared),
+        (*(parts[step] for step in far_first(split_count)), *prepared),
         vmem=24,
     )
     back = exchange(terms, "narrow")

time: 145 us -> 144 us (level); the launches traced: 143 us -> 144 us
  waiting for transfers between devices: 13.6 us -> 11.9 us
  transfers between devices with their start and end apart: 11 -> 11, of which waited for: 4 -> 3; matrix products, arithmetic and copies ran while one was open for 0% -> 0% of each run, Pallas kernels for 4% -> 4%
where the time goes in v7:
time: 144 us
  starting transfers between devices  61.4 us (43%)
  blocking collectives  55.7 us (39%)
  Pallas kernels  12.1 us (8%)
  waiting for transfers between devices  11.9 us (8%)
  local copies, waits for them, and re-layouts  1.59 us (1%)
    all_to_all x2, blocking collectives, exchange(): return lax.all_to_all(values, axis, split_axis=0, concat_axis=0, tiled=True)  55.7 us
    ppermute x9, starting transfers between devices, shift(): lax.ppermute(values, 'tp', [(source, (source + step) % count) for source...  34 us
    all_to_all x2, starting transfers between devices, exchange(): return lax.all_to_all(values, axis, split_axis=0, concat_axis=0, tiled=True)  27.4 us
    pallas_call x9, Pallas kernels, call(): pl.pallas_call(kernel, out_shape=outs, in_specs=[pl.BlockSpec(memory_spac...  12.1 us
    all_to_all x2, waiting for transfers between devices, exchange(): return lax.all_to_all(values, axis, split_axis=0, concat_axis=0, tiled=True)  9.05 us
    ppermute x9, waiting for transfers between devices, shift(): lax.ppermute(values, 'tp', [(source, (source + step) % count) for source...  2.89 us
  transfers between devices with their start and end apart: 11, of which 3 were waited for; matrix products, arithmetic and copies ran while one was open for 0% of the time, Pallas kernels for 4%

profile of v7, /device:TPU:1, one launch (start us, length us, event | category | flops | bytes accessed | tf_op | source)
XLA Modules:
  0.0 143.6 jit_solution(3008205999518054166)
XLA Ops:
  0.6 0.0 copy-start
  0.6 0.0 copy-start.1
  0.7 3.4 %shard_map.86 = (bf16[128,896]{1,0:T(8,128)(2,1)}, bf16[128,16]{1,0:T(8,128)(2,1)}, bf16[1408,128]{1,0:T(8,128)(2,1)}, bf16[1408,128]{1,0:T(8,128)(2,1)}, bf16[1408,128]{1,0:T(8,128)(2,1)}) custom-call(s32[8,16]{1,0:T(8,128)} %bitcast.24, bf16[8,16]{1,0:T(8,128)(2,1)} %bitcast.27, bf16[16,3584]{1,0:T(8,128)(2,1)} %refs_2_.1, bf16[128,3584]{1,0:T(8,128)(2,1)} %bitcast.17, ...), custom_call_target="tpu_custom_call" | custom-call | bytes 1048576 | tf_op jit(solution)/shard_map/pallas_call | solution.py:36
  4.1 0.0 copy-start.2
  4.1 17.6 %all-to-all-start = ((bf16[16,8,896]{2,1,0:T(8,128)(2,1)}), bf16[16,8,896]{2,1,0:T(8,128)(2,1)S(1)}, u32[]{:S(2)}, u32[]{:S(2)}) async-start(bf16[16,8,896]{2,1,0:T(8,128)(2,1)} %bitcast.26), calls=%async_computation | async-start | bytes 458752 | tf_op jit(solution)/shard_map/all_to_all | solution.py:300
  21.7 1.9 %collective-permute-start = (bf16[1408,128]{1,0:T(8,128)(2,1)}, bf16[1408,128]{1,0:T(8,128)(2,1)}, u32[]{:S(2)}, u32[]{:S(2)}) collective-permute-start(bf16[1408,128]{1,0:T(8,128)(2,1)} %get-tuple-element.23), channel_id=1, source_target_pairs={{0,2},{1,3},{2,0},{3,1},{4,6},{5,7},{6,4},{7,5},{8,10},{9,11},{10,... | collective-permute-start | bytes 1081352 | tf_op jit(solution)/shard_map/ppermute | solution.py:304
  23.6 1.9 %collective-permute-start.1 = (bf16[1408,128]{1,0:T(8,128)(2,1)}, bf16[1408,128]{1,0:T(8,128)(2,1)}, u32[]{:S(2)}, u32[]{:S(2)}) collective-permute-start(bf16[1408,128]{1,0:T(8,128)(2,1)} %get-tuple-element.24), channel_id=1, source_target_pairs={{0,1},{1,2},{2,3},{3,0},{4,5},{5,6},{6,7},{7,4},{8,9},{9,10},{10,1... | collective-permute-start | bytes 1081352 | tf_op jit(solution)/shard_map/ppermute | solution.py:304
  25.6 4.6 %collective-permute-start.2 = (bf16[1408,128]{1,0:T(8,128)(2,1)}, bf16[1408,128]{1,0:T(8,128)(2,1)}, u32[]{:S(2)}, u32[]{:S(2)}) collective-permute-start(bf16[1408,128]{1,0:T(8,128)(2,1)} %get-tuple-element.25), channel_id=1, source_target_pairs={{0,3},{1,0},{2,1},{3,2},{4,7},{5,4},{6,5},{7,6},{8,11},{9,8},{10,9... | collective-permute-start | bytes 1081352 | tf_op jit(solution)/shard_map/ppermute | solution.py:304
  30.1 2.7 %all-to-all-done = bf16[16,8,896]{2,1,0:T(8,128)(2,1)S(1)} async-done(((bf16[16,8,896]{2,1,0:T(8,128)(2,1)}), bf16[16,8,896]{2,1,0:T(8,128)(2,1)S(1)}, u32[]{:S(2)}, u32[]{:S(2)}) %all-to-all-start) | async-done | bytes 229408 | tf_op jit(solution)/shard_map/all_to_all | solution.py:300
  32.9 0.6 shard_map.87
  33.5 0.0 copy-start.4
  33.5 0.8 copy-done.4
  34.3 9.8 %all-to-all-start.1 = ((bf16[16,16,896]{2,1,0:T(8,128)(2,1)}), bf16[16,16,896]{2,1,0:T(8,128)(2,1)S(1)}, u32[]{:S(2)}, u32[]{:S(2)}) async-start(bf16[16,16,896]{2,1,0:T(8,128)(2,1)} %bitcast.23), calls=%async_computation.1 | async-start | bytes 917504 | tf_op jit(solution)/shard_map/all_to_all | solution.py:300
  44.1 0.0 copy-done
  44.1 0.0 copy-done.1
  44.1 1.2 shard_map.90
  45.3 0.8 copy-done.5
  46.1 4.5 %collective-permute-start.6 = (bf16[1792,128]{1,0:T(8,128)(2,1)}, bf16[1792,128]{1,0:T(8,128)(2,1)}, u32[]{:S(2)}, u32[]{:S(2)}) collective-permute-start(bf16[1792,128]{1,0:T(8,128)(2,1)} %get-tuple-element.27), channel_id=1, source_target_pairs={{0,2},{1,3},{2,0},{3,1},{4,6},{5,7},{6,4},{7,5},{8,10},{9,11},{10,... | collective-permute-start | bytes 1376264 | tf_op jit(solution)/shard_map/ppermute | solution.py:304
  50.6 2.2 %collective-permute-start.7 = (bf16[1792,128]{1,0:T(8,128)(2,1)}, bf16[1792,128]{1,0:T(8,128)(2,1)}, u32[]{:S(2)}, u32[]{:S(2)}) collective-permute-start(bf16[1792,128]{1,0:T(8,128)(2,1)} %get-tuple-element.28), channel_id=1, source_target_pairs={{0,1},{1,2},{2,3},{3,0},{4,5},{5,6},{6,7},{7,4},{8,9},{9,10},{10,1... | collective-permute-start | bytes 1376264 | tf_op jit(solution)/shard_map/ppermute | solution.py:304
  52.8 0.0 collective-permute-done.refs_0_.refs_5_
  52.8 0.0 copy-start.3
  52.8 4.4 %collective-permute-start.8 = (bf16[1792,128]{1,0:T(8,128)(2,1)}, bf16[1792,128]{1,0:T(8,128)(2,1)}, u32[]{:S(2)}, u32[]{:S(2)}) collective-permute-start(bf16[1792,128]{1,0:T(8,128)(2,1)} %get-tuple-element.29), channel_id=1, source_target_pairs={{0,3},{1,0},{2,1},{3,2},{4,7},{5,4},{6,5},{7,6},{8,11},{9,8},{10,9... | collective-permute-start | bytes 1376264 | tf_op jit(solution)/shard_map/ppermute | solution.py:304
  57.2 0.0 collective-permute-done.1.refs_1_.refs_6_
  57.2 0.0 collective-permute-done.2.refs_2_.refs_7_
  57.3 0.0 copy-done.2
  57.3 1.3 shard_map.88.down_ref
  58.6 0.0 copy-start.6
  58.6 6.3 %all-to-all-done.1 = bf16[16,16,896]{2,1,0:T(8,128)(2,1)S(1)} async-done(((bf16[16,16,896]{2,1,0:T(8,128)(2,1)}), bf16[16,16,896]{2,1,0:T(8,128)(2,1)S(1)}, u32[]{:S(2)}, u32[]{:S(2)}) %all-to-all-start.1) | async-done | bytes 458784 | tf_op jit(solution)/shard_map/all_to_all | solution.py:300
  64.9 0.5 shard_map.89.refs_0_
  65.4 8.0 %collective-permute-start.3 = (bf16[256,512]{1,0:T(8,128)(2,1)S(1)}, bf16[256,512]{1,0:T(8,128)(2,1)S(1)}, u32[]{:S(2)}, u32[]{:S(2)}) collective-permute-start(bf16[256,512]{1,0:T(8,128)(2,1)S(1)} %shard_map.89.refs_0_), channel_id=1, source_target_pairs={{0,2},{1,3},{2,0},{3,1},{4,6},{5,7},{6,4},{7,5},{8,10},{9,11},{10,... | collective-permute-start | bytes 786440 | tf_op jit(solution)/shard_map/ppermute | solution.py:304
  73.4 2.2 %collective-permute-start.4 = (bf16[256,512]{1,0:T(8,128)(2,1)S(1)}, bf16[256,512]{1,0:T(8,128)(2,1)S(1)}, u32[]{:S(2)}, u32[]{:S(2)}) collective-permute-start(bf16[256,512]{1,0:T(8,128)(2,1)S(1)} %shard_map.89.refs_0_), channel_id=1, source_target_pairs={{0,1},{1,2},{2,3},{3,0},{4,5},{5,6},{6,7},{7,4},{8,9},{9,10},{10,1... | collective-permute-start | bytes 786440 | tf_op jit(solution)/shard_map/ppermute | solution.py:304
  75.6 0.0 collective-permute-done.6.refs_2_
  75.7 4.3 %collective-permute-start.5 = (bf16[256,512]{1,0:T(8,128)(2,1)S(1)}, bf16[256,512]{1,0:T(8,128)(2,1)S(1)}, u32[]{:S(2)}, u32[]{:S(2)}) collective-permute-start(bf16[256,512]{1,0:T(8,128)(2,1)S(1)} %shard_map.89.refs_0_), channel_id=1, source_target_pairs={{0,3},{1,0},{2,1},{3,2},{4,7},{5,4},{6,5},{7,6},{8,11},{9,8},{10,9... | collective-permute-start | bytes 786440 | tf_op jit(solution)/shard_map/ppermute | solution.py:304
  79.9 0.0 collective-permute-done.7.refs_3_
  80.0 0.0 collective-permute-done.8.refs_4_
  80.0 0.0 copy-done.3
  80.0 0.0 copy-done.6
  80.0 2.6 %shard_map.91 = (bf16[896,1024]{1,0:T(8,128)(2,1)S(1)}, f32[256,512]{1,0:T(8,128)S(1)}, f32[256,512]{1,0:T(8,128)S(1)}, f32[256,512]{1,0:T(8,128)S(1)}) custom-call(bf16[512,128]{1,0:T(8,128)(2,1)S(1)} %bitcast.22, bf16[1792,128]{1,0:T(8,128)(2,1)S(1)} %copy-done.6, bf16[1792,128]{1,0:T(8,128)(2,1)} %collective-permute-done.6.refs_2_, ...), custom_call_target="tpu_custom_call" | custom-call | bytes 8388608 | tf_op jit(solution)/shard_map/pallas_call | solution.py:36
  82.6 0.0 collective-permute-done.3.refs_1_
  82.6 2.9 %collective-permute-done.4.refs_2_ = bf16[256,512]{1,0:T(8,128)(2,1)S(1)} collective-permute-done((bf16[256,512]{1,0:T(8,128)(2,1)S(1)}, bf16[256,512]{1,0:T(8,128)(2,1)S(1)}, u32[]{:S(2)}, u32[]{:S(2)}) %collective-permute-start.4) | collective-permute-done | bytes 262176 | tf_op jit(solution)/shard_map/ppermute | solution.py:304
  85.5 0.0 collective-permute-done.5.refs_3_
  85.5 0.8 shard_map.92
  86.3 0.0 copy-start.8
  86.3 30.4 %all_to_all.20.refs_1_ = bf16[16,120,128]{2,1,0:T(8,128)(2,1)S(1)} all-to-all(bf16[16,120,128]{2,1,0:T(8,128)(2,1)S(1)} %shard_map.92), channel_id=1, replica_groups=mesh['wide'=16,'narrow'=16,'tp'=4] {'narrow'}, dimensions={0} | all-to-all | bytes 983040 | tf_op jit(solution)/shard_map/all_to_all | solution.py:300
  116.7 0.4 shard_map.93
  117.1 25.3 %all_to_all.21 = bf16[16,8,896]{2,1,0:T(8,128)(2,1)S(1)} all-to-all(bf16[16,8,896]{2,1,0:T(8,128)(2,1)S(1)} %bitcast.20), channel_id=1, replica_groups=mesh['wide'=16,'narrow'=16,'tp'=4] {'wide'}, dimensions={0} | all-to-all | bytes 458752 | tf_op jit(solution)/shard_map/all_to_all | solution.py:300
  142.4 0.0 copy-done.7
  142.4 1.2 shard_map.94
  (3 shorter events, 0.0 us)
Async XLA Ops:
  0.6 43.5 %copy-start = (bf16[1,1,3584,128]{3,2,1,0:T(8,128)(2,1)S(1)}, bf16[1,1,3584,128]{3,2,1,0:T(8,128)(2,1)}, u32[]{:S(2)}) copy-start(bf16[1,1,3584,128]{3,2,1,0:T(8,128)(2,1)} %param.11) | copy-start | bytes 2752516
  0.6 43.5 %copy-start.1 = (bf16[1,1,3584,128]{3,2,1,0:T(8,128)(2,1)S(1)}, bf16[1,1,3584,128]{3,2,1,0:T(8,128)(2,1)}, u32[]{:S(2)}) copy-start(bf16[1,1,3584,128]{3,2,1,0:T(8,128)(2,1)} %param.12) | copy-start | bytes 2752516
  4.1 53.2 %copy-start.2 = (bf16[1,1,128,3584]{3,2,1,0:T(8,128)(2,1)S(1)}, bf16[1,1,128,3584]{3,2,1,0:T(8,128)(2,1)}, u32[]{:S(2)}) copy-start(bf16[1,1,128,3584]{3,2,1,0:T(8,128)(2,1)} %param.13) | copy-start | bytes 2752516
  4.1 28.8 %all-to-all-start = ((bf16[16,8,896]{2,1,0:T(8,128)(2,1)}), bf16[16,8,896]{2,1,0:T(8,128)(2,1)S(1)}, u32[]{:S(2)}, u32[]{:S(2)}) async-start(bf16[16,8,896]{2,1,0:T(8,128)(2,1)} %bitcast.26), calls=%async_computation | async-start | bytes 458752 | tf_op jit(solution)/shard_map/all_to_all | solution.py:300
  21.7 31.1 %collective-permute-start = (bf16[1408,128]{1,0:T(8,128)(2,1)}, bf16[1408,128]{1,0:T(8,128)(2,1)}, u32[]{:S(2)}, u32[]{:S(2)}) collective-permute-start(bf16[1408,128]{1,0:T(8,128)(2,1)} %get-tuple-element.23), channel_id=1, source_target_pairs={{0,2},{1,3},{2,0},{3,1},{4,6},{5,7},{6,4},{7,5},{8,10},{9,11},{10,... | collective-permute-start | bytes 1081352 | tf_op jit(solution)/shard_map/ppermute | solution.py:304
  23.6 33.6 %collective-permute-start.1 = (bf16[1408,128]{1,0:T(8,128)(2,1)}, bf16[1408,128]{1,0:T(8,128)(2,1)}, u32[]{:S(2)}, u32[]{:S(2)}) collective-permute-start(bf16[1408,128]{1,0:T(8,128)(2,1)} %get-tuple-element.24), channel_id=1, source_target_pairs={{0,1},{1,2},{2,3},{3,0},{4,5},{5,6},{6,7},{7,4},{8,9},{9,10},{10,1... | collective-permute-start | bytes 1081352 | tf_op jit(solution)/shard_map/ppermute | solution.py:304
  25.6 31.7 %collective-permute-start.2 = (bf16[1408,128]{1,0:T(8,128)(2,1)}, bf16[1408,128]{1,0:T(8,128)(2,1)}, u32[]{:S(2)}, u32[]{:S(2)}) collective-permute-start(bf16[1408,128]{1,0:T(8,128)(2,1)} %get-tuple-element.25), channel_id=1, source_target_pairs={{0,3},{1,0},{2,1},{3,2},{4,7},{5,4},{6,5},{7,6},{8,11},{9,8},{10,9... | collective-permute-start | bytes 1081352 | tf_op jit(solution)/shard_map/ppermute | solution.py:304
  33.5 0.8 copy-start.4
  34.3 30.6 %all-to-all-start.1 = ((bf16[16,16,896]{2,1,0:T(8,128)(2,1)}), bf16[16,16,896]{2,1,0:T(8,128)(2,1)S(1)}, u32[]{:S(2)}, u32[]{:S(2)}) async-start(bf16[16,16,896]{2,1,0:T(8,128)(2,1)} %bitcast.23), calls=%async_computation.1 | async-start | bytes 917504 | tf_op jit(solution)/shard_map/all_to_all | solution.py:300
  45.3 0.8 copy-start.5
  46.1 29.6 %collective-permute-start.6 = (bf16[1792,128]{1,0:T(8,128)(2,1)}, bf16[1792,128]{1,0:T(8,128)(2,1)}, u32[]{:S(2)}, u32[]{:S(2)}) collective-permute-start(bf16[1792,128]{1,0:T(8,128)(2,1)} %get-tuple-element.27), channel_id=1, source_target_pairs={{0,2},{1,3},{2,0},{3,1},{4,6},{5,7},{6,4},{7,5},{8,10},{9,11},{10,... | collective-permute-start | bytes 1376264 | tf_op jit(solution)/shard_map/ppermute | solution.py:304
  50.6 29.4 %collective-permute-start.7 = (bf16[1792,128]{1,0:T(8,128)(2,1)}, bf16[1792,128]{1,0:T(8,128)(2,1)}, u32[]{:S(2)}, u32[]{:S(2)}) collective-permute-start(bf16[1792,128]{1,0:T(8,128)(2,1)} %get-tuple-element.28), channel_id=1, source_target_pairs={{0,1},{1,2},{2,3},{3,0},{4,5},{5,6},{6,7},{7,4},{8,9},{9,10},{10,1... | collective-permute-start | bytes 1376264 | tf_op jit(solution)/shard_map/ppermute | solution.py:304
  52.8 27.2 %copy-start.3 = (bf16[1,1,256,2,128]{4,3,2,1,0:T(2,128)(2,1)S(1)}, bf16[1,1,256,2,128]{4,3,2,1,0:T(2,128)(2,1)}, u32[]{:S(2)}) copy-start(bf16[1,1,256,2,128]{4,3,2,1,0:T(2,128)(2,1)} %param.10) | copy-start | bytes 393220
  52.8 27.1 %collective-permute-start.8 = (bf16[1792,128]{1,0:T(8,128)(2,1)}, bf16[1792,128]{1,0:T(8,128)(2,1)}, u32[]{:S(2)}, u32[]{:S(2)}) collective-permute-start(bf16[1792,128]{1,0:T(8,128)(2,1)} %get-tuple-element.29), channel_id=1, source_target_pairs={{0,3},{1,0},{2,1},{3,2},{4,7},{5,4},{6,5},{7,6},{8,11},{9,8},{10,9... | collective-permute-start | bytes 1376264 | tf_op jit(solution)/shard_map/ppermute | solution.py:304
  58.6 21.4 %copy-start.6 = (bf16[1792,128]{1,0:T(8,128)(2,1)S(1)}, bf16[1792,128]{1,0:T(8,128)(2,1)}, u32[]{:S(2)}) copy-start(bf16[1792,128]{1,0:T(8,128)(2,1)} %copy-done.5) | copy-start | bytes 1376260
  65.4 17.2 %collective-permute-start.3 = (bf16[256,512]{1,0:T(8,128)(2,1)S(1)}, bf16[256,512]{1,0:T(8,128)(2,1)S(1)}, u32[]{:S(2)}, u32[]{:S(2)}) collective-permute-start(bf16[256,512]{1,0:T(8,128)(2,1)S(1)} %shard_map.89.refs_0_), channel_id=1, source_target_pairs={{0,2},{1,3},{2,0},{3,1},{4,6},{5,7},{6,4},{7,5},{8,10},{9,11},{10,... | collective-permute-start | bytes 786440 | tf_op jit(solution)/shard_map/ppermute | solution.py:304
  73.4 12.1 %collective-permute-start.4 = (bf16[256,512]{1,0:T(8,128)(2,1)S(1)}, bf16[256,512]{1,0:T(8,128)(2,1)S(1)}, u32[]{:S(2)}, u32[]{:S(2)}) collective-permute-start(bf16[256,512]{1,0:T(8,128)(2,1)S(1)} %shard_map.89.refs_0_), channel_id=1, source_target_pairs={{0,1},{1,2},{2,3},{3,0},{4,5},{5,6},{6,7},{7,4},{8,9},{9,10},{10,1... | collective-permute-start | bytes 786440 | tf_op jit(solution)/shard_map/ppermute | solution.py:304
  75.7 9.9 %collective-permute-start.5 = (bf16[256,512]{1,0:T(8,128)(2,1)S(1)}, bf16[256,512]{1,0:T(8,128)(2,1)S(1)}, u32[]{:S(2)}, u32[]{:S(2)}) collective-permute-start(bf16[256,512]{1,0:T(8,128)(2,1)S(1)} %shard_map.89.refs_0_), channel_id=1, source_target_pairs={{0,3},{1,0},{2,1},{3,2},{4,7},{5,4},{6,5},{7,6},{8,11},{9,8},{10,9... | collective-permute-start | bytes 786440 | tf_op jit(solution)/shard_map/ppermute | solution.py:304
  86.3 56.1 %copy-start.7 = (bf16[128,16]{1,0:T(8,128)(2,1)S(1)}, bf16[128,16]{1,0:T(8,128)(2,1)}, u32[]{:S(2)}) copy-start(bf16[128,16]{1,0:T(8,128)(2,1)} %get-tuple-element.19.refs_1_) | copy-start | bytes 12292
  86.3 56.1 %copy-start.8 = (s32[16,8]{0,1:T(8,128)S(1)}, s32[16,8]{0,1:T(8,128)}, u32[]{:S(2)}) copy-start(s32[16,8]{0,1:T(8,128)} %param.8) | copy-start | bytes 1540

commit v8 on v7

--- a/solution.py
+++ b/solution.py
@@ -51,10 +51,10 @@
 
 
 def pack_rest_kernel(gate_ref, up_ref, after_ref, *out_refs):
-    count = len(out_refs)
+    count = len(out_refs) + 1
     width = gate_ref.shape[0] // count
     me = lax.axis_index("tp")
-    for step, out_ref in enumerate(out_refs):
+    for step, out_ref in enumerate(out_refs, 1):
         to = lax.rem(me + step, count)
         rows = pl.ds(pl.multiple_of(to * width, TILE), width)
         out_ref[0:width, :] = gate_ref[rows, :]
@@ -95,7 +95,7 @@
 ):
     send_ref, place_ref = refs[:2]
     block_hbms = refs[2 : 1 + count]
-    ids_ref, gates_ref, rows_ref, block_refs, sems, out_sems = refs[1 + count :]
+    ids_ref, gates_ref, rows_ref, down_ref, block_refs, sems, out_sems = refs[1 + count :]
     columns = send_ref.shape[1]
     me = lax.axis_index("tp")
 
@@ -107,19 +107,12 @@
         pltpu.make_async_copy(gates_hbm, gates_ref, sems.at[1]),
         pltpu.make_async_copy(rows_hbm.at[:, columns_of(me)], rows_ref, sems.at[2]),
     ]
-    packs = []
     hidden = down_hbm.shape[0]
-    for step in range(1, count):
-        block_ref = block_refs.at[step - 1]
-        first = lax.rem(me + step, count) * columns
-        for tile in range(columns // TILE):
-            lanes = pl.ds(pl.multiple_of(first + tile * TILE, TILE), TILE)
-            packs.append((down_hbm.at[:, lanes], block_ref.at[pl.ds(tile * hidden, hidden)]))
-        tail = pl.ds(columns // TILE * hidden, preacts_hbm.shape[0])
-        packs.append((preacts_hbm, block_ref.at[tail]))
-    packs = [
-        pltpu.make_async_copy(source, target, sems.at[3 + at])
-        for at, (source, target) in enumerate(packs)
+    tiles = columns // TILE
+    tail = pl.ds(tiles * hidden, preacts_hbm.shape[0])
+    packs = [pltpu.make_async_copy(down_hbm, down_ref, sems.at[3])] + [
+        pltpu.make_async_copy(preacts_hbm, block_refs.at[at, tail], sems.at[4 + at])
+        for at in range(count - 1)
     ]
     for copy in loads + packs:
         copy.start()
@@ -147,6 +140,11 @@
     place_ref[...] = place
     for copy in packs:
         copy.wait()
+    for step in range(1, count):
+        begin = lax.rem(me + step, count) * columns
+        for tile in range(tiles):
+            lanes = pl.ds(pl.multiple_of(begin + tile * TILE, TILE), TILE)
+            block_refs[step - 1, tile * hidden : (tile + 1) * hidden, :] = down_ref[:, lanes]
     stores = [
         pltpu.make_async_copy(block_refs.at[at], block_hbm, out_sems.at[at])
         for at, block_hbm in enumerate(block_hbms)
@@ -198,13 +196,20 @@
     return terms[0]
 
 
-def prepare_kernel(count, preacts_ref, *refs):
-    blocks = by_step(refs[:count])
-    early = by_step([preacts_ref, *refs[count : 2 * count - 1]])
-    weight_ref, swish_ref, slope_ref, hidden_ref = refs[2 * count - 1 :]
+def prepare_kernel(count, preacts_ref, gate_hbm, up_hbm, *refs):
+    blocks = by_step([None, *refs[: count - 1]])
+    early = by_step([preacts_ref, *refs[count - 1 : 2 * count - 2]])
+    weight_ref, swish_ref, slope_ref, hidden_ref, own_ref, sems = refs[2 * count - 2 :]
     columns = weight_ref.shape[0]
     slots = swish_ref.shape[0]
-    for at, block_ref in enumerate(blocks):
+    own = pl.ds(pl.multiple_of(lax.axis_index("tp") * columns, TILE), columns)
+    copies = [
+        pltpu.make_async_copy(source.at[own], own_ref.at[part], sems.at[part])
+        for part, source in enumerate((gate_hbm, up_hbm))
+    ]
+    for copy in copies:
+        copy.start()
+    for at, block_ref in enumerate(blocks[1:], 1):
         for part in range(2):
             first = (2 * at + part) * TILE
             weight_ref[:, first : first + TILE] = block_ref[part * columns : (part + 1) * columns, :]
@@ -220,6 +225,9 @@
     swish_ref[...] = swish_value
     slope_ref[...] = up_pre * (sigmoid_value * (1.0 + gate_pre * (1.0 - sigmoid_value)))
     hidden_ref[...] = swish_value * up_pre
+    for part, copy in enumerate(copies):
+        copy.wait()
+        weight_ref[:, part * TILE : (part + 1) * TILE] = own_ref[part]
 
 
 def expert_kernel(count, lane_cap, *refs):
@@ -351,8 +359,9 @@
             pltpu.VMEM(ids.shape, ids.dtype),
             pltpu.VMEM(ids.shape, gate_values.dtype),
             pltpu.VMEM((token_count, columns), d_out.dtype),
+            pltpu.VMEM((hidden_width, model_width), d_out.dtype),
             pltpu.VMEM((others, early_rows, hidden_width), d_out.dtype),
-            pltpu.SemaphoreType.DMA((3 + others * (tiles + 1),)),
+            pltpu.SemaphoreType.DMA((4 + others,)),
             pltpu.SemaphoreType.DMA((others,)),
         ],
     )
@@ -374,7 +383,7 @@
     )
     rest_packed = call(
         pack_rest_kernel,
-        [shape(2 * columns, hidden_width)] * split_count,
+        [shape(2 * columns, hidden_width)] * others,
         (
             w_gate[0, 0],
             w_up[0, 0],
@@ -383,7 +392,7 @@
         size=4 << 20,
         spaces=[pltpu.VMEM] * 2 + [pl.ANY],
     )
-    blocks = shift_all(rest_packed)
+    blocks = shift_all([None, *rest_packed])
     slot_rows = exchange(forward.reshape(lane_count, lane_cap, columns), "narrow").reshape(
         slot_count, columns
     )
@@ -398,7 +407,18 @@
         lambda *refs: prepare_kernel(split_count, *refs),
         [shape(columns, 2 * hidden_all)]
         + [shape(slot_count, hidden_all, dtype=jnp.float32)] * 3,
-        (preacts, *(blocks[step] for step in far_first(split_count)), *early),
+        (
+            preacts,
+            w_gate[0, 0],
+            w_up[0, 0],
+            *(blocks[step] for step in far_first(split_count)[1:]),
+            *early,
+        ),
+        spaces=[pltpu.VMEM] + [pl.ANY] * 2 + [pltpu.VMEM] * (2 * others),
+        scratch=[
+            pltpu.VMEM((2, columns, hidden_width), w_gate.dtype),
+            pltpu.SemaphoreType.DMA((2,)),
+        ],
         size=8 << 20,
     )
     block_rows = columns // TILE * lane_cap + BLOCK

time: 144 us -> 144 us (level)
  local copies, waits for them, and re-layouts: 1.59 us -> 6.38 us
  waiting for transfers between devices: 11.9 us -> 7.43 us
    unnamed x18 -> x30, local copies, waits for them, and re-layouts: 1.59 us -> 6.38 us
    all_to_all x2, waiting for transfers between devices: 9.05 us -> 4.81 us  [exchange(): return lax.all_to_all(values, axis, split_axis=0, concat_axis=0, tiled=True)]
where the time goes in v8:
time: 144 us; the launch traced here: 143 us
  starting transfers between devices  61.1 us (42%)
  blocking collectives  55.3 us (38%)
  Pallas kernels  12.2 us (8%)
  waiting for transfers between devices  7.43 us (5%)
  local copies, waits for them, and re-layouts  6.38 us (4%)
    all_to_all x2, blocking collectives, exchange(): return lax.all_to_all(values, axis, split_axis=0, concat_axis=0, tiled=True)  55.3 us
    ppermute x9, starting transfers between devices, shift(): lax.ppermute(values, 'tp', [(source, (source + step) % count) for source...  33.9 us
    all_to_all x2, starting transfers between devices, exchange(): return lax.all_to_all(values, axis, split_axis=0, concat_axis=0, tiled=True)  27.3 us
    pallas_call x9, Pallas kernels, call(): pl.pallas_call(kernel, out_shape=outs, in_specs=[pl.BlockSpec(memory_spac...  12.2 us
    unnamed x30, local copies, waits for them, and re-layouts  6.38 us
    all_to_all x2, waiting for transfers between devices, exchange(): return lax.all_to_all(values, axis, split_axis=0, concat_axis=0, tiled=True)  4.81 us
  transfers between devices with their start and end apart: 11, of which 3 were waited for; matrix products, arithmetic and copies ran while one was open for 0% of the time, Pallas kernels for 4%

profile of v8, /device:TPU:1, one launch (start us, length us, event | category | flops | bytes accessed | tf_op | source)
XLA Modules:
  0.0 143.4 jit_solution(4015083792133705415)
XLA Ops:
  0.6 0.0 copy-start
  0.6 0.0 copy-start.1
  0.7 3.7 %shard_map.86 = (bf16[128,896]{1,0:T(8,128)(2,1)}, bf16[128,16]{1,0:T(8,128)(2,1)}, bf16[1408,128]{1,0:T(8,128)(2,1)}, bf16[1408,128]{1,0:T(8,128)(2,1)}, bf16[1408,128]{1,0:T(8,128)(2,1)}) custom-call(s32[8,16]{1,0:T(8,128)} %bitcast.25, bf16[8,16]{1,0:T(8,128)(2,1)} %bitcast.28, bf16[16,3584]{1,0:T(8,128)(2,1)} %refs_2_.1, bf16[128,3584]{1,0:T(8,128)(2,1)} %bitcast.19, ...), custom_call_target="tpu_custom_call" | custom-call | bytes 1048576 | tf_op jit(solution)/shard_map/pallas_call | solution.py:36
  4.4 17.5 %all-to-all-start = ((bf16[16,8,896]{2,1,0:T(8,128)(2,1)}), bf16[16,8,896]{2,1,0:T(8,128)(2,1)S(1)}, u32[]{:S(2)}, u32[]{:S(2)}) async-start(bf16[16,8,896]{2,1,0:T(8,128)(2,1)} %bitcast.27), calls=%async_computation | async-start | bytes 458752 | tf_op jit(solution)/shard_map/all_to_all | solution.py:308
  21.9 1.9 %collective-permute-start = (bf16[1408,128]{1,0:T(8,128)(2,1)}, bf16[1408,128]{1,0:T(8,128)(2,1)S(1)}, u32[]{:S(2)}, u32[]{:S(2)}) collective-permute-start(bf16[1408,128]{1,0:T(8,128)(2,1)} %get-tuple-element.22), channel_id=1, source_target_pairs={{0,2},{1,3},{2,0},{3,1},{4,6},{5,7},{6,4},{7,5},{8,10},{9,11},{10,... | collective-permute-start | bytes 1081352 | tf_op jit(solution)/shard_map/ppermute | solution.py:312
  23.8 1.9 %collective-permute-start.1 = (bf16[1408,128]{1,0:T(8,128)(2,1)}, bf16[1408,128]{1,0:T(8,128)(2,1)S(1)}, u32[]{:S(2)}, u32[]{:S(2)}) collective-permute-start(bf16[1408,128]{1,0:T(8,128)(2,1)} %get-tuple-element.23), channel_id=1, source_target_pairs={{0,1},{1,2},{2,3},{3,0},{4,5},{5,6},{6,7},{7,4},{8,9},{9,10},{10,1... | collective-permute-start | bytes 1081352 | tf_op jit(solution)/shard_map/ppermute | solution.py:312
  25.7 4.6 %collective-permute-start.2 = (bf16[1408,128]{1,0:T(8,128)(2,1)}, bf16[1408,128]{1,0:T(8,128)(2,1)S(1)}, u32[]{:S(2)}, u32[]{:S(2)}) collective-permute-start(bf16[1408,128]{1,0:T(8,128)(2,1)} %get-tuple-element.24), channel_id=1, source_target_pairs={{0,3},{1,0},{2,1},{3,2},{4,7},{5,4},{6,5},{7,6},{8,11},{9,8},{10,9... | collective-permute-start | bytes 1081352 | tf_op jit(solution)/shard_map/ppermute | solution.py:312
  30.3 2.7 %all-to-all-done = bf16[16,8,896]{2,1,0:T(8,128)(2,1)S(1)} async-done(((bf16[16,8,896]{2,1,0:T(8,128)(2,1)}), bf16[16,8,896]{2,1,0:T(8,128)(2,1)S(1)}, u32[]{:S(2)}, u32[]{:S(2)}) %all-to-all-start) | async-done | bytes 229408 | tf_op jit(solution)/shard_map/all_to_all | solution.py:308
  33.0 1.5 %shard_map.87 = (bf16[2,128,896]{2,1,0:T(8,128)(2,1)}, bf16[128,128]{1,0:T(8,128)(2,1)S(1)}) custom-call(bf16[128,896]{1,0:T(8,128)(2,1)S(1)} %bitcast.18), custom_call_target="tpu_custom_call" | custom-call | bytes 1048576 | tf_op jit(solution)/shard_map/pallas_call | solution.py:36
  34.5 9.8 %all-to-all-start.1 = ((bf16[16,16,896]{2,1,0:T(8,128)(2,1)}), bf16[16,16,896]{2,1,0:T(8,128)(2,1)S(1)}, u32[]{:S(2)}, u32[]{:S(2)}) async-start(bf16[16,16,896]{2,1,0:T(8,128)(2,1)} %bitcast.6), calls=%async_computation.1 | async-start | bytes 917504 | tf_op jit(solution)/shard_map/all_to_all | solution.py:308
  44.2 0.0 copy-done
  44.3 0.0 copy-done.1
  44.3 1.2 shard_map.90
  45.5 4.5 %collective-permute-start.6 = (bf16[1792,128]{1,0:T(8,128)(2,1)}, bf16[1792,128]{1,0:T(8,128)(2,1)}, u32[]{:S(2)}, u32[]{:S(2)}) collective-permute-start(bf16[1792,128]{1,0:T(8,128)(2,1)} %get-tuple-element.25), channel_id=1, source_target_pairs={{0,2},{1,3},{2,0},{3,1},{4,6},{5,7},{6,4},{7,5},{8,10},{9,11},{10,... | collective-permute-start | bytes 1376264 | tf_op jit(solution)/shard_map/ppermute | solution.py:312
  50.0 2.2 %collective-permute-start.7 = (bf16[1792,128]{1,0:T(8,128)(2,1)}, bf16[1792,128]{1,0:T(8,128)(2,1)}, u32[]{:S(2)}, u32[]{:S(2)}) collective-permute-start(bf16[1792,128]{1,0:T(8,128)(2,1)} %get-tuple-element.26), channel_id=1, source_target_pairs={{0,1},{1,2},{2,3},{3,0},{4,5},{5,6},{6,7},{7,4},{8,9},{9,10},{10,1... | collective-permute-start | bytes 1376264 | tf_op jit(solution)/shard_map/ppermute | solution.py:312
  52.2 0.0 collective-permute-done.refs_0_.refs_6_
  52.2 0.0 copy-start.4
  52.2 0.7 copy-done.4
  53.0 4.3 %collective-permute-start.8 = (bf16[1792,128]{1,0:T(8,128)(2,1)}, bf16[1792,128]{1,0:T(8,128)(2,1)}, u32[]{:S(2)}, u32[]{:S(2)}) collective-permute-start(bf16[1792,128]{1,0:T(8,128)(2,1)} %get-tuple-element.27), channel_id=1, source_target_pairs={{0,3},{1,0},{2,1},{3,2},{4,7},{5,4},{6,5},{7,6},{8,11},{9,8},{10,9... | collective-permute-start | bytes 1376264 | tf_op jit(solution)/shard_map/ppermute | solution.py:312
  57.2 0.0 collective-permute-done.1.refs_1_.refs_7_
  57.2 0.0 copy-start.7
  57.2 0.7 copy-done.7
  58.0 0.0 collective-permute-done.2.refs_2_.refs_8_
  58.0 0.7 copy-done.10
  58.7 1.2 copy-done.2
  59.9 1.0 copy-done.5
  60.9 1.0 copy-done.8
  61.9 1.0 copy-done.11
  62.9 0.1 shard_map.88.down_ref
  63.0 2.1 %all-to-all-done.1 = bf16[16,16,896]{2,1,0:T(8,128)(2,1)S(1)} async-done(((bf16[16,16,896]{2,1,0:T(8,128)(2,1)}), bf16[16,16,896]{2,1,0:T(8,128)(2,1)S(1)}, u32[]{:S(2)}, u32[]{:S(2)}) %all-to-all-start.1) | async-done | bytes 458784 | tf_op jit(solution)/shard_map/all_to_all | solution.py:308
  65.1 0.5 shard_map.89.refs_0_
  65.6 8.0 %collective-permute-start.3 = (bf16[256,512]{1,0:T(8,128)(2,1)S(1)}, bf16[256,512]{1,0:T(8,128)(2,1)S(1)}, u32[]{:S(2)}, u32[]{:S(2)}) collective-permute-start(bf16[256,512]{1,0:T(8,128)(2,1)S(1)} %shard_map.89.refs_0_), channel_id=1, source_target_pairs={{0,2},{1,3},{2,0},{3,1},{4,6},{5,7},{6,4},{7,5},{8,10},{9,11},{10,... | collective-permute-start | bytes 786440 | tf_op jit(solution)/shard_map/ppermute | solution.py:312
  73.6 2.2 %collective-permute-start.4 = (bf16[256,512]{1,0:T(8,128)(2,1)S(1)}, bf16[256,512]{1,0:T(8,128)(2,1)S(1)}, u32[]{:S(2)}, u32[]{:S(2)}) collective-permute-start(bf16[256,512]{1,0:T(8,128)(2,1)S(1)} %shard_map.89.refs_0_), channel_id=1, source_target_pairs={{0,1},{1,2},{2,3},{3,0},{4,5},{5,6},{6,7},{7,4},{8,9},{9,10},{10,1... | collective-permute-start | bytes 786440 | tf_op jit(solution)/shard_map/ppermute | solution.py:312
  75.8 0.0 collective-permute-done.6.refs_3_
  75.8 4.3 %collective-permute-start.5 = (bf16[256,512]{1,0:T(8,128)(2,1)S(1)}, bf16[256,512]{1,0:T(8,128)(2,1)S(1)}, u32[]{:S(2)}, u32[]{:S(2)}) collective-permute-start(bf16[256,512]{1,0:T(8,128)(2,1)S(1)} %shard_map.89.refs_0_), channel_id=1, source_target_pairs={{0,3},{1,0},{2,1},{3,2},{4,7},{5,4},{6,5},{7,6},{8,11},{9,8},{10,9... | collective-permute-start | bytes 786440 | tf_op jit(solution)/shard_map/ppermute | solution.py:312
  80.1 0.0 collective-permute-done.7.refs_4_
  80.1 0.0 collective-permute-done.8.refs_5_
  80.1 0.0 copy-done.3
  80.2 2.9 %shard_map.91 = (bf16[896,1024]{1,0:T(8,128)(2,1)S(1)}, f32[256,512]{1,0:T(8,128)S(1)}, f32[256,512]{1,0:T(8,128)S(1)}, f32[256,512]{1,0:T(8,128)S(1)}) custom-call(bf16[512,128]{1,0:T(8,128)(2,1)S(1)} %bitcast.24, bf16[3584,128]{1,0:T(8,128)(2,1)S(1)} %bitcast.14, bf16[3584,128]{1,0:T(8,128)(2,1)S(1)} %bitcast.16, ...), custom_call_target="tpu_custom_call" | custom-call | bytes 8388608 | tf_op jit(solution)/shard_map/pallas_call | solution.py:36
  83.1 0.0 collective-permute-done.3.refs_1_
  83.1 2.6 %collective-permute-done.4.refs_2_ = bf16[256,512]{1,0:T(8,128)(2,1)S(1)} collective-permute-done((bf16[256,512]{1,0:T(8,128)(2,1)S(1)}, bf16[256,512]{1,0:T(8,128)(2,1)S(1)}, u32[]{:S(2)}, u32[]{:S(2)}) %collective-permute-start.4) | collective-permute-done | bytes 262176 | tf_op jit(solution)/shard_map/ppermute | solution.py:312
  85.7 0.0 collective-permute-done.5.refs_3_
  85.7 0.7 shard_map.92
  86.5 0.0 copy-start.14
  86.5 30.1 %all_to_all.20.refs_1_ = bf16[16,120,128]{2,1,0:T(8,128)(2,1)S(1)} all-to-all(bf16[16,120,128]{2,1,0:T(8,128)(2,1)S(1)} %shard_map.92), channel_id=1, replica_groups=mesh['wide'=16,'narrow'=16,'tp'=4] {'narrow'}, dimensions={0} | all-to-all | bytes 983040 | tf_op jit(solution)/shard_map/all_to_all | solution.py:308
  116.6 0.4 shard_map.93
  117.0 25.2 %all_to_all.21 = bf16[16,8,896]{2,1,0:T(8,128)(2,1)S(1)} all-to-all(bf16[16,8,896]{2,1,0:T(8,128)(2,1)S(1)} %bitcast.22), channel_id=1, replica_groups=mesh['wide'=16,'narrow'=16,'tp'=4] {'wide'}, dimensions={0} | all-to-all | bytes 458752 | tf_op jit(solution)/shard_map/all_to_all | solution.py:308
  142.1 1.2 shard_map.94
  (15 shorter events, 0.0 us)
Async XLA Ops:
  0.6 43.6 %copy-start = (bf16[1,1,3584,128]{3,2,1,0:T(8,128)(2,1)S(1)}, bf16[1,1,3584,128]{3,2,1,0:T(8,128)(2,1)}, u32[]{:S(2)}) copy-start(bf16[1,1,3584,128]{3,2,1,0:T(8,128)(2,1)} %param.11) | copy-start | bytes 2752516
  0.6 43.6 %copy-start.1 = (bf16[1,1,3584,128]{3,2,1,0:T(8,128)(2,1)S(1)}, bf16[1,1,3584,128]{3,2,1,0:T(8,128)(2,1)}, u32[]{:S(2)}) copy-start(bf16[1,1,3584,128]{3,2,1,0:T(8,128)(2,1)} %param.12) | copy-start | bytes 2752516
  4.4 28.6 %all-to-all-start = ((bf16[16,8,896]{2,1,0:T(8,128)(2,1)}), bf16[16,8,896]{2,1,0:T(8,128)(2,1)S(1)}, u32[]{:S(2)}, u32[]{:S(2)}) async-start(bf16[16,8,896]{2,1,0:T(8,128)(2,1)} %bitcast.27), calls=%async_computation | async-start | bytes 458752 | tf_op jit(solution)/shard_map/all_to_all | solution.py:308
  21.9 30.3 %collective-permute-start = (bf16[1408,128]{1,0:T(8,128)(2,1)}, bf16[1408,128]{1,0:T(8,128)(2,1)S(1)}, u32[]{:S(2)}, u32[]{:S(2)}) collective-permute-start(bf16[1408,128]{1,0:T(8,128)(2,1)} %get-tuple-element.22), channel_id=1, source_target_pairs={{0,2},{1,3},{2,0},{3,1},{4,6},{5,7},{6,4},{7,5},{8,10},{9,11},{10,... | collective-permute-start | bytes 1081352 | tf_op jit(solution)/shard_map/ppermute | solution.py:312
  23.8 33.5 %collective-permute-start.1 = (bf16[1408,128]{1,0:T(8,128)(2,1)}, bf16[1408,128]{1,0:T(8,128)(2,1)S(1)}, u32[]{:S(2)}, u32[]{:S(2)}) collective-permute-start(bf16[1408,128]{1,0:T(8,128)(2,1)} %get-tuple-element.23), channel_id=1, source_target_pairs={{0,1},{1,2},{2,3},{3,0},{4,5},{5,6},{6,7},{7,4},{8,9},{9,10},{10,1... | collective-permute-start | bytes 1081352 | tf_op jit(solution)/shard_map/ppermute | solution.py:312
  25.7 32.3 %collective-permute-start.2 = (bf16[1408,128]{1,0:T(8,128)(2,1)}, bf16[1408,128]{1,0:T(8,128)(2,1)S(1)}, u32[]{:S(2)}, u32[]{:S(2)}) collective-permute-start(bf16[1408,128]{1,0:T(8,128)(2,1)} %get-tuple-element.24), channel_id=1, source_target_pairs={{0,3},{1,0},{2,1},{3,2},{4,7},{5,4},{6,5},{7,6},{8,11},{9,8},{10,9... | collective-permute-start | bytes 1081352 | tf_op jit(solution)/shard_map/ppermute | solution.py:312
  34.5 30.6 %all-to-all-start.1 = ((bf16[16,16,896]{2,1,0:T(8,128)(2,1)}), bf16[16,16,896]{2,1,0:T(8,128)(2,1)S(1)}, u32[]{:S(2)}, u32[]{:S(2)}) async-start(bf16[16,16,896]{2,1,0:T(8,128)(2,1)} %bitcast.6), calls=%async_computation.1 | async-start | bytes 917504 | tf_op jit(solution)/shard_map/all_to_all | solution.py:308
  45.5 30.4 %collective-permute-start.6 = (bf16[1792,128]{1,0:T(8,128)(2,1)}, bf16[1792,128]{1,0:T(8,128)(2,1)}, u32[]{:S(2)}, u32[]{:S(2)}) collective-permute-start(bf16[1792,128]{1,0:T(8,128)(2,1)} %get-tuple-element.25), channel_id=1, source_target_pairs={{0,2},{1,3},{2,0},{3,1},{4,6},{5,7},{6,4},{7,5},{8,10},{9,11},{10,... | collective-permute-start | bytes 1376264 | tf_op jit(solution)/shard_map/ppermute | solution.py:312
  50.0 30.2 %collective-permute-start.7 = (bf16[1792,128]{1,0:T(8,128)(2,1)}, bf16[1792,128]{1,0:T(8,128)(2,1)}, u32[]{:S(2)}, u32[]{:S(2)}) collective-permute-start(bf16[1792,128]{1,0:T(8,128)(2,1)} %get-tuple-element.26), channel_id=1, source_target_pairs={{0,1},{1,2},{2,3},{3,0},{4,5},{5,6},{6,7},{7,4},{8,9},{9,10},{10,1... | collective-permute-start | bytes 1376264 | tf_op jit(solution)/shard_map/ppermute | solution.py:312
  52.2 0.8 copy-start.4
  53.0 27.2 %collective-permute-start.8 = (bf16[1792,128]{1,0:T(8,128)(2,1)}, bf16[1792,128]{1,0:T(8,128)(2,1)}, u32[]{:S(2)}, u32[]{:S(2)}) collective-permute-start(bf16[1792,128]{1,0:T(8,128)(2,1)} %get-tuple-element.27), channel_id=1, source_target_pairs={{0,3},{1,0},{2,1},{3,2},{4,7},{5,4},{6,5},{7,6},{8,11},{9,8},{10,9... | collective-permute-start | bytes 1376264 | tf_op jit(solution)/shard_map/ppermute | solution.py:312
  57.2 0.7 copy-start.7
  58.0 0.7 copy-start.10
  58.7 1.2 copy-start.2
  59.9 1.0 copy-start.5
  60.9 1.0 copy-start.8
  61.9 1.0 copy-start.11
  62.9 17.3 %copy-start.3 = (bf16[1,1,256,2,128]{4,3,2,1,0:T(2,128)(2,1)S(1)}, bf16[1,1,256,2,128]{4,3,2,1,0:T(2,128)(2,1)}, u32[]{:S(2)}) copy-start(bf16[1,1,256,2,128]{4,3,2,1,0:T(2,128)(2,1)} %param.10) | copy-start | bytes 393220
  65.1 15.1 %copy-start.6 = (bf16[1408,128]{1,0:T(8,128)(2,1)S(1)}, bf16[1408,128]{1,0:T(8,128)(2,1)}, u32[]{:S(2)}) copy-start(bf16[1408,128]{1,0:T(8,128)(2,1)} %copy-done.4) | copy-start | bytes 1081348
  65.1 15.1 %copy-start.9 = (bf16[1408,128]{1,0:T(8,128)(2,1)S(1)}, bf16[1408,128]{1,0:T(8,128)(2,1)}, u32[]{:S(2)}) copy-start(bf16[1408,128]{1,0:T(8,128)(2,1)} %copy-done.7) | copy-start | bytes 1081348
  65.1 15.1 %copy-start.12 = (bf16[1408,128]{1,0:T(8,128)(2,1)S(1)}, bf16[1408,128]{1,0:T(8,128)(2,1)}, u32[]{:S(2)}) copy-start(bf16[1408,128]{1,0:T(8,128)(2,1)} %copy-done.10) | copy-start | bytes 1081348
  65.6 17.5 %collective-permute-start.3 = (bf16[256,512]{1,0:T(8,128)(2,1)S(1)}, bf16[256,512]{1,0:T(8,128)(2,1)S(1)}, u32[]{:S(2)}, u32[]{:S(2)}) collective-permute-start(bf16[256,512]{1,0:T(8,128)(2,1)S(1)} %shard_map.89.refs_0_), channel_id=1, source_target_pairs={{0,2},{1,3},{2,0},{3,1},{4,6},{5,7},{6,4},{7,5},{8,10},{9,11},{10,... | collective-permute-start | bytes 786440 | tf_op jit(solution)/shard_map/ppermute | solution.py:312
  73.6 12.1 %collective-permute-start.4 = (bf16[256,512]{1,0:T(8,128)(2,1)S(1)}, bf16[256,512]{1,0:T(8,128)(2,1)S(1)}, u32[]{:S(2)}, u32[]{:S(2)}) collective-permute-start(bf16[256,512]{1,0:T(8,128)(2,1)S(1)} %shard_map.89.refs_0_), channel_id=1, source_target_pairs={{0,1},{1,2},{2,3},{3,0},{4,5},{5,6},{6,7},{7,4},{8,9},{9,10},{10,1... | collective-permute-start | bytes 786440 | tf_op jit(solution)/shard_map/ppermute | solution.py:312
  75.8 9.8 %collective-permute-start.5 = (bf16[256,512]{1,0:T(8,128)(2,1)S(1)}, bf16[256,512]{1,0:T(8,128)(2,1)S(1)}, u32[]{:S(2)}, u32[]{:S(2)}) collective-permute-start(bf16[256,512]{1,0:T(8,128)(2,1)S(1)} %shard_map.89.refs_0_), channel_id=1, source_target_pairs={{0,3},{1,0},{2,1},{3,2},{4,7},{5,4},{6,5},{7,6},{8,11},{9,8},{10,9... | collective-permute-start | bytes 786440 | tf_op jit(solution)/shard_map/ppermute | solution.py:312
  86.4 55.7 %copy-start.13 = (bf16[128,16]{1,0:T(8,128)(2,1)S(1)}, bf16[128,16]{1,0:T(8,128)(2,1)}, u32[]{:S(2)}) copy-start(bf16[128,16]{1,0:T(8,128)(2,1)} %get-tuple-element.18.refs_1_) | copy-start | bytes 12292
  86.5 55.7 %copy-start.14 = (s32[16,8]{0,1:T(8,128)S(1)}, s32[16,8]{0,1:T(8,128)}, u32[]{:S(2)}) copy-start(s32[16,8]{0,1:T(8,128)} %param.8) | copy-start | bytes 1540

commit v9 on v7

--- a/solution.py
+++ b/solution.py
@@ -94,8 +94,8 @@
     group_cap, width, count, ids_hbm, gates_hbm, rows_hbm, down_hbm, preacts_hbm, *refs
 ):
     send_ref, place_ref = refs[:2]
-    block_hbms = refs[2 : 1 + count]
-    ids_ref, gates_ref, rows_ref, block_refs, sems, out_sems = refs[1 + count :]
+    block_refs = refs[2 : 1 + count]
+    ids_ref, gates_ref, rows_ref, sems = refs[1 + count :]
     columns = send_ref.shape[1]
     me = lax.axis_index("tp")
 
@@ -109,8 +109,7 @@
     ]
     packs = []
     hidden = down_hbm.shape[0]
-    for step in range(1, count):
-        block_ref = block_refs.at[step - 1]
+    for step, block_ref in enumerate(block_refs, 1):
         first = lax.rem(me + step, count) * columns
         for tile in range(columns // TILE):
             lanes = pl.ds(pl.multiple_of(first + tile * TILE, TILE), TILE)
@@ -145,14 +144,6 @@
     ).astype(jnp.float32)
     place = bits(place)
     place_ref[...] = place
-    for copy in packs:
-        copy.wait()
-    stores = [
-        pltpu.make_async_copy(block_refs.at[at], block_hbm, out_sems.at[at])
-        for at, block_hbm in enumerate(block_hbms)
-    ]
-    for copy in stores:
-        copy.start()
     send_ref[...] = nn(place, rows_ref[...]).astype(jnp.bfloat16)
     r, c = iota((rows, groups * width), 0), iota((rows, groups * width), 1)
     paired = nt(place, table.astype(jnp.bfloat16))
@@ -163,7 +154,7 @@
     notes = nn(spread(group_cap, rows), repeated)
     first = send_ref[:, 0:rows].astype(jnp.float32)
     send_ref[:, 0:rows] = (first + notes).astype(jnp.bfloat16)
-    for copy in stores:
+    for copy in packs:
         copy.wait()
 
 
@@ -345,15 +336,13 @@
         + [shape(early_rows, hidden_width)] * others,
         (ids, gate_values.T, d_out, w_down[0, 0], preacts),
         spaces=[pltpu.HBM] * 5,
-        out_spaces=[pltpu.VMEM] * 2 + [pltpu.HBM] * others,
+        out_spaces=[pltpu.VMEM] * (2 + others),
         vmem=60,
         scratch=[
             pltpu.VMEM(ids.shape, ids.dtype),
             pltpu.VMEM(ids.shape, gate_values.dtype),
             pltpu.VMEM((token_count, columns), d_out.dtype),
-            pltpu.VMEM((others, early_rows, hidden_width), d_out.dtype),
             pltpu.SemaphoreType.DMA((3 + others * (tiles + 1),)),
-            pltpu.SemaphoreType.DMA((others,)),
         ],
     )
     early = shift_all([None] + early)

time: 144 us -> 144 us (level)
  no operation moved by 1% of the time
where the time goes in v9:
time: 144 us; the launch traced here: 143 us
  starting transfers between devices  61.4 us (43%)
  blocking collectives  55.7 us (39%)
  waiting for transfers between devices  11.9 us (8%)
  Pallas kernels  11.6 us (8%)
  local copies, waits for them, and re-layouts  1.59 us (1%)
    all_to_all x2, blocking collectives, exchange(): return lax.all_to_all(values, axis, split_axis=0, concat_axis=0, tiled=True)  55.7 us
    ppermute x9, starting transfers between devices, shift(): lax.ppermute(values, 'tp', [(source, (source + step) % count) for source...  34 us
    all_to_all x2, starting transfers between devices, exchange(): return lax.all_to_all(values, axis, split_axis=0, concat_axis=0, tiled=True)  27.4 us
    pallas_call x9, Pallas kernels, call(): pl.pallas_call(kernel, out_shape=outs, in_specs=[pl.BlockSpec(memory_spac...  11.6 us
    all_to_all x2, waiting for transfers between devices, exchange(): return lax.all_to_all(values, axis, split_axis=0, concat_axis=0, tiled=True)  9.03 us
    ppermute x9, waiting for transfers between devices, shift(): lax.ppermute(values, 'tp', [(source, (source + step) % count) for source...  2.9 us
  transfers between devices with their start and end apart: 11, of which 3 were waited for; matrix products, arithmetic and copies ran while one was open for 0% of the time, Pallas kernels for 4%

profile of v9, /device:TPU:1, one launch (start us, length us, event | category | flops | bytes accessed | tf_op | source)
XLA Modules:
  0.0 143.2 jit_solution(9148802636689585730)
XLA Ops:
  0.6 0.0 copy-start
  0.6 0.0 copy-start.1
  0.7 3.0 %shard_map.86 = (bf16[128,896]{1,0:T(8,128)(2,1)}, bf16[128,16]{1,0:T(8,128)(2,1)}, bf16[1408,128]{1,0:T(8,128)(2,1)}, bf16[1408,128]{1,0:T(8,128)(2,1)}, bf16[1408,128]{1,0:T(8,128)(2,1)}) custom-call(s32[8,16]{1,0:T(8,128)} %bitcast.24, bf16[8,16]{1,0:T(8,128)(2,1)} %bitcast.27, bf16[16,3584]{1,0:T(8,128)(2,1)} %refs_2_.1, bf16[128,3584]{1,0:T(8,128)(2,1)} %bitcast.17, ...), custom_call_target="tpu_custom_call" | custom-call | bytes 1048576 | tf_op jit(solution)/shard_map/pallas_call | solution.py:36
  3.6 0.0 copy-start.2
  3.6 17.6 %all-to-all-start = ((bf16[16,8,896]{2,1,0:T(8,128)(2,1)}), bf16[16,8,896]{2,1,0:T(8,128)(2,1)S(1)}, u32[]{:S(2)}, u32[]{:S(2)}) async-start(bf16[16,8,896]{2,1,0:T(8,128)(2,1)} %bitcast.26), calls=%async_computation | async-start | bytes 458752 | tf_op jit(solution)/shard_map/all_to_all | solution.py:291
  21.3 1.9 %collective-permute-start = (bf16[1408,128]{1,0:T(8,128)(2,1)}, bf16[1408,128]{1,0:T(8,128)(2,1)}, u32[]{:S(2)}, u32[]{:S(2)}) collective-permute-start(bf16[1408,128]{1,0:T(8,128)(2,1)} %get-tuple-element.23), channel_id=1, source_target_pairs={{0,2},{1,3},{2,0},{3,1},{4,6},{5,7},{6,4},{7,5},{8,10},{9,11},{10,... | collective-permute-start | bytes 1081352 | tf_op jit(solution)/shard_map/ppermute | solution.py:295
  23.2 1.9 %collective-permute-start.1 = (bf16[1408,128]{1,0:T(8,128)(2,1)}, bf16[1408,128]{1,0:T(8,128)(2,1)}, u32[]{:S(2)}, u32[]{:S(2)}) collective-permute-start(bf16[1408,128]{1,0:T(8,128)(2,1)} %get-tuple-element.24), channel_id=1, source_target_pairs={{0,1},{1,2},{2,3},{3,0},{4,5},{5,6},{6,7},{7,4},{8,9},{9,10},{10,1... | collective-permute-start | bytes 1081352 | tf_op jit(solution)/shard_map/ppermute | solution.py:295
  25.1 4.6 %collective-permute-start.2 = (bf16[1408,128]{1,0:T(8,128)(2,1)}, bf16[1408,128]{1,0:T(8,128)(2,1)}, u32[]{:S(2)}, u32[]{:S(2)}) collective-permute-start(bf16[1408,128]{1,0:T(8,128)(2,1)} %get-tuple-element.25), channel_id=1, source_target_pairs={{0,3},{1,0},{2,1},{3,2},{4,7},{5,4},{6,5},{7,6},{8,11},{9,8},{10,9... | collective-permute-start | bytes 1081352 | tf_op jit(solution)/shard_map/ppermute | solution.py:295
  29.7 2.7 %all-to-all-done = bf16[16,8,896]{2,1,0:T(8,128)(2,1)S(1)} async-done(((bf16[16,8,896]{2,1,0:T(8,128)(2,1)}), bf16[16,8,896]{2,1,0:T(8,128)(2,1)S(1)}, u32[]{:S(2)}, u32[]{:S(2)}) %all-to-all-start) | async-done | bytes 229408 | tf_op jit(solution)/shard_map/all_to_all | solution.py:291
  32.4 0.6 shard_map.87
  33.1 0.0 copy-start.4
  33.1 0.8 copy-done.4
  33.8 9.8 %all-to-all-start.1 = ((bf16[16,16,896]{2,1,0:T(8,128)(2,1)}), bf16[16,16,896]{2,1,0:T(8,128)(2,1)S(1)}, u32[]{:S(2)}, u32[]{:S(2)}) async-start(bf16[16,16,896]{2,1,0:T(8,128)(2,1)} %bitcast.23), calls=%async_computation.1 | async-start | bytes 917504 | tf_op jit(solution)/shard_map/all_to_all | solution.py:291
  43.6 0.0 copy-done
  43.6 0.0 copy-done.1
  43.7 1.2 shard_map.90
  44.8 0.8 copy-done.5
  45.6 4.5 %collective-permute-start.6 = (bf16[1792,128]{1,0:T(8,128)(2,1)}, bf16[1792,128]{1,0:T(8,128)(2,1)}, u32[]{:S(2)}, u32[]{:S(2)}) collective-permute-start(bf16[1792,128]{1,0:T(8,128)(2,1)} %get-tuple-element.27), channel_id=1, source_target_pairs={{0,2},{1,3},{2,0},{3,1},{4,6},{5,7},{6,4},{7,5},{8,10},{9,11},{10,... | collective-permute-start | bytes 1376264 | tf_op jit(solution)/shard_map/ppermute | solution.py:295
  50.1 2.2 %collective-permute-start.7 = (bf16[1792,128]{1,0:T(8,128)(2,1)}, bf16[1792,128]{1,0:T(8,128)(2,1)}, u32[]{:S(2)}, u32[]{:S(2)}) collective-permute-start(bf16[1792,128]{1,0:T(8,128)(2,1)} %get-tuple-element.28), channel_id=1, source_target_pairs={{0,1},{1,2},{2,3},{3,0},{4,5},{5,6},{6,7},{7,4},{8,9},{9,10},{10,1... | collective-permute-start | bytes 1376264 | tf_op jit(solution)/shard_map/ppermute | solution.py:295
  52.4 0.0 collective-permute-done.refs_0_.refs_5_
  52.4 0.0 copy-start.3
  52.4 4.4 %collective-permute-start.8 = (bf16[1792,128]{1,0:T(8,128)(2,1)}, bf16[1792,128]{1,0:T(8,128)(2,1)}, u32[]{:S(2)}, u32[]{:S(2)}) collective-permute-start(bf16[1792,128]{1,0:T(8,128)(2,1)} %get-tuple-element.29), channel_id=1, source_target_pairs={{0,3},{1,0},{2,1},{3,2},{4,7},{5,4},{6,5},{7,6},{8,11},{9,8},{10,9... | collective-permute-start | bytes 1376264 | tf_op jit(solution)/shard_map/ppermute | solution.py:295
  56.8 0.0 collective-permute-done.1.refs_1_.refs_6_
  56.8 0.0 collective-permute-done.2.refs_2_.refs_7_
  56.8 0.0 copy-done.2
  56.8 1.3 shard_map.88.down_ref
  58.2 0.0 copy-start.6
  58.2 6.3 %all-to-all-done.1 = bf16[16,16,896]{2,1,0:T(8,128)(2,1)S(1)} async-done(((bf16[16,16,896]{2,1,0:T(8,128)(2,1)}), bf16[16,16,896]{2,1,0:T(8,128)(2,1)S(1)}, u32[]{:S(2)}, u32[]{:S(2)}) %all-to-all-start.1) | async-done | bytes 458784 | tf_op jit(solution)/shard_map/all_to_all | solution.py:291
  64.5 0.5 shard_map.89.refs_0_
  64.9 8.0 %collective-permute-start.3 = (bf16[256,512]{1,0:T(8,128)(2,1)S(1)}, bf16[256,512]{1,0:T(8,128)(2,1)S(1)}, u32[]{:S(2)}, u32[]{:S(2)}) collective-permute-start(bf16[256,512]{1,0:T(8,128)(2,1)S(1)} %shard_map.89.refs_0_), channel_id=1, source_target_pairs={{0,2},{1,3},{2,0},{3,1},{4,6},{5,7},{6,4},{7,5},{8,10},{9,11},{10,... | collective-permute-start | bytes 786440 | tf_op jit(solution)/shard_map/ppermute | solution.py:295
  73.0 2.3 %collective-permute-start.4 = (bf16[256,512]{1,0:T(8,128)(2,1)S(1)}, bf16[256,512]{1,0:T(8,128)(2,1)S(1)}, u32[]{:S(2)}, u32[]{:S(2)}) collective-permute-start(bf16[256,512]{1,0:T(8,128)(2,1)S(1)} %shard_map.89.refs_0_), channel_id=1, source_target_pairs={{0,1},{1,2},{2,3},{3,0},{4,5},{5,6},{6,7},{7,4},{8,9},{9,10},{10,1... | collective-permute-start | bytes 786440 | tf_op jit(solution)/shard_map/ppermute | solution.py:295
  75.2 0.0 collective-permute-done.6.refs_2_
  75.2 4.2 %collective-permute-start.5 = (bf16[256,512]{1,0:T(8,128)(2,1)S(1)}, bf16[256,512]{1,0:T(8,128)(2,1)S(1)}, u32[]{:S(2)}, u32[]{:S(2)}) collective-permute-start(bf16[256,512]{1,0:T(8,128)(2,1)S(1)} %shard_map.89.refs_0_), channel_id=1, source_target_pairs={{0,3},{1,0},{2,1},{3,2},{4,7},{5,4},{6,5},{7,6},{8,11},{9,8},{10,9... | collective-permute-start | bytes 786440 | tf_op jit(solution)/shard_map/ppermute | solution.py:295
  79.5 0.0 collective-permute-done.7.refs_3_
  79.5 0.0 collective-permute-done.8.refs_4_
  79.5 0.0 copy-done.3
  79.5 0.0 copy-done.6
  79.5 2.6 %shard_map.91 = (bf16[896,1024]{1,0:T(8,128)(2,1)S(1)}, f32[256,512]{1,0:T(8,128)S(1)}, f32[256,512]{1,0:T(8,128)S(1)}, f32[256,512]{1,0:T(8,128)S(1)}) custom-call(bf16[512,128]{1,0:T(8,128)(2,1)S(1)} %bitcast.22, bf16[1792,128]{1,0:T(8,128)(2,1)S(1)} %copy-done.6, bf16[1792,128]{1,0:T(8,128)(2,1)} %collective-permute-done.6.refs_2_, ...), custom_call_target="tpu_custom_call" | custom-call | bytes 8388608 | tf_op jit(solution)/shard_map/pallas_call | solution.py:36
  82.2 0.0 collective-permute-done.3.refs_1_
  82.2 2.9 %collective-permute-done.4.refs_2_ = bf16[256,512]{1,0:T(8,128)(2,1)S(1)} collective-permute-done((bf16[256,512]{1,0:T(8,128)(2,1)S(1)}, bf16[256,512]{1,0:T(8,128)(2,1)S(1)}, u32[]{:S(2)}, u32[]{:S(2)}) %collective-permute-start.4) | collective-permute-done | bytes 262176 | tf_op jit(solution)/shard_map/ppermute | solution.py:295
  85.1 0.0 collective-permute-done.5.refs_3_
  85.1 0.8 shard_map.92
  85.8 0.0 copy-start.7
  85.8 0.0 copy-start.8
  85.8 30.4 %all_to_all.20.refs_1_ = bf16[16,120,128]{2,1,0:T(8,128)(2,1)S(1)} all-to-all(bf16[16,120,128]{2,1,0:T(8,128)(2,1)S(1)} %shard_map.92), channel_id=1, replica_groups=mesh['wide'=16,'narrow'=16,'tp'=4] {'narrow'}, dimensions={0} | all-to-all | bytes 983040 | tf_op jit(solution)/shard_map/all_to_all | solution.py:291
  116.3 0.4 shard_map.93
  116.7 25.3 %all_to_all.21 = bf16[16,8,896]{2,1,0:T(8,128)(2,1)S(1)} all-to-all(bf16[16,8,896]{2,1,0:T(8,128)(2,1)S(1)} %bitcast.20), channel_id=1, replica_groups=mesh['wide'=16,'narrow'=16,'tp'=4] {'wide'}, dimensions={0} | all-to-all | bytes 458752 | tf_op jit(solution)/shard_map/all_to_all | solution.py:291
  141.9 1.2 shard_map.94
  (3 shorter events, 0.0 us)
Async XLA Ops:
  0.6 43.0 %copy-start = (bf16[1,1,3584,128]{3,2,1,0:T(8,128)(2,1)S(1)}, bf16[1,1,3584,128]{3,2,1,0:T(8,128)(2,1)}, u32[]{:S(2)}) copy-start(bf16[1,1,3584,128]{3,2,1,0:T(8,128)(2,1)} %param.11) | copy-start | bytes 2752516
  0.6 43.0 %copy-start.1 = (bf16[1,1,3584,128]{3,2,1,0:T(8,128)(2,1)S(1)}, bf16[1,1,3584,128]{3,2,1,0:T(8,128)(2,1)}, u32[]{:S(2)}) copy-start(bf16[1,1,3584,128]{3,2,1,0:T(8,128)(2,1)} %param.12) | copy-start | bytes 2752516
  3.6 53.2 %copy-start.2 = (bf16[1,1,128,3584]{3,2,1,0:T(8,128)(2,1)S(1)}, bf16[1,1,128,3584]{3,2,1,0:T(8,128)(2,1)}, u32[]{:S(2)}) copy-start(bf16[1,1,128,3584]{3,2,1,0:T(8,128)(2,1)} %param.13) | copy-start | bytes 2752516
  3.6 28.8 %all-to-all-start = ((bf16[16,8,896]{2,1,0:T(8,128)(2,1)}), bf16[16,8,896]{2,1,0:T(8,128)(2,1)S(1)}, u32[]{:S(2)}, u32[]{:S(2)}) async-start(bf16[16,8,896]{2,1,0:T(8,128)(2,1)} %bitcast.26), calls=%async_computation | async-start | bytes 458752 | tf_op jit(solution)/shard_map/all_to_all | solution.py:291
  21.3 31.1 %collective-permute-start = (bf16[1408,128]{1,0:T(8,128)(2,1)}, bf16[1408,128]{1,0:T(8,128)(2,1)}, u32[]{:S(2)}, u32[]{:S(2)}) collective-permute-start(bf16[1408,128]{1,0:T(8,128)(2,1)} %get-tuple-element.23), channel_id=1, source_target_pairs={{0,2},{1,3},{2,0},{3,1},{4,6},{5,7},{6,4},{7,5},{8,10},{9,11},{10,... | collective-permute-start | bytes 1081352 | tf_op jit(solution)/shard_map/ppermute | solution.py:295
  23.2 33.6 %collective-permute-start.1 = (bf16[1408,128]{1,0:T(8,128)(2,1)}, bf16[1408,128]{1,0:T(8,128)(2,1)}, u32[]{:S(2)}, u32[]{:S(2)}) collective-permute-start(bf16[1408,128]{1,0:T(8,128)(2,1)} %get-tuple-element.24), channel_id=1, source_target_pairs={{0,1},{1,2},{2,3},{3,0},{4,5},{5,6},{6,7},{7,4},{8,9},{9,10},{10,1... | collective-permute-start | bytes 1081352 | tf_op jit(solution)/shard_map/ppermute | solution.py:295
  25.1 31.7 %collective-permute-start.2 = (bf16[1408,128]{1,0:T(8,128)(2,1)}, bf16[1408,128]{1,0:T(8,128)(2,1)}, u32[]{:S(2)}, u32[]{:S(2)}) collective-permute-start(bf16[1408,128]{1,0:T(8,128)(2,1)} %get-tuple-element.25), channel_id=1, source_target_pairs={{0,3},{1,0},{2,1},{3,2},{4,7},{5,4},{6,5},{7,6},{8,11},{9,8},{10,9... | collective-permute-start | bytes 1081352 | tf_op jit(solution)/shard_map/ppermute | solution.py:295
  33.1 0.8 copy-start.4
  33.8 30.6 %all-to-all-start.1 = ((bf16[16,16,896]{2,1,0:T(8,128)(2,1)}), bf16[16,16,896]{2,1,0:T(8,128)(2,1)S(1)}, u32[]{:S(2)}, u32[]{:S(2)}) async-start(bf16[16,16,896]{2,1,0:T(8,128)(2,1)} %bitcast.23), calls=%async_computation.1 | async-start | bytes 917504 | tf_op jit(solution)/shard_map/all_to_all | solution.py:291
  44.8 0.8 copy-start.5
  45.6 29.6 %collective-permute-start.6 = (bf16[1792,128]{1,0:T(8,128)(2,1)}, bf16[1792,128]{1,0:T(8,128)(2,1)}, u32[]{:S(2)}, u32[]{:S(2)}) collective-permute-start(bf16[1792,128]{1,0:T(8,128)(2,1)} %get-tuple-element.27), channel_id=1, source_target_pairs={{0,2},{1,3},{2,0},{3,1},{4,6},{5,7},{6,4},{7,5},{8,10},{9,11},{10,... | collective-permute-start | bytes 1376264 | tf_op jit(solution)/shard_map/ppermute | solution.py:295
  50.1 29.4 %collective-permute-start.7 = (bf16[1792,128]{1,0:T(8,128)(2,1)}, bf16[1792,128]{1,0:T(8,128)(2,1)}, u32[]{:S(2)}, u32[]{:S(2)}) collective-permute-start(bf16[1792,128]{1,0:T(8,128)(2,1)} %get-tuple-element.28), channel_id=1, source_target_pairs={{0,1},{1,2},{2,3},{3,0},{4,5},{5,6},{6,7},{7,4},{8,9},{9,10},{10,1... | collective-permute-start | bytes 1376264 | tf_op jit(solution)/shard_map/ppermute | solution.py:295
  52.4 27.1 %copy-start.3 = (bf16[1,1,256,2,128]{4,3,2,1,0:T(2,128)(2,1)S(1)}, bf16[1,1,256,2,128]{4,3,2,1,0:T(2,128)(2,1)}, u32[]{:S(2)}) copy-start(bf16[1,1,256,2,128]{4,3,2,1,0:T(2,128)(2,1)} %param.10) | copy-start | bytes 393220
  52.4 27.1 %collective-permute-start.8 = (bf16[1792,128]{1,0:T(8,128)(2,1)}, bf16[1792,128]{1,0:T(8,128)(2,1)}, u32[]{:S(2)}, u32[]{:S(2)}) collective-permute-start(bf16[1792,128]{1,0:T(8,128)(2,1)} %get-tuple-element.29), channel_id=1, source_target_pairs={{0,3},{1,0},{2,1},{3,2},{4,7},{5,4},{6,5},{7,6},{8,11},{9,8},{10,9... | collective-permute-start | bytes 1376264 | tf_op jit(solution)/shard_map/ppermute | solution.py:295
  58.2 21.4 %copy-start.6 = (bf16[1792,128]{1,0:T(8,128)(2,1)S(1)}, bf16[1792,128]{1,0:T(8,128)(2,1)}, u32[]{:S(2)}) copy-start(bf16[1792,128]{1,0:T(8,128)(2,1)} %copy-done.5) | copy-start | bytes 1376260
  64.9 17.2 %collective-permute-start.3 = (bf16[256,512]{1,0:T(8,128)(2,1)S(1)}, bf16[256,512]{1,0:T(8,128)(2,1)S(1)}, u32[]{:S(2)}, u32[]{:S(2)}) collective-permute-start(bf16[256,512]{1,0:T(8,128)(2,1)S(1)} %shard_map.89.refs_0_), channel_id=1, source_target_pairs={{0,2},{1,3},{2,0},{3,1},{4,6},{5,7},{6,4},{7,5},{8,10},{9,11},{10,... | collective-permute-start | bytes 786440 | tf_op jit(solution)/shard_map/ppermute | solution.py:295
  73.0 12.1 %collective-permute-start.4 = (bf16[256,512]{1,0:T(8,128)(2,1)S(1)}, bf16[256,512]{1,0:T(8,128)(2,1)S(1)}, u32[]{:S(2)}, u32[]{:S(2)}) collective-permute-start(bf16[256,512]{1,0:T(8,128)(2,1)S(1)} %shard_map.89.refs_0_), channel_id=1, source_target_pairs={{0,1},{1,2},{2,3},{3,0},{4,5},{5,6},{6,7},{7,4},{8,9},{9,10},{10,1... | collective-permute-start | bytes 786440 | tf_op jit(solution)/shard_map/ppermute | solution.py:295
  75.2 9.8 %collective-permute-start.5 = (bf16[256,512]{1,0:T(8,128)(2,1)S(1)}, bf16[256,512]{1,0:T(8,128)(2,1)S(1)}, u32[]{:S(2)}, u32[]{:S(2)}) collective-permute-start(bf16[256,512]{1,0:T(8,128)(2,1)S(1)} %shard_map.89.refs_0_), channel_id=1, source_target_pairs={{0,3},{1,0},{2,1},{3,2},{4,7},{5,4},{6,5},{7,6},{8,11},{9,8},{10,9... | collective-permute-start | bytes 786440 | tf_op jit(solution)/shard_map/ppermute | solution.py:295
  85.8 56.1 %copy-start.7 = (bf16[128,16]{1,0:T(8,128)(2,1)S(1)}, bf16[128,16]{1,0:T(8,128)(2,1)}, u32[]{:S(2)}) copy-start(bf16[128,16]{1,0:T(8,128)(2,1)} %get-tuple-element.19.refs_1_) | copy-start | bytes 12292
  85.8 56.1 %copy-start.8 = (s32[16,8]{0,1:T(8,128)S(1)}, s32[16,8]{0,1:T(8,128)}, u32[]{:S(2)}) copy-start(s32[16,8]{0,1:T(8,128)} %param.8) | copy-start | bytes 1540

commit v10 on v9

--- a/solution.py
+++ b/solution.py
@@ -51,10 +51,10 @@
 
 
 def pack_rest_kernel(gate_ref, up_ref, after_ref, *out_refs):
-    count = len(out_refs)
+    count = len(out_refs) + 1
     width = gate_ref.shape[0] // count
     me = lax.axis_index("tp")
-    for step, out_ref in enumerate(out_refs):
+    for step, out_ref in enumerate(out_refs, 1):
         to = lax.rem(me + step, count)
         rows = pl.ds(pl.multiple_of(to * width, TILE), width)
         out_ref[0:width, :] = gate_ref[rows, :]
@@ -189,13 +189,20 @@
     return terms[0]
 
 
-def prepare_kernel(count, preacts_ref, *refs):
-    blocks = by_step(refs[:count])
-    early = by_step([preacts_ref, *refs[count : 2 * count - 1]])
-    weight_ref, swish_ref, slope_ref, hidden_ref = refs[2 * count - 1 :]
+def prepare_kernel(count, preacts_ref, gate_hbm, up_hbm, *refs):
+    blocks = by_step([None, *refs[: count - 1]])
+    early = by_step([preacts_ref, *refs[count - 1 : 2 * count - 2]])
+    weight_ref, swish_ref, slope_ref, hidden_ref, own_ref, sems = refs[2 * count - 2 :]
     columns = weight_ref.shape[0]
     slots = swish_ref.shape[0]
-    for at, block_ref in enumerate(blocks):
+    own = pl.ds(pl.multiple_of(lax.axis_index("tp") * columns, TILE), columns)
+    copies = [
+        pltpu.make_async_copy(source.at[own], own_ref.at[part], sems.at[part])
+        for part, source in enumerate((gate_hbm, up_hbm))
+    ]
+    for copy in copies:
+        copy.start()
+    for at, block_ref in enumerate(blocks[1:], 1):
         for part in range(2):
             first = (2 * at + part) * TILE
             weight_ref[:, first : first + TILE] = block_ref[part * columns : (part + 1) * columns, :]
@@ -211,6 +218,9 @@
     swish_ref[...] = swish_value
     slope_ref[...] = up_pre * (sigmoid_value * (1.0 + gate_pre * (1.0 - sigmoid_value)))
     hidden_ref[...] = swish_value * up_pre
+    for part, copy in enumerate(copies):
+        copy.wait()
+        weight_ref[:, part * TILE : (part + 1) * TILE] = own_ref[part]
 
 
 def expert_kernel(count, lane_cap, *refs):
@@ -363,7 +373,7 @@
     )
     rest_packed = call(
         pack_rest_kernel,
-        [shape(2 * columns, hidden_width)] * split_count,
+        [shape(2 * columns, hidden_width)] * others,
         (
             w_gate[0, 0],
             w_up[0, 0],
@@ -372,7 +382,7 @@
         size=4 << 20,
         spaces=[pltpu.VMEM] * 2 + [pl.ANY],
     )
-    blocks = shift_all(rest_packed)
+    blocks = shift_all([None, *rest_packed])
     slot_rows = exchange(forward.reshape(lane_count, lane_cap, columns), "narrow").reshape(
         slot_count, columns
     )
@@ -387,7 +397,18 @@
         lambda *refs: prepare_kernel(split_count, *refs),
         [shape(columns, 2 * hidden_all)]
         + [shape(slot_count, hidden_all, dtype=jnp.float32)] * 3,
-        (preacts, *(blocks[step] for step in far_first(split_count)), *early),
+        (
+            preacts,
+            w_gate[0, 0],
+            w_up[0, 0],
+            *(blocks[step] for step in far_first(split_count)[1:]),
+            *early,
+        ),
+        spaces=[pltpu.VMEM] + [pl.ANY] * 2 + [pltpu.VMEM] * (2 * others),
+        scratch=[
+            pltpu.VMEM((2, columns, hidden_width), w_gate.dtype),
+            pltpu.SemaphoreType.DMA((2,)),
+        ],
         size=8 << 20,
     )
     block_rows = columns // TILE * lane_cap + BLOCK

time: 144 us -> 144 us (level)
  local copies, waits for them, and re-layouts: 1.59 us -> 6.38 us
  waiting for transfers between devices: 11.9 us -> 7.42 us
    unnamed x18 -> x30, local copies, waits for them, and re-layouts: 1.59 us -> 6.38 us
    all_to_all x2, waiting for transfers between devices: 9.03 us -> 4.81 us  [exchange(): return lax.all_to_all(values, axis, split_axis=0, concat_axis=0, tiled=True)]
where the time goes in v10:
time: 144 us; the launch traced here: 143 us
  starting transfers between devices  61.2 us (42%)
  blocking collectives  55.3 us (38%)
  Pallas kernels  11.5 us (8%)
  waiting for transfers between devices  7.42 us (5%)
  local copies, waits for them, and re-layouts  6.38 us (4%)
    all_to_all x2, blocking collectives, exchange(): return lax.all_to_all(values, axis, split_axis=0, concat_axis=0, tiled=True)  55.3 us
    ppermute x9, starting transfers between devices, shift(): lax.ppermute(values, 'tp', [(source, (source + step) % count) for source...  33.9 us
    all_to_all x2, starting transfers between devices, exchange(): return lax.all_to_all(values, axis, split_axis=0, concat_axis=0, tiled=True)  27.3 us
    pallas_call x9, Pallas kernels, call(): pl.pallas_call(kernel, out_shape=outs, in_specs=[pl.BlockSpec(memory_spac...  11.5 us
    unnamed x30, local copies, waits for them, and re-layouts  6.38 us
    all_to_all x2, waiting for transfers between devices, exchange(): return lax.all_to_all(values, axis, split_axis=0, concat_axis=0, tiled=True)  4.81 us
  transfers between devices with their start and end apart: 11, of which 3 were waited for; matrix products, arithmetic and copies ran while one was open for 0% of the time, Pallas kernels for 4%

profile of v10, /device:TPU:1, one launch (start us, length us, event | category | flops | bytes accessed | tf_op | source)
XLA Modules:
  0.0 142.6 jit_solution(4838564147245087356)
XLA Ops:
  0.6 0.0 copy-start
  0.6 0.0 copy-start.1
  0.7 3.0 %shard_map.86 = (bf16[128,896]{1,0:T(8,128)(2,1)}, bf16[128,16]{1,0:T(8,128)(2,1)}, bf16[1408,128]{1,0:T(8,128)(2,1)}, bf16[1408,128]{1,0:T(8,128)(2,1)}, bf16[1408,128]{1,0:T(8,128)(2,1)}) custom-call(s32[8,16]{1,0:T(8,128)} %bitcast.25, bf16[8,16]{1,0:T(8,128)(2,1)} %bitcast.28, bf16[16,3584]{1,0:T(8,128)(2,1)} %refs_2_.1, bf16[128,3584]{1,0:T(8,128)(2,1)} %bitcast.19, ...), custom_call_target="tpu_custom_call" | custom-call | bytes 1048576 | tf_op jit(solution)/shard_map/pallas_call | solution.py:36
  3.6 17.5 %all-to-all-start = ((bf16[16,8,896]{2,1,0:T(8,128)(2,1)}), bf16[16,8,896]{2,1,0:T(8,128)(2,1)S(1)}, u32[]{:S(2)}, u32[]{:S(2)}) async-start(bf16[16,8,896]{2,1,0:T(8,128)(2,1)} %bitcast.27), calls=%async_computation | async-start | bytes 458752 | tf_op jit(solution)/shard_map/all_to_all | solution.py:301
  21.1 1.9 %collective-permute-start = (bf16[1408,128]{1,0:T(8,128)(2,1)}, bf16[1408,128]{1,0:T(8,128)(2,1)S(1)}, u32[]{:S(2)}, u32[]{:S(2)}) collective-permute-start(bf16[1408,128]{1,0:T(8,128)(2,1)} %get-tuple-element.22), channel_id=1, source_target_pairs={{0,2},{1,3},{2,0},{3,1},{4,6},{5,7},{6,4},{7,5},{8,10},{9,11},{10,... | collective-permute-start | bytes 1081352 | tf_op jit(solution)/shard_map/ppermute | solution.py:305
  23.0 1.9 %collective-permute-start.1 = (bf16[1408,128]{1,0:T(8,128)(2,1)}, bf16[1408,128]{1,0:T(8,128)(2,1)S(1)}, u32[]{:S(2)}, u32[]{:S(2)}) collective-permute-start(bf16[1408,128]{1,0:T(8,128)(2,1)} %get-tuple-element.23), channel_id=1, source_target_pairs={{0,1},{1,2},{2,3},{3,0},{4,5},{5,6},{6,7},{7,4},{8,9},{9,10},{10,1... | collective-permute-start | bytes 1081352 | tf_op jit(solution)/shard_map/ppermute | solution.py:305
  25.0 4.6 %collective-permute-start.2 = (bf16[1408,128]{1,0:T(8,128)(2,1)}, bf16[1408,128]{1,0:T(8,128)(2,1)S(1)}, u32[]{:S(2)}, u32[]{:S(2)}) collective-permute-start(bf16[1408,128]{1,0:T(8,128)(2,1)} %get-tuple-element.24), channel_id=1, source_target_pairs={{0,3},{1,0},{2,1},{3,2},{4,7},{5,4},{6,5},{7,6},{8,11},{9,8},{10,9... | collective-permute-start | bytes 1081352 | tf_op jit(solution)/shard_map/ppermute | solution.py:305
  29.5 2.7 %all-to-all-done = bf16[16,8,896]{2,1,0:T(8,128)(2,1)S(1)} async-done(((bf16[16,8,896]{2,1,0:T(8,128)(2,1)}), bf16[16,8,896]{2,1,0:T(8,128)(2,1)S(1)}, u32[]{:S(2)}, u32[]{:S(2)}) %all-to-all-start) | async-done | bytes 229408 | tf_op jit(solution)/shard_map/all_to_all | solution.py:301
  32.3 1.5 %shard_map.87 = (bf16[2,128,896]{2,1,0:T(8,128)(2,1)}, bf16[128,128]{1,0:T(8,128)(2,1)S(1)}) custom-call(bf16[128,896]{1,0:T(8,128)(2,1)S(1)} %bitcast.18), custom_call_target="tpu_custom_call" | custom-call | bytes 1048576 | tf_op jit(solution)/shard_map/pallas_call | solution.py:36
  33.7 9.8 %all-to-all-start.1 = ((bf16[16,16,896]{2,1,0:T(8,128)(2,1)}), bf16[16,16,896]{2,1,0:T(8,128)(2,1)S(1)}, u32[]{:S(2)}, u32[]{:S(2)}) async-start(bf16[16,16,896]{2,1,0:T(8,128)(2,1)} %bitcast.6), calls=%async_computation.1 | async-start | bytes 917504 | tf_op jit(solution)/shard_map/all_to_all | solution.py:301
  43.5 0.0 copy-done
  43.5 0.0 copy-done.1
  43.5 1.2 shard_map.90
  44.7 4.5 %collective-permute-start.6 = (bf16[1792,128]{1,0:T(8,128)(2,1)}, bf16[1792,128]{1,0:T(8,128)(2,1)}, u32[]{:S(2)}, u32[]{:S(2)}) collective-permute-start(bf16[1792,128]{1,0:T(8,128)(2,1)} %get-tuple-element.25), channel_id=1, source_target_pairs={{0,2},{1,3},{2,0},{3,1},{4,6},{5,7},{6,4},{7,5},{8,10},{9,11},{10,... | collective-permute-start | bytes 1376264 | tf_op jit(solution)/shard_map/ppermute | solution.py:305
  49.2 2.2 %collective-permute-start.7 = (bf16[1792,128]{1,0:T(8,128)(2,1)}, bf16[1792,128]{1,0:T(8,128)(2,1)}, u32[]{:S(2)}, u32[]{:S(2)}) collective-permute-start(bf16[1792,128]{1,0:T(8,128)(2,1)} %get-tuple-element.26), channel_id=1, source_target_pairs={{0,1},{1,2},{2,3},{3,0},{4,5},{5,6},{6,7},{7,4},{8,9},{9,10},{10,1... | collective-permute-start | bytes 1376264 | tf_op jit(solution)/shard_map/ppermute | solution.py:305
  51.5 0.0 collective-permute-done.refs_0_.refs_6_
  51.5 0.0 copy-start.4
  51.5 0.7 copy-done.4
  52.2 4.3 %collective-permute-start.8 = (bf16[1792,128]{1,0:T(8,128)(2,1)}, bf16[1792,128]{1,0:T(8,128)(2,1)}, u32[]{:S(2)}, u32[]{:S(2)}) collective-permute-start(bf16[1792,128]{1,0:T(8,128)(2,1)} %get-tuple-element.27), channel_id=1, source_target_pairs={{0,3},{1,0},{2,1},{3,2},{4,7},{5,4},{6,5},{7,6},{8,11},{9,8},{10,9... | collective-permute-start | bytes 1376264 | tf_op jit(solution)/shard_map/ppermute | solution.py:305
  56.5 0.0 collective-permute-done.1.refs_1_.refs_7_
  56.5 0.0 copy-start.7
  56.5 0.7 copy-done.7
  57.2 0.0 collective-permute-done.2.refs_2_.refs_8_
  57.3 0.7 copy-done.10
  58.0 1.2 copy-done.2
  59.2 1.0 copy-done.5
  60.2 1.0 copy-done.8
  61.1 1.0 copy-done.11
  62.1 0.1 shard_map.88.down_ref
  62.3 2.1 %all-to-all-done.1 = bf16[16,16,896]{2,1,0:T(8,128)(2,1)S(1)} async-done(((bf16[16,16,896]{2,1,0:T(8,128)(2,1)}), bf16[16,16,896]{2,1,0:T(8,128)(2,1)S(1)}, u32[]{:S(2)}, u32[]{:S(2)}) %all-to-all-start.1) | async-done | bytes 458784 | tf_op jit(solution)/shard_map/all_to_all | solution.py:301
  64.4 0.5 shard_map.89.refs_0_
  64.8 8.0 %collective-permute-start.3 = (bf16[256,512]{1,0:T(8,128)(2,1)S(1)}, bf16[256,512]{1,0:T(8,128)(2,1)S(1)}, u32[]{:S(2)}, u32[]{:S(2)}) collective-permute-start(bf16[256,512]{1,0:T(8,128)(2,1)S(1)} %shard_map.89.refs_0_), channel_id=1, source_target_pairs={{0,2},{1,3},{2,0},{3,1},{4,6},{5,7},{6,4},{7,5},{8,10},{9,11},{10,... | collective-permute-start | bytes 786440 | tf_op jit(solution)/shard_map/ppermute | solution.py:305
  72.9 2.2 %collective-permute-start.4 = (bf16[256,512]{1,0:T(8,128)(2,1)S(1)}, bf16[256,512]{1,0:T(8,128)(2,1)S(1)}, u32[]{:S(2)}, u32[]{:S(2)}) collective-permute-start(bf16[256,512]{1,0:T(8,128)(2,1)S(1)} %shard_map.89.refs_0_), channel_id=1, source_target_pairs={{0,1},{1,2},{2,3},{3,0},{4,5},{5,6},{6,7},{7,4},{8,9},{9,10},{10,1... | collective-permute-start | bytes 786440 | tf_op jit(solution)/shard_map/ppermute | solution.py:305
  75.1 0.0 collective-permute-done.6.refs_3_
  75.1 4.3 %collective-permute-start.5 = (bf16[256,512]{1,0:T(8,128)(2,1)S(1)}, bf16[256,512]{1,0:T(8,128)(2,1)S(1)}, u32[]{:S(2)}, u32[]{:S(2)}) collective-permute-start(bf16[256,512]{1,0:T(8,128)(2,1)S(1)} %shard_map.89.refs_0_), channel_id=1, source_target_pairs={{0,3},{1,0},{2,1},{3,2},{4,7},{5,4},{6,5},{7,6},{8,11},{9,8},{10,9... | collective-permute-start | bytes 786440 | tf_op jit(solution)/shard_map/ppermute | solution.py:305
  79.4 0.0 collective-permute-done.7.refs_4_
  79.4 0.0 collective-permute-done.8.refs_5_
  79.4 0.0 copy-done.3
  79.5 2.9 %shard_map.91 = (bf16[896,1024]{1,0:T(8,128)(2,1)S(1)}, f32[256,512]{1,0:T(8,128)S(1)}, f32[256,512]{1,0:T(8,128)S(1)}, f32[256,512]{1,0:T(8,128)S(1)}) custom-call(bf16[512,128]{1,0:T(8,128)(2,1)S(1)} %bitcast.24, bf16[3584,128]{1,0:T(8,128)(2,1)S(1)} %bitcast.14, bf16[3584,128]{1,0:T(8,128)(2,1)S(1)} %bitcast.16, ...), custom_call_target="tpu_custom_call" | custom-call | bytes 8388608 | tf_op jit(solution)/shard_map/pallas_call | solution.py:36
  82.4 0.0 collective-permute-done.3.refs_1_
  82.4 2.6 %collective-permute-done.4.refs_2_ = bf16[256,512]{1,0:T(8,128)(2,1)S(1)} collective-permute-done((bf16[256,512]{1,0:T(8,128)(2,1)S(1)}, bf16[256,512]{1,0:T(8,128)(2,1)S(1)}, u32[]{:S(2)}, u32[]{:S(2)}) %collective-permute-start.4) | collective-permute-done | bytes 262176 | tf_op jit(solution)/shard_map/ppermute | solution.py:305
  85.0 0.0 collective-permute-done.5.refs_3_
  85.0 0.8 shard_map.92
  85.7 0.0 copy-start.14
  85.7 30.1 %all_to_all.20.refs_1_ = bf16[16,120,128]{2,1,0:T(8,128)(2,1)S(1)} all-to-all(bf16[16,120,128]{2,1,0:T(8,128)(2,1)S(1)} %shard_map.92), channel_id=1, replica_groups=mesh['wide'=16,'narrow'=16,'tp'=4] {'narrow'}, dimensions={0} | all-to-all | bytes 983040 | tf_op jit(solution)/shard_map/all_to_all | solution.py:301
  115.9 0.4 shard_map.93
  116.2 25.2 %all_to_all.21 = bf16[16,8,896]{2,1,0:T(8,128)(2,1)S(1)} all-to-all(bf16[16,8,896]{2,1,0:T(8,128)(2,1)S(1)} %bitcast.22), channel_id=1, replica_groups=mesh['wide'=16,'narrow'=16,'tp'=4] {'wide'}, dimensions={0} | all-to-all | bytes 458752 | tf_op jit(solution)/shard_map/all_to_all | solution.py:301
  141.4 1.2 shard_map.94
  (15 shorter events, 0.0 us)
Async XLA Ops:
  0.6 42.9 %copy-start = (bf16[1,1,3584,128]{3,2,1,0:T(8,128)(2,1)S(1)}, bf16[1,1,3584,128]{3,2,1,0:T(8,128)(2,1)}, u32[]{:S(2)}) copy-start(bf16[1,1,3584,128]{3,2,1,0:T(8,128)(2,1)} %param.11) | copy-start | bytes 2752516
  0.6 42.9 %copy-start.1 = (bf16[1,1,3584,128]{3,2,1,0:T(8,128)(2,1)S(1)}, bf16[1,1,3584,128]{3,2,1,0:T(8,128)(2,1)}, u32[]{:S(2)}) copy-start(bf16[1,1,3584,128]{3,2,1,0:T(8,128)(2,1)} %param.12) | copy-start | bytes 2752516
  3.6 28.6 %all-to-all-start = ((bf16[16,8,896]{2,1,0:T(8,128)(2,1)}), bf16[16,8,896]{2,1,0:T(8,128)(2,1)S(1)}, u32[]{:S(2)}, u32[]{:S(2)}) async-start(bf16[16,8,896]{2,1,0:T(8,128)(2,1)} %bitcast.27), calls=%async_computation | async-start | bytes 458752 | tf_op jit(solution)/shard_map/all_to_all | solution.py:301
  21.1 30.3 %collective-permute-start = (bf16[1408,128]{1,0:T(8,128)(2,1)}, bf16[1408,128]{1,0:T(8,128)(2,1)S(1)}, u32[]{:S(2)}, u32[]{:S(2)}) collective-permute-start(bf16[1408,128]{1,0:T(8,128)(2,1)} %get-tuple-element.22), channel_id=1, source_target_pairs={{0,2},{1,3},{2,0},{3,1},{4,6},{5,7},{6,4},{7,5},{8,10},{9,11},{10,... | collective-permute-start | bytes 1081352 | tf_op jit(solution)/shard_map/ppermute | solution.py:305
  23.0 33.5 %collective-permute-start.1 = (bf16[1408,128]{1,0:T(8,128)(2,1)}, bf16[1408,128]{1,0:T(8,128)(2,1)S(1)}, u32[]{:S(2)}, u32[]{:S(2)}) collective-permute-start(bf16[1408,128]{1,0:T(8,128)(2,1)} %get-tuple-element.23), channel_id=1, source_target_pairs={{0,1},{1,2},{2,3},{3,0},{4,5},{5,6},{6,7},{7,4},{8,9},{9,10},{10,1... | collective-permute-start | bytes 1081352 | tf_op jit(solution)/shard_map/ppermute | solution.py:305
  25.0 32.3 %collective-permute-start.2 = (bf16[1408,128]{1,0:T(8,128)(2,1)}, bf16[1408,128]{1,0:T(8,128)(2,1)S(1)}, u32[]{:S(2)}, u32[]{:S(2)}) collective-permute-start(bf16[1408,128]{1,0:T(8,128)(2,1)} %get-tuple-element.24), channel_id=1, source_target_pairs={{0,3},{1,0},{2,1},{3,2},{4,7},{5,4},{6,5},{7,6},{8,11},{9,8},{10,9... | collective-permute-start | bytes 1081352 | tf_op jit(solution)/shard_map/ppermute | solution.py:305
  33.7 30.6 %all-to-all-start.1 = ((bf16[16,16,896]{2,1,0:T(8,128)(2,1)}), bf16[16,16,896]{2,1,0:T(8,128)(2,1)S(1)}, u32[]{:S(2)}, u32[]{:S(2)}) async-start(bf16[16,16,896]{2,1,0:T(8,128)(2,1)} %bitcast.6), calls=%async_computation.1 | async-start | bytes 917504 | tf_op jit(solution)/shard_map/all_to_all | solution.py:301
  44.7 30.4 %collective-permute-start.6 = (bf16[1792,128]{1,0:T(8,128)(2,1)}, bf16[1792,128]{1,0:T(8,128)(2,1)}, u32[]{:S(2)}, u32[]{:S(2)}) collective-permute-start(bf16[1792,128]{1,0:T(8,128)(2,1)} %get-tuple-element.25), channel_id=1, source_target_pairs={{0,2},{1,3},{2,0},{3,1},{4,6},{5,7},{6,4},{7,5},{8,10},{9,11},{10,... | collective-permute-start | bytes 1376264 | tf_op jit(solution)/shard_map/ppermute | solution.py:305
  49.2 30.2 %collective-permute-start.7 = (bf16[1792,128]{1,0:T(8,128)(2,1)}, bf16[1792,128]{1,0:T(8,128)(2,1)}, u32[]{:S(2)}, u32[]{:S(2)}) collective-permute-start(bf16[1792,128]{1,0:T(8,128)(2,1)} %get-tuple-element.26), channel_id=1, source_target_pairs={{0,1},{1,2},{2,3},{3,0},{4,5},{5,6},{6,7},{7,4},{8,9},{9,10},{10,1... | collective-permute-start | bytes 1376264 | tf_op jit(solution)/shard_map/ppermute | solution.py:305
  51.5 0.8 copy-start.4
  52.2 27.2 %collective-permute-start.8 = (bf16[1792,128]{1,0:T(8,128)(2,1)}, bf16[1792,128]{1,0:T(8,128)(2,1)}, u32[]{:S(2)}, u32[]{:S(2)}) collective-permute-start(bf16[1792,128]{1,0:T(8,128)(2,1)} %get-tuple-element.27), channel_id=1, source_target_pairs={{0,3},{1,0},{2,1},{3,2},{4,7},{5,4},{6,5},{7,6},{8,11},{9,8},{10,9... | collective-permute-start | bytes 1376264 | tf_op jit(solution)/shard_map/ppermute | solution.py:305
  56.5 0.7 copy-start.7
  57.2 0.7 copy-start.10
  58.0 1.2 copy-start.2
  59.2 1.0 copy-start.5
  60.2 1.0 copy-start.8
  61.1 1.0 copy-start.11
  62.1 17.3 %copy-start.3 = (bf16[1,1,256,2,128]{4,3,2,1,0:T(2,128)(2,1)S(1)}, bf16[1,1,256,2,128]{4,3,2,1,0:T(2,128)(2,1)}, u32[]{:S(2)}) copy-start(bf16[1,1,256,2,128]{4,3,2,1,0:T(2,128)(2,1)} %param.10) | copy-start | bytes 393220
  64.4 15.1 %copy-start.6 = (bf16[1408,128]{1,0:T(8,128)(2,1)S(1)}, bf16[1408,128]{1,0:T(8,128)(2,1)}, u32[]{:S(2)}) copy-start(bf16[1408,128]{1,0:T(8,128)(2,1)} %copy-done.4) | copy-start | bytes 1081348
  64.4 15.1 %copy-start.9 = (bf16[1408,128]{1,0:T(8,128)(2,1)S(1)}, bf16[1408,128]{1,0:T(8,128)(2,1)}, u32[]{:S(2)}) copy-start(bf16[1408,128]{1,0:T(8,128)(2,1)} %copy-done.7) | copy-start | bytes 1081348
  64.4 15.1 %copy-start.12 = (bf16[1408,128]{1,0:T(8,128)(2,1)S(1)}, bf16[1408,128]{1,0:T(8,128)(2,1)}, u32[]{:S(2)}) copy-start(bf16[1408,128]{1,0:T(8,128)(2,1)} %copy-done.10) | copy-start | bytes 1081348
  64.8 17.5 %collective-permute-start.3 = (bf16[256,512]{1,0:T(8,128)(2,1)S(1)}, bf16[256,512]{1,0:T(8,128)(2,1)S(1)}, u32[]{:S(2)}, u32[]{:S(2)}) collective-permute-start(bf16[256,512]{1,0:T(8,128)(2,1)S(1)} %shard_map.89.refs_0_), channel_id=1, source_target_pairs={{0,2},{1,3},{2,0},{3,1},{4,6},{5,7},{6,4},{7,5},{8,10},{9,11},{10,... | collective-permute-start | bytes 786440 | tf_op jit(solution)/shard_map/ppermute | solution.py:305
  72.9 12.1 %collective-permute-start.4 = (bf16[256,512]{1,0:T(8,128)(2,1)S(1)}, bf16[256,512]{1,0:T(8,128)(2,1)S(1)}, u32[]{:S(2)}, u32[]{:S(2)}) collective-permute-start(bf16[256,512]{1,0:T(8,128)(2,1)S(1)} %shard_map.89.refs_0_), channel_id=1, source_target_pairs={{0,1},{1,2},{2,3},{3,0},{4,5},{5,6},{6,7},{7,4},{8,9},{9,10},{10,1... | collective-permute-start | bytes 786440 | tf_op jit(solution)/shard_map/ppermute | solution.py:305
  75.1 9.8 %collective-permute-start.5 = (bf16[256,512]{1,0:T(8,128)(2,1)S(1)}, bf16[256,512]{1,0:T(8,128)(2,1)S(1)}, u32[]{:S(2)}, u32[]{:S(2)}) collective-permute-start(bf16[256,512]{1,0:T(8,128)(2,1)S(1)} %shard_map.89.refs_0_), channel_id=1, source_target_pairs={{0,3},{1,0},{2,1},{3,2},{4,7},{5,4},{6,5},{7,6},{8,11},{9,8},{10,9... | collective-permute-start | bytes 786440 | tf_op jit(solution)/shard_map/ppermute | solution.py:305
  85.7 55.7 %copy-start.13 = (bf16[128,16]{1,0:T(8,128)(2,1)S(1)}, bf16[128,16]{1,0:T(8,128)(2,1)}, u32[]{:S(2)}) copy-start(bf16[128,16]{1,0:T(8,128)(2,1)} %get-tuple-element.18.refs_1_) | copy-start | bytes 12292
  85.7 55.7 %copy-start.14 = (s32[16,8]{0,1:T(8,128)S(1)}, s32[16,8]{0,1:T(8,128)}, u32[]{:S(2)}) copy-start(s32[16,8]{0,1:T(8,128)} %param.8) | copy-start | bytes 1540
